TPU v7x, 256 devices: a whole 4x4x8 slice. The times are simulated.
256 devices in a mesh: dp: 64 (over y_hi, z, x), tensor: 4 (over y_lo, core).
Axes of the slice: x: 4, y: 4 (y_hi: 2, y_lo: 2; y = y_hi * 2 + y_lo), z: 8, core: 2. Of those that a mesh axis runs over, the one named last changes fastest.
Arguments:
- hidden: bfloat16 [8192, 28672], P('dp', 'tensor'), may hold values from -6 to 6
- sign_bits: int32 [28672], P('tensor'), may hold values from 0 to 1
- exponents: int32 [8192, 224], P('dp', 'tensor'), may hold values from -9 to -6
- down_weight: bfloat16 [28672, 512], P('tensor'), may hold values from -0.03125 to 0.03125
- grad_out: bfloat16 [8192, 512], P('dp'), may hold values from -18 to 18
Outputs:
- output: bfloat16 [8192, 512], P(('dp', 'tensor'))
- grad_hidden: bfloat16 [8192, 28672], P('dp', 'tensor')
- grad_weight: float32 [28672, 512], P(('tensor', 'dp'))
All inputs are finite; a program needn't handle non-finite values.
Results may differ from a plain program's by a relative error of at most 0.018.
Values may be sent and summed in bfloat16 or wider, within the bound.
No kernel may reach another device: no remote copies, remote signals or barrier semaphores. Data moves between devices by JAX's collectives and lax.ppermute only.
A program may use at most 192 MiB of HBM per device.

v0:
```python
import math

import jax
import jax.numpy as jnp
import numpy as np
from jax import lax
from jax.sharding import PartitionSpec as P

HIGHEST_MODE = lax.Precision.HIGHEST


def from_partner(value, axis, apart):
    mask = 2**apart
    pairs = [(source, source ^ mask) for source in range(lax.axis_size(axis))]
    return lax.ppermute(value, axis, pairs)


def paley_table():
    squares_set = set((factor * factor % 13 for factor in range(1, 13)))
    core_matrix = np.zeros((14, 14))
    core_matrix[0, 1:] = 1.0
    core_matrix[1:, 0] = 1.0
    for row_idx in range(13):
        for col_idx in range(13):
            offset = (col_idx - row_idx) % 13
            if offset != 0:
                core_matrix[row_idx + 1, col_idx + 1] = 1.0 if offset in squares_set else -1.0
    first_pat = np.array([[1.0, -1.0], [-1.0, -1.0]])
    second_pat = np.array([[1.0, 1.0], [1.0, -1.0]])
    return np.kron(core_matrix, first_pat) + np.kron(np.eye(14), second_pat)


def sylvester_table(order):
    result = np.ones((1, 1))
    base_pat = np.array([[1.0, 1.0], [1.0, -1.0]])
    while result.shape[0] < order:
        result = np.kron(base_pat, result)
    return result


def spin_block(values, block_local):
    tok_rows = values.shape[0]
    cube = values.reshape(tok_rows, block_local, 28)
    if values.dtype == jnp.bfloat16:
        left_table = jnp.asarray(sylvester_table(block_local), jnp.bfloat16)
        inner = jnp.einsum("tba,cb->tca", cube, left_table, preferred_element_type=jnp.float32)
    else:
        left_table = jnp.asarray(sylvester_table(block_local), jnp.float32)
        inner = jnp.einsum(
            "tba,cb->tca",
            cube,
            left_table,
            precision=HIGHEST_MODE,
            preferred_element_type=jnp.float32,
        )
    right_table = jnp.asarray(paley_table(), jnp.float32)
    outer = jnp.einsum("tca,da->tcd", inner, right_table, precision=HIGHEST_MODE)
    return outer.reshape(tok_rows, block_local * 28)


def butterfly(partial_sum):
    width_bits = lax.axis_size("tensor").bit_length() - 1
    my_index = lax.axis_index("tensor")
    result = partial_sum
    for bit_num in range(width_bits):
        partner = from_partner(result.astype(jnp.bfloat16), "tensor", bit_num).astype(result.dtype)
        upper_side = my_index >> bit_num & 1 == 1
        result = jnp.where(upper_side, partner - result, result + partner)
    return result


def saturate(rotated, expo_float, group_cols):
    tok_rows = rotated.shape[0]
    bound = 448.0 * jnp.exp2(expo_float)[:, :, None]
    ratio = jnp.tanh(rotated.reshape(tok_rows, -1, group_cols) / bound)
    quant_vals = (bound * ratio).reshape(rotated.shape)
    slope = (1.0 - ratio * ratio).reshape(rotated.shape)
    return (quant_vals, slope)


def local(hidden, sign_bits, exponents, down_weight, grad_out):
    tok_count, ff_local = hidden.shape
    n_tensor = lax.axis_size("tensor")
    n_data = lax.axis_size("dp")
    block_local = ff_local // 28
    ff_total = ff_local * n_tensor
    group_cols = ff_local // exponents.shape[1]
    norm_factor = 1.0 / math.sqrt(ff_total)
    sign_vals = (2 * sign_bits - 1).astype(jnp.bfloat16)
    flipped = hidden * sign_vals[None, :]
    rotated = butterfly(spin_block(flipped, block_local)) * norm_factor
    quant_vals, slope = saturate(rotated, exponents.astype(jnp.float32), group_cols)
    quantized = quant_vals.astype(jnp.bfloat16)
    output = lax.psum_scatter(
        jnp.dot(quantized, down_weight, preferred_element_type=jnp.float32).astype(jnp.bfloat16),
        "tensor",
        scatter_dimension=0,
        tiled=True,
    )
    grad_quant = lax.dot_general(
        grad_out, down_weight, (((1,), (1,)), ((), ())), preferred_element_type=jnp.float32
    )
    spun = butterfly(spin_block(grad_quant * slope, block_local)) * norm_factor
    grad_hidden = spun.astype(jnp.bfloat16) * sign_vals[None, :]
    inv_root = 1.0 / math.sqrt(tok_count * n_data)
    grad_weight = lax.psum_scatter(
        lax.dot_general(
            quantized, grad_out, (((0,), (0,)), ((), ())), preferred_element_type=jnp.float32
        )
        * inv_root,
        "dp",
        scatter_dimension=0,
        tiled=True,
    )
    return (output, grad_hidden, grad_weight)


def solution(mesh):
    return jax.shard_map(
        local,
        mesh=mesh,
        in_specs=(
            P("dp", "tensor"),
            P("tensor"),
            P("dp", "tensor"),
            P("tensor", None),
            P("dp", None),
        ),
        out_specs=(P(("dp", "tensor"), None), P("dp", "tensor"), P(("tensor", "dp"), None)),
        check_vma=False,
    )
```

profile of v0, /device:TPU:0, one launch (start us, length us, event | category | flops | bytes accessed | tf_op | source)
XLA Modules:
  0.0 535.8 jit_solution(11963196582880421591)
XLA Ops:
  7.2 0.8 add_convert_fusion
  8.0 1.6 broadcast_multiply_fusion
  9.7 2.3 copy.15
  12.0 2.4 reshape.27
  14.4 3.3 convolution_bitcast_fusion
  17.6 5.5 %copy.27 = f32[128,256,28]{0,2,1:T(8,128)} copy(f32[128,256,28]{1,0,2:T(8,128)} %convolution_bitcast_fusion) | data formatting | bytes 7340032 | tf_op jit(solution)/shard_map/tba,cb->tca/transpose | solution.py:46
  23.1 7.8 %fusion.19 = f32[128,256,28]{0,2,1:T(8,128)} fusion(f32[128,256,28]{0,2,1:T(8,128)} %copy.27, f32[28,28,1]{1,0,2:T(8,128)S(1)} %copy-done.9), kind=kOutput, calls=%fused_computation.33 | convolution fusion | flops 308281344 | bytes 7343168 | tf_op jit(solution)/shard_map/tca,da->tcd/dot_general | solution.py:57
  30.9 4.7 reshape.28
  35.6 5.3 copy.17
  40.9 3.5 convert_element_type.41
  44.4 4.0 collective-permute-done
  48.4 4.5 fusion.13
  53.0 42.2 %collective-permute-done.1 = bf16[128,7168]{1,0:T(8,128)(2,1)} collective-permute-done((bf16[128,7168]{1,0:T(8,128)(2,1)}, bf16[128,7168]{1,0:T(8,128)(2,1)}, u32[]{:S(2)}, u32[]{:S(2)}) %collective-permute-start.1) | collective-permute-done | bytes 1835040 | tf_op jit(solution)/shard_map/ppermute | solution.py:15
  95.2 1.0 mul.59
  96.3 4.6 fusion.9
  100.9 4.9 convolution_convert_fusion
  106.0 7.3 %convolution_multiply_fusion = f32[7168,512]{1,0:T(8,128)} fusion(bf16[128,7168]{1,0:T(8,128)(2,1)S(1)} %fusion.9, bf16[128,512]{1,0:T(8,128)(2,1)S(1)} %copy-done), kind=kOutput, calls=%fused_computation | convolution fusion | flops 943194112 | bytes 16646144 | tf_op jit(solution)/shard_map/dot_general | solution.py:107
  113.3 1.5 copy-done.6
  114.8 11.5 %convolution_multiply_fusion.1 = f32[128,7168]{1,0:T(8,128)} fusion(bf16[128,512]{1,0:T(8,128)(2,1)S(1)} %copy-done, bf16[7168,512]{1,0:T(8,128)(2,1)} %param.12, f32[16,8,56,128]{3,2,1,0:T(8,128)} %bitcast.40, f32[128,7168]{1,0:T(8,128)} %copy.17, bf16[128,7168]{1,0:T(8,128)(2,1)S(1)} %copy-done.6, pred[]{:T(512)S(6)} %eq.9, ...), kind=kOutput, calls=%fused_computation.1 | convolution fusion | flops 951451648 | bytes 22151170 | tf_op jit(solution)/shard_map/dot_general | solution.py:100
  126.3 5.3 copy.20
  131.6 4.7 reshape.29
  136.3 11.3 %fusion.14 = f32[128,256,28]{1,0,2:T(8,128)} fusion(f32[256,256,1]{1,0,2:T(8,128)S(1)} %copy-done.7, f32[128,256,28]{0,2,1:T(8,128)} %reshape.29), kind=kOutput, calls=%fused_computation.25 | convolution fusion | flops 2818572288 | bytes 7602176 | tf_op jit(solution)/shard_map/tba,cb->tca/dot_general | solution.py:49
  147.6 5.6 %copy.31 = f32[128,256,28]{0,2,1:T(8,128)} copy(f32[128,256,28]{1,0,2:T(8,128)} %fusion.14) | data formatting | bytes 7340032 | tf_op jit(solution)/shard_map/tba,cb->tca/transpose | solution.py:49
  153.2 7.9 %fusion.20 = f32[128,256,28]{0,2,1:T(8,128)} fusion(f32[128,256,28]{0,2,1:T(8,128)} %copy.31, f32[28,28,1]{1,0,2:T(8,128)S(1)} %copy-done.9), kind=kOutput, calls=%fused_computation.34 | convolution fusion | flops 308281344 | bytes 7343168 | tf_op jit(solution)/shard_map/tca,da->tcd/dot_general | solution.py:57
  161.1 4.7 reshape.30
  165.8 5.3 copy.22
  171.2 2.4 convert_element_type.47
  173.7 3.8 collective-permute-done.2
  177.4 0.5 fusion.12
  178.4 72.2 %collective-permute-done.3 = bf16[128,7168]{1,0:T(8,128)(2,1)S(1)} collective-permute-done((bf16[128,7168]{1,0:T(8,128)(2,1)S(1)}, bf16[128,7168]{1,0:T(8,128)(2,1)S(1)}, u32[]{:S(2)}, u32[]{:S(2)}) %collective-permute-start.3) | collective-permute-done | bytes 1835040 | tf_op jit(solution)/shard_map/ppermute | solution.py:15
  250.6 2.5 fusion.17
  253.0 275.9 %reduce-scatter.5.cloned.1.call-done = f32[112,512]{1,0:T(8,128)} async-done(((f32[7168,512]{1,0:T(8,128)}), f32[112,512]{1,0:T(8,128)}) %reduce-scatter.5.cloned.1.call-update) | async-done | bytes 229392 | tf_op jit(solution)/shard_map/reduce_scatter | solution.py:106
  (32 shorter events, 0.9 us)
Async XLA Ops:
  7.2 98.8 %copy-start = (bf16[128,512]{1,0:T(8,128)(2,1)S(1)}, bf16[128,512]{1,0:T(8,128)(2,1)}, u32[]{:S(2)}) copy-start(bf16[128,512]{1,0:T(8,128)(2,1)} %param.13) | copy-start | bytes 393220
  7.2 245.9 %reduce-scatter.3.cloned.1.call-start = ((), (), s32[]{:S(2)}) async-start(), calls=%async_computation.2 | async-start | bytes 163840 | tf_op jit(solution)/shard_map/reduce_scatter | solution.py:94
  9.6 4.7 copy-start.8
  17.6 5.5 %copy-start.9 = (f32[28,28,1]{1,0,2:T(8,128)S(1)}, f32[28,28,1]{1,0,2:T(8,128)}, u32[]{:S(2)}) copy-start(f32[28,28,1]{1,0,2:T(8,128)} %constant.33) | copy-start | bytes 9412
  44.4 4.0 collective-permute-start
  44.4 8.5 %copy-start.10 = (s32[128,56]{0,1:T(8,128)S(1)}, s32[128,56]{0,1:T(8,128)}, u32[]{:S(2)}) copy-start(s32[128,56]{0,1:T(8,128)} %param.11) | copy-start | bytes 86020
  48.4 4.5 copy-start.5
  52.9 42.4 %collective-permute-start.1 = (bf16[128,7168]{1,0:T(8,128)(2,1)}, bf16[128,7168]{1,0:T(8,128)(2,1)}, u32[]{:S(2)}, u32[]{:S(2)}) collective-permute-start(bf16[128,7168]{1,0:T(8,128)(2,1)} %fusion.13), channel_id=1, source_target_pairs={{0,2},{1,3},{2,0},{3,1},{4,6},{5,7},{6,4},{7,5},{8,10},{9,11},{10,... | collective-permute-start | bytes 5505032 | tf_op jit(solution)/shard_map/ppermute | solution.py:15
  53.0 43.3 %copy-start.2 = (f32[128,7168]{1,0:T(8,128)S(1)}, f32[128,7168]{1,0:T(8,128)}, u32[]{:S(2)}) copy-start(f32[128,7168]{1,0:T(8,128)} %copy.17) | copy-start | bytes 11010052
  96.2 4.6 copy-start.4
  105.8 423.2 %reduce-scatter.5.cloned.1.call-start = ((), (), s32[]{:S(2)}) async-start(), calls=%async_computation.3 | async-start | bytes 14909440 | tf_op jit(solution)/shard_map/reduce_scatter | solution.py:106
  113.3 1.5 copy-start.6
  131.6 4.7 copy-start.7
  171.2 6.3 %copy-start.3 = (f32[128,7168]{1,0:T(8,128)S(1)}, f32[128,7168]{1,0:T(8,128)}, u32[]{:S(2)}) copy-start(f32[128,7168]{1,0:T(8,128)} %copy.22) | copy-start | bytes 11010052
  173.6 3.9 collective-permute-start.2
  177.4 351.5 %copy-start.1 = (bf16[128,512]{1,0:T(8,128)(2,1)S(1)}, bf16[128,512]{1,0:T(8,128)(2,1)}, u32[]{:S(2)}) copy-start(bf16[128,512]{1,0:T(8,128)(2,1)} %param.13) | copy-start | bytes 393220
  178.0 72.6 %collective-permute-start.3 = (bf16[128,7168]{1,0:T(8,128)(2,1)S(1)}, bf16[128,7168]{1,0:T(8,128)(2,1)S(1)}, u32[]{:S(2)}, u32[]{:S(2)}) collective-permute-start(bf16[128,7168]{1,0:T(8,128)(2,1)S(1)} %fusion.12), channel_id=1, source_target_pairs={{0,2},{1,3},{2,0},{3,1},{4,6},{5,7},{6,4},{7,5},{8,10},{9,11},{10,... | collective-permute-start | bytes 5505032 | tf_op jit(solution)/shard_map/ppermute | solution.py:15
Sparse Core Ops, SparseCore 0:
  105.9 20.5 reduce-scatter.2
  129.8 399.1 reduce-scatter.4
where the time goes:
time: 537 us; the launch traced here: 536 us
  waiting for transfers between devices  398 us (74%)
  matrix products  54 us (10%)
  local copies, waits for them, and re-layouts  48.3 us (9%)
  other arithmetic  20.4 us (4%)
  between operations  14.2 us (3%)
    reduce_scatter x1, waiting for transfers between devices, local(): lax.psum_scatter(lax.dot_general(quantized, grad_out, (((0,), (0,)), ((),...  276 us
    ppermute x4, waiting for transfers between devices, from_partner(): return lax.ppermute(value, axis, pairs)  122 us
    reshape x4, local copies, waits for them, and re-layouts, spin_block(): return outer.reshape(tok_rows, block_local * 28)  20 us
    dot_general x2, matrix products, spin_block(): jnp.einsum('tca,da->tcd', inner, right_table, precision=HIGHEST_MODE)  15.7 us
    dot_general x1, matrix products, local(): lax.dot_general(grad_out, down_weight, (((1,), (1,)), ((), ())), preferre...  11.5 us
    dot_general x1, matrix products, spin_block(): jnp.einsum('tba,cb->tca', cube, left_table, precision=HIGHEST_MODE, prefe...  11.3 us
    convert_element_type x4, other arithmetic, butterfly(): result.astype(jnp.bfloat16)  10.9 us
  transfers between devices with their start and end apart: 6, of which 5 were waited for; matrix products, arithmetic and copies ran while one was open for 13% of the time, Pallas kernels for 0%

commit v1 on v0

v1 whole, which is shorter than its diff:
```python
import functools
import math

import jax
import jax.numpy as jnp
import numpy as np
from jax import lax
from jax.experimental import pallas as pl
from jax.experimental.pallas import tpu as pltpu
from jax.sharding import Mesh
from jax.sharding import PartitionSpec as P

AXES = ("yh", "z", "x", "yl", "core")
BLOCK = 896
LANES = 128


def paley_table():
    squares_set = set((factor * factor % 13 for factor in range(1, 13)))
    core_matrix = np.zeros((14, 14))
    core_matrix[0, 1:] = 1.0
    core_matrix[1:, 0] = 1.0
    for row_idx in range(13):
        for col_idx in range(13):
            offset = (col_idx - row_idx) % 13
            if offset != 0:
                core_matrix[row_idx + 1, col_idx + 1] = 1.0 if offset in squares_set else -1.0
    first_pat = np.array([[1.0, -1.0], [-1.0, -1.0]])
    second_pat = np.array([[1.0, 1.0], [1.0, -1.0]])
    return np.kron(core_matrix, first_pat) + np.kron(np.eye(14), second_pat)


def sylvester_table(order):
    result = np.ones((1, 1))
    base_pat = np.array([[1.0, 1.0], [1.0, -1.0]])
    while result.shape[0] < order:
        result = np.kron(base_pat, result)
    return result


def block_table():
    return np.kron(sylvester_table(BLOCK // 28), paley_table())


def pairs_xor():
    return [(0, 1), (1, 0)]


def swap(value, axis):
    return lax.ppermute(value, axis, pairs_xor())


def butterfly(parts):
    parts = list(parts)
    step = 1
    while step < len(parts):
        for base in range(len(parts)):
            if base & step == 0:
                a, b = parts[base], parts[base + step]
                parts[base], parts[base + step] = a + b, a - b
        step *= 2
    return parts


def rotate_kernel(nblk, norm, sgn_ref, own_ref, core_ref, far_ref, fcore_ref, table_ref, bound_ref, q_ref, slope_ref, qt_ref, w_ref, spun_ref):
    rows = own_ref.shape[0]
    so_core, so_y = sgn_ref[0], sgn_ref[1]
    for j in range(nblk):
        cols = pl.ds(j * BLOCK, BLOCK)
        near = so_core * own_ref[:, cols].astype(jnp.float32) + core_ref[:, cols].astype(jnp.float32)
        far = so_core * far_ref[:, cols].astype(jnp.float32) + fcore_ref[:, cols].astype(jnp.float32)
        w_ref[pl.ds(j * rows, rows), :] = (so_y * near + far).astype(jnp.bfloat16)
    spun_ref[...] = jnp.dot(w_ref[...], table_ref[...], preferred_element_type=jnp.float32)
    half = nblk // 2
    for lane in range(BLOCK // LANES):
        lcols = pl.ds(lane * LANES, LANES)
        parts = butterfly([spun_ref[pl.ds(j * rows, rows), lcols] for j in range(nblk)])
        quants = []
        for j in range(nblk):
            group = j * (BLOCK // LANES) + lane
            bound = bound_ref[:, group : group + 1]
            ratio = jnp.tanh(parts[j] * (norm / bound))
            quant = bound * ratio
            cols = pl.ds(j * BLOCK + lane * LANES, LANES)
            q_ref[:, cols] = quant.astype(jnp.bfloat16)
            slope_ref[:, cols] = (1.0 - ratio * ratio).astype(jnp.bfloat16)
            quants.append(quant)
        for j in range(half):
            both = jnp.concatenate([quants[j], quants[j + half]], axis=0)
            qt_ref[pl.ds(j * BLOCK + lane * LANES, LANES), :] = both.T.astype(jnp.bfloat16)


def rotate(sgn, own, core, far, fcore, table, bound, norm):
    rows, cols = own.shape
    nblk = cols // BLOCK
    vm = pl.BlockSpec(memory_space=pltpu.VMEM)
    return pl.pallas_call(
        functools.partial(rotate_kernel, nblk, norm),
        out_shape=(
            jax.ShapeDtypeStruct((rows, cols), jnp.bfloat16),
            jax.ShapeDtypeStruct((rows, cols), jnp.bfloat16),
            jax.ShapeDtypeStruct((cols // 2, 2 * rows), jnp.bfloat16),
        ),
        in_specs=[pl.BlockSpec(memory_space=pltpu.SMEM)] + [vm] * 6,
        out_specs=(vm, vm, vm),
        scratch_shapes=[
            pltpu.VMEM((nblk * rows, BLOCK), jnp.bfloat16),
            pltpu.VMEM((nblk * rows, BLOCK), jnp.float32),
        ],
        compiler_params=pltpu.CompilerParams(vmem_limit_bytes=40 * 2**20),
        name="rotate",
    )(sgn, own, core, far, fcore, table, bound)


def project_kernel(nblk, norm, q_ref, slope_ref, go_ref, w_ref, table_ref, out_ref, s_ref, acc_ref, g_ref, spun_ref):
    j = pl.program_id(0)
    rows = q_ref.shape[0]
    weight = w_ref[...]
    part = jnp.dot(q_ref[...], weight, preferred_element_type=jnp.float32)

    @pl.when(j == 0)
    def _():
        acc_ref[...] = part

    @pl.when(j > 0)
    def _():
        acc_ref[...] += part

    grad = lax.dot_general(go_ref[...], weight, (((1,), (1,)), ((), ())), preferred_element_type=jnp.float32)
    start = pl.multiple_of(j * rows, rows)
    g_ref[pl.ds(start, rows), :] = (grad * slope_ref[...].astype(jnp.float32)).astype(jnp.bfloat16)

    @pl.when(j == nblk - 1)
    def _():
        out_ref[...] = acc_ref[...].astype(out_ref.dtype)
        spun_ref[...] = jnp.dot(g_ref[...], table_ref[...], preferred_element_type=jnp.float32)
        for lane in range(BLOCK // LANES):
            lcols = pl.ds(lane * LANES, LANES)
            parts = butterfly([spun_ref[pl.ds(b * rows, rows), lcols] for b in range(nblk)])
            for b in range(nblk):
                s_ref[:, pl.ds(b * BLOCK + lane * LANES, LANES)] = (parts[b] * norm).astype(jnp.bfloat16)


def project(quant, slope, grad_out, weight, table, norm):
    rows, cols = quant.shape
    nblk = cols // BLOCK
    wide = weight.shape[1]
    return pl.pallas_call(
        functools.partial(project_kernel, nblk, norm),
        grid=(nblk,),
        out_shape=(
            jax.ShapeDtypeStruct((rows, wide), jnp.bfloat16),
            jax.ShapeDtypeStruct((rows, cols), jnp.bfloat16),
        ),
        in_specs=[
            pl.BlockSpec((rows, BLOCK), lambda j: (0, j)),
            pl.BlockSpec((rows, BLOCK), lambda j: (0, j)),
            pl.BlockSpec((rows, wide), lambda j: (0, 0)),
            pl.BlockSpec((BLOCK, wide), lambda j: (j, 0)),
            pl.BlockSpec((BLOCK, BLOCK), lambda j: (0, 0)),
        ],
        out_specs=(
            pl.BlockSpec((rows, wide), lambda j: (0, 0)),
            pl.BlockSpec((rows, cols), lambda j: (0, 0)),
        ),
        scratch_shapes=[
            pltpu.VMEM((rows, wide), jnp.float32),
            pltpu.VMEM((nblk * rows, BLOCK), jnp.bfloat16),
            pltpu.VMEM((nblk * rows, BLOCK), jnp.float32),
        ],
        compiler_params=pltpu.CompilerParams(vmem_limit_bytes=40 * 2**20),
        name="project",
    )(quant, slope, grad_out, weight, table)


def weight_grad_kernel(nsrc, rows, r_ref, go_ref, acc_in_ref, out_ref, lhs_ref, rhs_ref):
    toks = LANES // 2
    lane = lax.broadcasted_iota(jnp.int32, (rows, LANES), 1)
    low = lane < toks
    for s in range(nsrc):
        value = r_ref[s]
        zero = jnp.zeros_like(value)
        cols = pl.ds(s * LANES, LANES)
        lhs_ref[0:rows, cols] = jnp.where(low, value, zero)
        lhs_ref[rows : 2 * rows, cols] = jnp.where(low, zero, value)
        grads = go_ref[s]
        rhs_ref[pl.ds(s * LANES, toks), :] = grads
        rhs_ref[pl.ds(s * LANES + toks, toks), :] = grads
    out_ref[...] = acc_in_ref[...] + jnp.dot(lhs_ref[...], rhs_ref[...], preferred_element_type=jnp.float32)


def weight_grad(received, grads, chunk, acc):
    nsrc, rows, _ = received.shape
    toks, wide = LANES // 2, grads.shape[2]
    return pl.pallas_call(
        functools.partial(weight_grad_kernel, nsrc, rows),
        grid=(1,),
        out_shape=jax.ShapeDtypeStruct((2 * rows, wide), jnp.float32),
        in_specs=[
            pl.BlockSpec((nsrc, rows, LANES), lambda i: (0, 0, 0)),
            pl.BlockSpec((nsrc, toks, wide), lambda i: (0, chunk, 0)),
            pl.BlockSpec((2 * rows, wide), lambda i: (0, 0)),
        ],
        out_specs=pl.BlockSpec((2 * rows, wide), lambda i: (0, 0)),
        scratch_shapes=[
            pltpu.VMEM((2 * rows, nsrc * LANES), jnp.bfloat16),
            pltpu.VMEM((nsrc * LANES, wide), jnp.bfloat16),
        ],
        compiler_params=pltpu.CompilerParams(vmem_limit_bytes=48 * 2**20),
        name="weight_grad",
    )(received, grads, acc)


def gather_zx(value):
    return lax.all_gather(value, ("z", "x"), axis=0, tiled=False)


def exchange_zx(quant_t):
    nsrc = lax.axis_size("z") * lax.axis_size("x")
    blocks = quant_t.reshape(nsrc, -1, quant_t.shape[1])
    return lax.all_to_all(blocks, ("z", "x"), 0, 0, tiled=True)


def local(hidden, sign_bits, exponents, down_weight, grad_out):
    tok_count, ff_local = hidden.shape
    n_tensor = lax.axis_size("yl") * lax.axis_size("core")
    n_data = lax.axis_size("yh") * lax.axis_size("z") * lax.axis_size("x")
    norm = 1.0 / math.sqrt(ff_local * n_tensor)
    half = tok_count // 2
    table = jnp.asarray(block_table(), jnp.bfloat16)
    sign_vals = (2 * sign_bits - 1).astype(jnp.bfloat16)[None, :]
    core, yl, yh = lax.axis_index("core"), lax.axis_index("yl"), lax.axis_index("yh")
    so_core = (1 - 2 * core).astype(jnp.float32)
    so_y = (1 - 2 * yl).astype(jnp.float32)
    sgn = jnp.stack([so_core, so_y])
    bound = 448.0 * jnp.exp2(exponents.astype(jnp.float32))

    flipped = [hidden[k * half : (k + 1) * half] * sign_vals for k in range(2)]
    far = [swap(f, "yl") for f in flipped]
    near = [swap(f, "core") for f in flipped]
    grads_all = gather_zx(grad_out)

    outs, folded, crossed, received = [], [], [], []
    for k in range(2):
        rows = slice(k * half, (k + 1) * half)
        fcore = swap(far[k], "core")
        quant, slope, quant_t = rotate(sgn, flipped[k], near[k], far[k], fcore, table, bound[rows], norm)
        out, spun = project(quant, slope, grad_out[rows], down_weight, table, norm)
        outs.append(out)
        partner = swap(spun, "core")
        fold = (so_core * spun.astype(jnp.float32) + partner.astype(jnp.float32)).astype(jnp.bfloat16)
        folded.append(fold)
        crossed.append(swap(fold, "yl"))
        received.append(exchange_zx(quant_t))

    out_all = jnp.concatenate(outs, axis=0).reshape(2, 2, -1, outs[0].shape[1])
    keep = lax.dynamic_index_in_dim(out_all, yl, 0, keepdims=False)
    give = lax.dynamic_index_in_dim(out_all, 1 - yl, 0, keepdims=False)
    summed = keep.astype(jnp.float32) + swap(give, "yl").astype(jnp.float32)
    keep = lax.dynamic_index_in_dim(summed, core, 0, keepdims=False)
    give = lax.dynamic_index_in_dim(summed, 1 - core, 0, keepdims=False).astype(jnp.bfloat16)
    output = (keep + swap(give, "core").astype(jnp.float32)).astype(jnp.bfloat16)

    acc = jnp.zeros((2 * received[0].shape[1], grad_out.shape[1]), jnp.float32)
    for k in range(2):
        acc = weight_grad(received[k], grads_all, k, acc)
    acc = acc.reshape(2, -1, grad_out.shape[1])
    mine = lax.dynamic_index_in_dim(acc, yh, 0, keepdims=False)
    give = lax.dynamic_index_in_dim(acc, 1 - yh, 0, keepdims=False).astype(jnp.bfloat16)
    inv_root = 1.0 / math.sqrt(tok_count * n_data)
    grad_weight = (mine + swap(give, "yh").astype(jnp.float32)) * inv_root

    grad_hidden = jnp.concatenate(
        [
            (so_y * folded[k].astype(jnp.float32) + crossed[k].astype(jnp.float32)).astype(jnp.bfloat16) * sign_vals
            for k in range(2)
        ],
        axis=0,
    )
    return (output, grad_hidden, grad_weight)


def solution(mesh):
    fine = Mesh(mesh.devices.reshape(2, 8, 4, 2, 2), AXES)
    dp, tensor = ("yh", "z", "x"), ("yl", "core")
    return jax.shard_map(
        local,
        mesh=fine,
        in_specs=(P(dp, tensor), P(tensor), P(dp, tensor), P(tensor, None), P(dp, None)),
        out_specs=(P(dp + tensor, None), P(dp, tensor), P(tensor + dp, None)),
        check_vma=False,
    )
```

time: 537 us -> 195 us (0.36)
  the two profiles are of different devices: /device:TPU:0 before, /device:TPU:1 now
where the time goes in v1:
time: 195 us; the launch traced here: 193 us
  waiting for transfers between devices  85 us (44%)
  starting transfers between devices  41.6 us (21%)
  Pallas kernels  28.1 us (14%)
  other arithmetic  14.3 us (7%)
  between operations  14.2 us (7%)
  local copies, waits for them, and re-layouts  10.1 us (5%)
    ppermute x13, waiting for transfers between devices, swap(): return lax.ppermute(value, axis, pairs_xor())  68.1 us
    ppermute x13, starting transfers between devices, swap(): return lax.ppermute(value, axis, pairs_xor())  20.9 us
    all_to_all x2, starting transfers between devices, exchange_zx(): return lax.all_to_all(blocks, ('z', 'x'), 0, 0, tiled=True)  20.6 us
    pallas_call x2, Pallas kernels, project(): pl.pallas_call(functools.partial(project_kernel, nblk, norm), grid=(nblk,...  17.3 us
    all_to_all x2, waiting for transfers between devices, exchange_zx(): return lax.all_to_all(blocks, ('z', 'x'), 0, 0, tiled=True)  16.9 us
    unnamed x26, local copies, waits for them, and re-layouts  9.89 us
    pallas_call x2, Pallas kernels, rotate(): pl.pallas_call(functools.partial(rotate_kernel, nblk, norm), out_shape=(j...  8.55 us
    convert_element_type x2, other arithmetic, local(): (so_core * spun.astype(jnp.float32) + partner.astype(jnp.float32)).astype...  4.19 us
  transfers between devices with their start and end apart: 16, of which 5 were waited for; matrix products, arithmetic and copies ran while one was open for 5% of the time, Pallas kernels for 14%

profile of v1, /device:TPU:1, one launch (start us, length us, event | category | flops | bytes accessed | tf_op | source)
XLA Modules:
  0.0 193.3 jit_solution(11346037020375801026)
XLA Ops:
  7.2 0.8 add_convert_fusion.4
  8.0 2.9 %slice_multiply_fusion.1 = (bf16[64,7168]{1,0:T(8,128)(2,1)}, bf16[64,7168]{1,0:T(8,128)(2,1)}) fusion(bf16[128,7168]{1,0:T(8,128)(2,1)} %param.6, bf16[7168]{0:T(1024)(128)(2,1)S(1)} %add_convert_fusion.4), kind=kLoop, calls=%fused_computation.8 | loop fusion | flops 917504 | bytes 3684352 | tf_op jit(solution)/shard_map/mul | solution.py:238
  10.8 2.1 %collective-permute-start.1 = (bf16[64,7168]{1,0:T(8,128)(2,1)}, bf16[64,7168]{1,0:T(8,128)(2,1)}, u32[]{:S(2)}, u32[]{:S(2)}) collective-permute-start(bf16[64,7168]{1,0:T(8,128)(2,1)} %get-tuple-element.23.own_ref), channel_id=1, source_target_pairs={{0,2},{2,0},{1,3},{3,1},{4,6},{6,4},{5,7},{7,5},{8,10},{10,8},{9,1... | collective-permute-start | bytes 2752520 | tf_op jit(solution)/shard_map/ppermute | solution.py:50
  13.1 3.1 %collective-permute-start = (bf16[64,7168]{1,0:T(8,128)(2,1)}, bf16[64,7168]{1,0:T(8,128)(2,1)}, u32[]{:S(2)}, u32[]{:S(2)}) collective-permute-start(bf16[64,7168]{1,0:T(8,128)(2,1)} %get-tuple-element.23.own_ref), channel_id=1, source_target_pairs={{0,1},{1,0},{2,3},{3,2},{4,5},{5,4},{6,7},{7,6},{8,9},{9,8},{10,11... | collective-permute-start | bytes 2752520 | tf_op jit(solution)/shard_map/ppermute | solution.py:50
  16.2 15.9 %collective-permute-done.1.far_ref = bf16[64,7168]{1,0:T(8,128)(2,1)} collective-permute-done((bf16[64,7168]{1,0:T(8,128)(2,1)}, bf16[64,7168]{1,0:T(8,128)(2,1)}, u32[]{:S(2)}, u32[]{:S(2)}) %collective-permute-start.1) | collective-permute-done | bytes 917536 | tf_op jit(solution)/shard_map/ppermute | solution.py:50
  32.1 5.6 %collective-permute-start.2 = (bf16[64,7168]{1,0:T(8,128)(2,1)}, bf16[64,7168]{1,0:T(8,128)(2,1)}, u32[]{:S(2)}, u32[]{:S(2)}) collective-permute-start(bf16[64,7168]{1,0:T(8,128)(2,1)} %collective-permute-done.1.far_ref), channel_id=1, source_target_pairs={{0,1},{1,0},{2,3},{3,2},{4,5},{5,4},{6,7},{7,6},{8,9},{9,8},{10,11... | collective-permute-start | bytes 2752520 | tf_op jit(solution)/shard_map/ppermute | solution.py:50
  37.9 13.8 %collective-permute-done.4.far_ref = bf16[64,7168]{1,0:T(8,128)(2,1)} collective-permute-done((bf16[64,7168]{1,0:T(8,128)(2,1)}, bf16[64,7168]{1,0:T(8,128)(2,1)}, u32[]{:S(2)}, u32[]{:S(2)}) %collective-permute-start.4) | collective-permute-done | bytes 917536 | tf_op jit(solution)/shard_map/ppermute | solution.py:50
  51.8 2.5 %collective-permute-start.5 = (bf16[64,7168]{1,0:T(8,128)(2,1)}, bf16[64,7168]{1,0:T(8,128)(2,1)S(1)}, u32[]{:S(2)}, u32[]{:S(2)}) collective-permute-start(bf16[64,7168]{1,0:T(8,128)(2,1)} %collective-permute-done.4.far_ref), channel_id=1, source_target_pairs={{0,1},{1,0},{2,3},{3,2},{4,5},{5,4},{6,7},{7,6},{8,9},{9,8},{10,11... | collective-permute-start | bytes 2752520 | tf_op jit(solution)/shard_map/ppermute | solution.py:50
  54.3 1.4 copy-done.1
  55.7 4.1 %rotate.2 = (bf16[64,7168]{1,0:T(8,128)(2,1)S(1)}, bf16[64,7168]{1,0:T(8,128)(2,1)S(1)}, bf16[3584,128]{1,0:T(8,128)(2,1)S(1)}) custom-call(f32[2]{0:T(128)S(1)} %pad_maximum_fusion.2.sgn_ref, bf16[64,7168]{1,0:T(8,128)(2,1)} %get-tuple-element.23.own_ref, bf16[64,7168]{1,0:T(8,128)(2,1)} %collective-permute-done.core_ref, ...), custom_call_target="tpu_custom_call" | custom-call | tf_op jit(solution)/shard_map/rotate/pallas_call | solution.py:97
  59.8 1.0 copy-done.6
  60.8 3.1 %copy-done = bf16[7168,512]{1,0:T(8,128)(2,1)S(1)} copy-done((bf16[7168,512]{1,0:T(8,128)(2,1)S(1)}, bf16[7168,512]{1,0:T(8,128)(2,1)}, u32[]{:S(2)}) %copy-start) | copy-done | bytes 7340056
  63.9 8.7 %project.2 = (bf16[64,512]{1,0:T(8,128)(2,1)S(1)}, bf16[64,7168]{1,0:T(8,128)(2,1)}) custom-call(bf16[64,7168]{1,0:T(8,128)(2,1)S(1)} %get-tuple-element.13.q_ref, bf16[64,7168]{1,0:T(8,128)(2,1)S(1)} %get-tuple-element.14.slope_ref, bf16[64,512]{1,0:T(8,128)(2,1)S(1)} %get-tuple-element.25.go_ref, bf16[7168,512]{1,0:T(8,128)(2,1)S(1)} %copy-done, ...), custom_call_target="tpu_custom_call" | custom-call | tf_op jit(solution)/shard_map/project/pallas_call | solution.py:148
  72.6 4.4 %rotate.3 = (bf16[64,7168]{1,0:T(8,128)(2,1)S(1)}, bf16[64,7168]{1,0:T(8,128)(2,1)S(1)}, bf16[3584,128]{1,0:T(8,128)(2,1)}) custom-call(f32[2]{0:T(128)S(1)} %pad_maximum_fusion.2.sgn_ref, bf16[64,7168]{1,0:T(8,128)(2,1)S(1)} %copy-done.5, bf16[64,7168]{1,0:T(8,128)(2,1)} %collective-permute-done.3.core_ref, ...), custom_call_target="tpu_custom_call" | custom-call | tf_op jit(solution)/shard_map/rotate/pallas_call | solution.py:97
  77.0 8.6 %project.3 = (bf16[64,512]{1,0:T(8,128)(2,1)S(1)}, bf16[64,7168]{1,0:T(8,128)(2,1)}) custom-call(bf16[64,7168]{1,0:T(8,128)(2,1)S(1)} %get-tuple-element.16.q_ref, bf16[64,7168]{1,0:T(8,128)(2,1)S(1)} %get-tuple-element.17.slope_ref, bf16[64,512]{1,0:T(8,128)(2,1)S(1)} %get-tuple-element.26.go_ref, bf16[7168,512]{1,0:T(8,128)(2,1)S(1)} %bitcast.25, ...), custom_call_target="tpu_custom_call" | custom-call | tf_op jit(solution)/shard_map/project/pallas_call | solution.py:148
  86.1 11.4 %all-to-all-start.1 = ((bf16[32,112,128]{2,1,0:T(8,128)(2,1)}), bf16[32,112,128]{2,1,0:T(8,128)(2,1)S(1)}, u32[]{:S(2)}, u32[]{:S(2)}) async-start(bf16[32,112,128]{2,1,0:T(8,128)(2,1)} %bitcast.30), calls=%async_computation.1 | async-start | bytes 1835008 | tf_op jit(solution)/shard_map/all_to_all | solution.py:221
  97.5 1.7 add_convert_fusion.3
  99.3 1.4 collective-permute-start.9
  100.6 2.5 %add_convert_fusion.1 = bf16[64,7168]{1,0:T(8,128)(2,1)} fusion(bf16[64,7168]{1,0:T(8,128)(2,1)S(1)} %collective-permute-done.10, bf16[64,7168]{1,0:T(8,128)(2,1)} %get-tuple-element.20, f32[]{:T(128)} %convert_element_type.78), kind=kLoop, calls=%fused_computation.2 | loop fusion | flops 2293760 | bytes 2752516 | tf_op jit(solution)/shard_map/convert_element_type | solution.py:251
  103.4 1.3 collective-permute-start.6
  104.7 37.5 %collective-permute-done.6 = bf16[2,32,512]{2,1,0:T(8,128)(2,1)S(1)} collective-permute-done((bf16[2,32,512]{2,1,0:T(8,128)(2,1)S(1)}, bf16[2,32,512]{2,1,0:T(8,128)(2,1)S(1)}, u32[]{:S(2)}, u32[]{:S(2)}) %collective-permute-start.6) | collective-permute-done | bytes 65568 | tf_op jit(solution)/shard_map/ppermute | solution.py:50
  142.2 1.1 collective-permute-start.7
  143.3 9.2 %all-to-all-start = ((bf16[32,112,128]{2,1,0:T(8,128)(2,1)}), bf16[32,112,128]{2,1,0:T(8,128)(2,1)S(1)}, u32[]{:S(2)}, u32[]{:S(2)}) async-start(bf16[32,112,128]{2,1,0:T(8,128)(2,1)} %bitcast.7), calls=%async_computation | async-start | bytes 1835008 | tf_op jit(solution)/shard_map/all_to_all | solution.py:221
  153.2 3.7 %fusion = (bf16[64,7168]{1,0:T(8,128)(2,1)S(1)}, bf16[64,7168]{1,0:T(8,128)(2,1)}) fusion(bf16[64,7168]{1,0:T(8,128)(2,1)} %collective-permute-done.9, bf16[64,7168]{1,0:T(8,128)(2,1)} %copy-done.8, f32[]{:T(128)} %convert_element_type.79, bf16[7168]{0:T(1024)(128)(2,1)S(1)} %add_convert_fusion.4, bf16[64,7168]{1,0:T(8,128)(2,1)} %collective-permute-done.11, ...), kind=kLoop, calls=%fused_computation.5 | loop fusion | flops 5505024 | bytes 5519364 | tf_op jit(solution)/shard_map/mul | solution.py:275
  156.9 2.2 %copy-done.3 = bf16[4096,512]{1,0:T(8,128)(2,1)S(1)} copy-done((bf16[4096,512]{1,0:T(8,128)(2,1)S(1)}, bf16[4096,512]{1,0:T(8,128)(2,1)}, u32[]{:S(2)}) %copy-start.3) | copy-done | bytes 4194328
  159.1 1.1 weight_grad.2.acc_in_ref
  160.3 16.9 %all-to-all-done.r_ref = bf16[32,112,128]{2,1,0:T(8,128)(2,1)S(1)} async-done(((bf16[32,112,128]{2,1,0:T(8,128)(2,1)}), bf16[32,112,128]{2,1,0:T(8,128)(2,1)S(1)}, u32[]{:S(2)}, u32[]{:S(2)}) %all-to-all-start) | async-done | bytes 917536 | tf_op jit(solution)/shard_map/all_to_all | solution.py:221
  177.1 2.2 %copy-done.4 = bf16[4096,512]{1,0:T(8,128)(2,1)S(1)} copy-done((bf16[4096,512]{1,0:T(8,128)(2,1)S(1)}, bf16[4096,512]{1,0:T(8,128)(2,1)}, u32[]{:S(2)}) %copy-start.4) | copy-done | bytes 4194328
  179.3 1.1 weight_grad.3
  180.5 3.0 %collective-permute-start.12 = (bf16[112,512]{1,0:T(8,128)(2,1)S(1)}, bf16[112,512]{1,0:T(8,128)(2,1)S(1)}, u32[]{:S(2)}, u32[]{:S(2)}) collective-permute-start(bf16[112,512]{1,0:T(8,128)(2,1)S(1)} %fusion.3), channel_id=1, source_target_pairs={{0,128},{128,0},{1,129},{129,1},{2,130},{130,2},{3,131},{131,3},{4... | collective-permute-start | bytes 344072 | tf_op jit(solution)/shard_map/ppermute | solution.py:50
  183.5 1.4 pad_maximum_fusion
  184.8 0.9 collective-permute-done.12
  (54 shorter events, 2.7 us)
Async XLA Ops:
  7.2 149.7 %all-gather.3.cloned.1.call-start = ((), (), s32[]{:S(2)}) async-start(), calls=%async_computation.2 | async-start | bytes 4325376 | tf_op jit(solution)/shard_map/all_gather | solution.py:215
  8.0 29.7 %copy-start.10 = (s32[128,56]{0,1:T(8,128)S(1)}, s32[128,56]{0,1:T(8,128)}, u32[]{:S(2)}) copy-start(s32[128,56]{0,1:T(8,128)} %param.8) | copy-start | bytes 86020
  8.0 29.9 %copy-start.9 = (bf16[128,512]{1,0:T(8,128)(2,1)S(1)}, bf16[128,512]{1,0:T(8,128)(2,1)}, u32[]{:S(2)}) copy-start(bf16[128,512]{1,0:T(8,128)(2,1)} %param.10) | copy-start | bytes 393220
  10.8 21.3 %collective-permute-start.1 = (bf16[64,7168]{1,0:T(8,128)(2,1)}, bf16[64,7168]{1,0:T(8,128)(2,1)}, u32[]{:S(2)}, u32[]{:S(2)}) collective-permute-start(bf16[64,7168]{1,0:T(8,128)(2,1)} %get-tuple-element.23.own_ref), channel_id=1, source_target_pairs={{0,2},{2,0},{1,3},{3,1},{4,6},{6,4},{5,7},{7,5},{8,10},{10,8},{9,1... | collective-permute-start | bytes 2752520 | tf_op jit(solution)/shard_map/ppermute | solution.py:50
  13.0 64.0 %slice-start = ((s8[7340032]{0:T(1024)(128)(4,1)}), s8[3145728]{0:T(1024)(128)(4,1)S(1)}, s32[]{:S(2)}) async-start(s8[7340032]{0:T(1024)(128)(4,1)} %bitcast.24), calls=%async_computation.3 | async-start | bytes 6291456
  13.0 38.8 %collective-permute-start.4 = (bf16[64,7168]{1,0:T(8,128)(2,1)}, bf16[64,7168]{1,0:T(8,128)(2,1)}, u32[]{:S(2)}, u32[]{:S(2)}) collective-permute-start(bf16[64,7168]{1,0:T(8,128)(2,1)} %get-tuple-element.24.own_ref), channel_id=1, source_target_pairs={{0,2},{2,0},{1,3},{3,1},{4,6},{6,4},{5,7},{7,5},{8,10},{10,8},{9,1... | collective-permute-start | bytes 2752520 | tf_op jit(solution)/shard_map/ppermute | solution.py:50
  13.1 41.2 %collective-permute-start = (bf16[64,7168]{1,0:T(8,128)(2,1)}, bf16[64,7168]{1,0:T(8,128)(2,1)}, u32[]{:S(2)}, u32[]{:S(2)}) collective-permute-start(bf16[64,7168]{1,0:T(8,128)(2,1)} %get-tuple-element.23.own_ref), channel_id=1, source_target_pairs={{0,1},{1,0},{2,3},{3,2},{4,5},{5,4},{6,7},{7,6},{8,9},{9,8},{10,11... | collective-permute-start | bytes 2752520 | tf_op jit(solution)/shard_map/ppermute | solution.py:50
  32.1 22.1 %collective-permute-start.2 = (bf16[64,7168]{1,0:T(8,128)(2,1)}, bf16[64,7168]{1,0:T(8,128)(2,1)}, u32[]{:S(2)}, u32[]{:S(2)}) collective-permute-start(bf16[64,7168]{1,0:T(8,128)(2,1)} %collective-permute-done.1.far_ref), channel_id=1, source_target_pairs={{0,1},{1,0},{2,3},{3,2},{4,5},{5,4},{6,7},{7,6},{8,9},{9,8},{10,11... | collective-permute-start | bytes 2752520 | tf_op jit(solution)/shard_map/ppermute | solution.py:50
  37.7 34.9 %collective-permute-start.3 = (bf16[64,7168]{1,0:T(8,128)(2,1)}, bf16[64,7168]{1,0:T(8,128)(2,1)}, u32[]{:S(2)}, u32[]{:S(2)}) collective-permute-start(bf16[64,7168]{1,0:T(8,128)(2,1)} %get-tuple-element.24.own_ref), channel_id=1, source_target_pairs={{0,1},{1,0},{2,3},{3,2},{4,5},{5,4},{6,7},{7,6},{8,9},{9,8},{10,11... | collective-permute-start | bytes 2752520 | tf_op jit(solution)/shard_map/ppermute | solution.py:50
  51.8 20.8 %collective-permute-start.5 = (bf16[64,7168]{1,0:T(8,128)(2,1)}, bf16[64,7168]{1,0:T(8,128)(2,1)S(1)}, u32[]{:S(2)}, u32[]{:S(2)}) collective-permute-start(bf16[64,7168]{1,0:T(8,128)(2,1)} %collective-permute-done.4.far_ref), channel_id=1, source_target_pairs={{0,1},{1,0},{2,3},{3,2},{4,5},{5,4},{6,7},{7,6},{8,9},{9,8},{10,11... | collective-permute-start | bytes 2752520 | tf_op jit(solution)/shard_map/ppermute | solution.py:50
  54.3 1.4 copy-start.1
  55.7 5.2 %copy-start.2 = (bf16[896,896]{1,0:T(8,128)(2,1)S(1)}, bf16[896,896]{1,0:T(8,128)(2,1)}, u32[]{:S(2)}) copy-start(bf16[896,896]{1,0:T(8,128)(2,1)} %constant.51.clone.table_ref) | copy-start | bytes 4816900
  59.8 1.0 copy-start.6
  60.8 3.1 %copy-start = (bf16[7168,512]{1,0:T(8,128)(2,1)S(1)}, bf16[7168,512]{1,0:T(8,128)(2,1)}, u32[]{:S(2)}) copy-start(bf16[7168,512]{1,0:T(8,128)(2,1)} %w_ref.3) | copy-start | bytes 22020100
  63.9 8.7 %copy-start.5 = (bf16[64,7168]{1,0:T(8,128)(2,1)S(1)}, bf16[64,7168]{1,0:T(8,128)(2,1)}, u32[]{:S(2)}) copy-start(bf16[64,7168]{1,0:T(8,128)(2,1)} %get-tuple-element.24.own_ref) | copy-start | bytes 2752516
  63.9 13.1 %slice-start.1 = ((s8[7340032]{0:T(1024)(128)(4,1)}), s8[4194304]{0:T(1024)(128)(4,1)S(1)}, s32[]{:S(2)}) async-start(s8[7340032]{0:T(1024)(128)(4,1)} %bitcast.24), calls=%async_computation.4 | async-start | bytes 8388608
  72.6 24.9 %collective-permute-start.8 = (bf16[64,7168]{1,0:T(8,128)(2,1)}, bf16[64,7168]{1,0:T(8,128)(2,1)}, u32[]{:S(2)}, u32[]{:S(2)}) collective-permute-start(bf16[64,7168]{1,0:T(8,128)(2,1)} %get-tuple-element.19), channel_id=1, source_target_pairs={{0,1},{1,0},{2,3},{3,2},{4,5},{5,4},{6,7},{7,6},{8,9},{9,8},{10,11... | collective-permute-start | bytes 2752520 | tf_op jit(solution)/shard_map/ppermute | solution.py:50
  85.6 15.0 %collective-permute-start.10 = (bf16[64,7168]{1,0:T(8,128)(2,1)}, bf16[64,7168]{1,0:T(8,128)(2,1)S(1)}, u32[]{:S(2)}, u32[]{:S(2)}) collective-permute-start(bf16[64,7168]{1,0:T(8,128)(2,1)} %get-tuple-element.20), channel_id=1, source_target_pairs={{0,1},{1,0},{2,3},{3,2},{4,5},{5,4},{6,7},{7,6},{8,9},{9,8},{10,11... | collective-permute-start | bytes 2752520 | tf_op jit(solution)/shard_map/ppermute | solution.py:50
  86.1 57.2 %all-to-all-start.1 = ((bf16[32,112,128]{2,1,0:T(8,128)(2,1)}), bf16[32,112,128]{2,1,0:T(8,128)(2,1)S(1)}, u32[]{:S(2)}, u32[]{:S(2)}) async-start(bf16[32,112,128]{2,1,0:T(8,128)(2,1)} %bitcast.30), calls=%async_computation.1 | async-start | bytes 1835008 | tf_op jit(solution)/shard_map/all_to_all | solution.py:221
  99.3 44.1 %copy-start.8 = (bf16[64,7168]{1,0:T(8,128)(2,1)}, bf16[64,7168]{1,0:T(8,128)(2,1)S(1)}, u32[]{:S(2)}) copy-start(bf16[64,7168]{1,0:T(8,128)(2,1)S(1)} %add_convert_fusion.3) | copy-start | bytes 2752516
  99.3 53.9 %collective-permute-start.9 = (bf16[64,7168]{1,0:T(8,128)(2,1)S(1)}, bf16[64,7168]{1,0:T(8,128)(2,1)}, u32[]{:S(2)}, u32[]{:S(2)}) collective-permute-start(bf16[64,7168]{1,0:T(8,128)(2,1)S(1)} %add_convert_fusion.3), channel_id=1, source_target_pairs={{0,2},{2,0},{1,3},{3,1},{4,6},{6,4},{5,7},{7,5},{8,10},{10,8},{9,1... | collective-permute-start | bytes 2752520 | tf_op jit(solution)/shard_map/ppermute | solution.py:50
  103.1 50.1 %collective-permute-start.11 = (bf16[64,7168]{1,0:T(8,128)(2,1)}, bf16[64,7168]{1,0:T(8,128)(2,1)}, u32[]{:S(2)}, u32[]{:S(2)}) collective-permute-start(bf16[64,7168]{1,0:T(8,128)(2,1)} %add_convert_fusion.1), channel_id=1, source_target_pairs={{0,2},{2,0},{1,3},{3,1},{4,6},{6,4},{5,7},{7,5},{8,10},{10,8},{9,1... | collective-permute-start | bytes 2752520 | tf_op jit(solution)/shard_map/ppermute | solution.py:50
  103.4 38.8 %collective-permute-start.6 = (bf16[2,32,512]{2,1,0:T(8,128)(2,1)S(1)}, bf16[2,32,512]{2,1,0:T(8,128)(2,1)S(1)}, u32[]{:S(2)}, u32[]{:S(2)}) collective-permute-start(bf16[2,32,512]{2,1,0:T(8,128)(2,1)S(1)} %dynamic-slice_bitcast_fusion), channel_id=1, source_target_pairs={{0,2},{2,0},{1,3},{3,1},{4,6},{6,4},{5,7},{7,5},{8,10},{10,8},{9,1... | collective-permute-start | bytes 196616 | tf_op jit(solution)/shard_map/ppermute | solution.py:50
  142.2 10.3 %collective-permute-start.7 = (bf16[32,512]{1,0:T(8,128)(2,1)S(1)}, bf16[32,512]{1,0:T(8,128)(2,1)S(1)}, u32[]{:S(2)}, u32[]{:S(2)}) collective-permute-start(bf16[32,512]{1,0:T(8,128)(2,1)S(1)} %fusion.5), channel_id=1, source_target_pairs={{0,1},{1,0},{2,3},{3,2},{4,5},{5,4},{6,7},{7,6},{8,9},{9,8},{10,11... | collective-permute-start | bytes 98312 | tf_op jit(solution)/shard_map/ppermute | solution.py:50
  143.3 33.8 %all-to-all-start = ((bf16[32,112,128]{2,1,0:T(8,128)(2,1)}), bf16[32,112,128]{2,1,0:T(8,128)(2,1)S(1)}, u32[]{:S(2)}, u32[]{:S(2)}) async-start(bf16[32,112,128]{2,1,0:T(8,128)(2,1)} %bitcast.7), calls=%async_computation | async-start | bytes 1835008 | tf_op jit(solution)/shard_map/all_to_all | solution.py:221
  156.9 2.2 %copy-start.3 = (bf16[4096,512]{1,0:T(8,128)(2,1)S(1)}, bf16[4096,512]{1,0:T(8,128)(2,1)}, u32[]{:S(2)}) copy-start(bf16[4096,512]{1,0:T(8,128)(2,1)} %all-gather.3.cloned.1.call-done) | copy-start | bytes 12582916
  177.1 2.2 %copy-start.4 = (bf16[4096,512]{1,0:T(8,128)(2,1)S(1)}, bf16[4096,512]{1,0:T(8,128)(2,1)}, u32[]{:S(2)}) copy-start(bf16[4096,512]{1,0:T(8,128)(2,1)} %all-gather.3.cloned.1.call-done) | copy-start | bytes 12582916
  179.3 4.2 %copy-start.7 = (bf16[64,7168]{1,0:T(8,128)(2,1)S(1)}, bf16[64,7168]{1,0:T(8,128)(2,1)}, u32[]{:S(2)}) copy-start(bf16[64,7168]{1,0:T(8,128)(2,1)} %get-tuple-element.30) | copy-start | bytes 2752516
  180.5 5.2 %collective-permute-start.12 = (bf16[112,512]{1,0:T(8,128)(2,1)S(1)}, bf16[112,512]{1,0:T(8,128)(2,1)S(1)}, u32[]{:S(2)}, u32[]{:S(2)}) collective-permute-start(bf16[112,512]{1,0:T(8,128)(2,1)S(1)} %fusion.3), channel_id=1, source_target_pairs={{0,128},{128,0},{1,129},{129,1},{2,130},{130,2},{3,131},{131,3},{4... | collective-permute-start | bytes 344072 | tf_op jit(solution)/shard_map/ppermute | solution.py:50
Sparse Core Ops, SparseCore 0:
  13.1 82.0 all-gather.2

commit v2 on v1

v2 whole, which is shorter than its diff:
```python
import functools
import math

import jax
import jax.numpy as jnp
import numpy as np
from jax import lax
from jax.experimental import pallas as pl
from jax.experimental.pallas import tpu as pltpu
from jax.sharding import Mesh
from jax.sharding import PartitionSpec as P

AXES = ("yh", "z", "x", "yl", "core")
BLOCK = 896
LANES = 128
VM = pl.BlockSpec(memory_space=pltpu.VMEM)
SM = pl.BlockSpec(memory_space=pltpu.SMEM)
ANY = pl.BlockSpec(memory_space=pl.ANY)


def paley_table():
    squares_set = set((factor * factor % 13 for factor in range(1, 13)))
    core_matrix = np.zeros((14, 14))
    core_matrix[0, 1:] = 1.0
    core_matrix[1:, 0] = 1.0
    for row_idx in range(13):
        for col_idx in range(13):
            offset = (col_idx - row_idx) % 13
            if offset != 0:
                core_matrix[row_idx + 1, col_idx + 1] = 1.0 if offset in squares_set else -1.0
    first_pat = np.array([[1.0, -1.0], [-1.0, -1.0]])
    second_pat = np.array([[1.0, 1.0], [1.0, -1.0]])
    return np.kron(core_matrix, first_pat) + np.kron(np.eye(14), second_pat)


def sylvester_table(order):
    result = np.ones((1, 1))
    base_pat = np.array([[1.0, 1.0], [1.0, -1.0]])
    while result.shape[0] < order:
        result = np.kron(base_pat, result)
    return result


def block_table():
    return np.kron(sylvester_table(BLOCK // 28), paley_table())


def swap(value, axis):
    return lax.ppermute(value, axis, [(0, 1), (1, 0)])


def shift(value, axis, by):
    size = lax.axis_size(axis)
    return lax.ppermute(value, axis, [(i, (i + by) % size) for i in range(size)])


def params(mib):
    return pltpu.CompilerParams(vmem_limit_bytes=mib * 2**20)


def cost(flops, nbytes):
    return pl.CostEstimate(flops=flops, bytes_accessed=nbytes, transcendentals=0)


def butterfly(parts):
    parts = list(parts)
    step = 1
    while step < len(parts):
        for base in range(len(parts)):
            if base & step == 0:
                a, b = parts[base], parts[base + step]
                parts[base], parts[base + step] = a + b, a - b
        step *= 2
    return parts


def flip_kernel(h_ref, sign_ref, *rest):
    out_ref = rest[-1]
    sign = (2 * sign_ref[...] - 1).astype(jnp.float32)
    out_ref[...] = (h_ref[...].astype(jnp.float32) * sign).astype(jnp.bfloat16)


def flip(hidden, sign_bits, chunk, rows, after=()):
    cols = hidden.shape[1]
    wide = 2 * BLOCK
    return pl.pallas_call(
        flip_kernel,
        grid=(cols // wide,),
        out_shape=jax.ShapeDtypeStruct((rows, cols), jnp.bfloat16),
        in_specs=[
            pl.BlockSpec((rows, wide), lambda j: (chunk, j)),
            pl.BlockSpec((1, wide), lambda j: (0, j)),
        ]
        + [ANY] * len(after),
        out_specs=pl.BlockSpec((rows, wide), lambda j: (0, j)),
        compiler_params=params(16),
        cost_estimate=cost(rows * cols, 4 * rows * cols),
        name="flip",
    )(hidden, sign_bits, *after)


def fold_kernel(sgn_ref, a_ref, b_ref, *rest):
    out_ref = rest[-1]
    total = sgn_ref[0] * a_ref[...].astype(jnp.float32) + b_ref[...].astype(jnp.float32)
    out_ref[...] = total.astype(jnp.bfloat16)


def fold(sgn, a, b, after=()):
    rows, cols = a.shape
    wide = 2 * BLOCK
    block = pl.BlockSpec((rows, wide), lambda j: (0, j))
    return pl.pallas_call(
        fold_kernel,
        grid=(cols // wide,),
        out_shape=jax.ShapeDtypeStruct((rows, cols), jnp.bfloat16),
        in_specs=[SM, block, block] + [ANY] * len(after),
        out_specs=block,
        compiler_params=params(16),
        cost_estimate=cost(2 * rows * cols, 6 * rows * cols),
        name="fold",
    )(sgn, a, b, *after)


def finish_kernel(sgn_ref, a_ref, b_ref, sign_ref, *rest):
    out_ref = rest[-1]
    total = sgn_ref[0] * a_ref[...].astype(jnp.float32) + b_ref[...].astype(jnp.float32)
    sign = (2 * sign_ref[...] - 1).astype(jnp.float32)
    out_ref[...] = (total * sign).astype(jnp.bfloat16)


def finish(sgn, a, b, sign_bits, chunk, into=None):
    rows, cols = a.shape
    wide = 2 * BLOCK
    block = pl.BlockSpec((rows, wide), lambda j: (0, j))
    more = [] if into is None else [into]
    return pl.pallas_call(
        finish_kernel,
        grid=(cols // wide,),
        out_shape=jax.ShapeDtypeStruct((2 * rows, cols), jnp.bfloat16),
        in_specs=[SM, block, block, pl.BlockSpec((1, wide), lambda j: (0, j))] + [ANY] * len(more),
        out_specs=pl.BlockSpec((rows, wide), lambda j: (chunk, j)),
        input_output_aliases={4: 0} if more else {},
        compiler_params=params(16),
        cost_estimate=cost(2 * rows * cols, 6 * rows * cols),
        name="finish",
    )(sgn, a, b, sign_bits, *more)


def back_kernel(go_ref, w_ref, *rest):
    out_ref = rest[-1]
    grad = lax.dot_general(go_ref[...], w_ref[...], (((1,), (1,)), ((), ())), preferred_element_type=jnp.float32)
    out_ref[...] = grad.astype(out_ref.dtype)


def back(grad_out, weight, after=()):
    rows, wide = grad_out.shape
    cols = weight.shape[0]
    return pl.pallas_call(
        back_kernel,
        grid=(cols // BLOCK,),
        out_shape=jax.ShapeDtypeStruct((rows, cols), jnp.float32),
        in_specs=[
            pl.BlockSpec((rows, wide), lambda j: (0, 0)),
            pl.BlockSpec((BLOCK, wide), lambda j: (j, 0)),
        ]
        + [ANY] * len(after),
        out_specs=pl.BlockSpec((rows, BLOCK), lambda j: (0, j)),
        compiler_params=params(24),
        cost_estimate=cost(2 * rows * cols * wide, 2 * cols * wide + 4 * rows * cols),
        name="back",
    )(grad_out, weight, *after)


def project_kernel(q0_ref, q1_ref, w_ref, *rest):
    out_ref, acc_ref = rest[-2:]
    j = pl.program_id(0)
    quant = jnp.concatenate([q0_ref[...], q1_ref[...]], axis=0)
    part = jnp.dot(quant, w_ref[...], preferred_element_type=jnp.float32)

    @pl.when(j == 0)
    def _():
        acc_ref[...] = part

    @pl.when(j > 0)
    def _():
        acc_ref[...] += part

    @pl.when(j == pl.num_programs(0) - 1)
    def _():
        out_ref[...] = acc_ref[...].astype(out_ref.dtype)


def project(quants, weight, after=()):
    rows, cols = quants[0].shape
    wide = weight.shape[1]
    block = pl.BlockSpec((rows, BLOCK), lambda j: (0, j))
    return pl.pallas_call(
        project_kernel,
        grid=(cols // BLOCK,),
        out_shape=jax.ShapeDtypeStruct((2 * rows, wide), jnp.bfloat16),
        in_specs=[block, block, pl.BlockSpec((BLOCK, wide), lambda j: (j, 0))] + [ANY] * len(after),
        out_specs=pl.BlockSpec((2 * rows, wide), lambda j: (0, 0)),
        scratch_shapes=[pltpu.VMEM((2 * rows, wide), jnp.float32)],
        compiler_params=params(24),
        cost_estimate=cost(4 * rows * cols * wide, 2 * cols * wide),
        name="project",
    )(*quants, weight, *after)


def turn_kernel(nblk, norm, n_in, sgn_ref, *refs):
    ins, (table_ref, bound_ref, gq_ref), refs = refs[:n_in], refs[n_in : n_in + 3], refs[n_in + 3 :]
    q_ref, qt_ref, s_ref, w_ref, spun_ref = refs[-5:]
    rows = ins[0].shape[0]
    so_core, so_y = sgn_ref[0], sgn_ref[1]
    for j in range(nblk):
        cols = pl.ds(j * BLOCK, BLOCK)
        parts = [r[:, cols].astype(jnp.float32) for r in ins]
        if n_in == 4:
            parts = [so_core * parts[0] + parts[1], so_core * parts[2] + parts[3]]
        w_ref[pl.ds(j * rows, rows), :] = (so_y * parts[0] + parts[1]).astype(jnp.bfloat16)
    spun_ref[...] = jnp.dot(w_ref[...], table_ref[...], preferred_element_type=jnp.float32)
    half = nblk // 2
    for lane in range(BLOCK // LANES):
        lcols = pl.ds(lane * LANES, LANES)
        parts = butterfly([spun_ref[pl.ds(j * rows, rows), lcols] for j in range(nblk)])
        quants = []
        for j in range(nblk):
            group = j * (BLOCK // LANES) + lane
            bound = bound_ref[:, group : group + 1]
            ratio = jnp.tanh(parts[j] * (norm / bound))
            quant = bound * ratio
            cols = pl.ds(j * BLOCK + lane * LANES, LANES)
            q_ref[:, cols] = quant.astype(jnp.bfloat16)
            grad = gq_ref[:, cols] * (1.0 - ratio * ratio)
            w_ref[pl.ds(j * rows, rows), lcols] = grad.astype(jnp.bfloat16)
            quants.append(quant)
        for j in range(half):
            both = jnp.concatenate([quants[j], quants[j + half]], axis=0)
            qt_ref[pl.ds(j * BLOCK + lane * LANES, LANES), :] = both.T.astype(jnp.bfloat16)
    spun_ref[...] = jnp.dot(w_ref[...], table_ref[...], preferred_element_type=jnp.float32)
    for lane in range(BLOCK // LANES):
        lcols = pl.ds(lane * LANES, LANES)
        parts = butterfly([spun_ref[pl.ds(j * rows, rows), lcols] for j in range(nblk)])
        for j in range(nblk):
            s_ref[:, pl.ds(j * BLOCK + lane * LANES, LANES)] = (parts[j] * norm).astype(jnp.bfloat16)


def turn(sgn, ins, table, bound, gq, chunk, norm, after=()):
    rows, cols = ins[0].shape
    nblk = cols // BLOCK
    return pl.pallas_call(
        functools.partial(turn_kernel, nblk, norm, len(ins)),
        grid=(1,),
        out_shape=(
            jax.ShapeDtypeStruct((rows, cols), jnp.bfloat16),
            jax.ShapeDtypeStruct((cols // 2, 2 * rows), jnp.bfloat16),
            jax.ShapeDtypeStruct((rows, cols), jnp.bfloat16),
        ),
        in_specs=[SM]
        + [VM] * (len(ins) + 1)
        + [
            pl.BlockSpec((rows, bound.shape[1]), lambda i: (chunk, 0)),
            pl.BlockSpec((rows, cols), lambda i: (chunk, 0)),
        ]
        + [ANY] * len(after),
        out_specs=(VM, VM, VM),
        scratch_shapes=[
            pltpu.VMEM((nblk * rows, BLOCK), jnp.bfloat16),
            pltpu.VMEM((nblk * rows, BLOCK), jnp.float32),
        ],
        compiler_params=params(44),
        cost_estimate=cost(4 * rows * cols * BLOCK, 2 * rows * cols * (len(ins) + 5)),
        name="turn",
    )(sgn, *ins, table, bound, gq, *after)


def weight_grad_kernel(nsrc, rows, chunk, src_ref, r_ref, mine_ref, theirs_ref, acc_in_ref, out_ref, lhs_ref, rhs_ref):
    toks = LANES // 2
    low = lax.broadcasted_iota(jnp.int32, (rows, LANES), 1) < toks
    is_mine = src_ref[nsrc] == chunk
    for s in range(nsrc):
        value = r_ref[src_ref[s]]
        zero = jnp.zeros_like(value)
        cols = pl.ds(s * LANES, LANES)
        lhs_ref[0:rows, cols] = jnp.where(low, value, zero)
        lhs_ref[rows : 2 * rows, cols] = jnp.where(low, zero, value)
        here = pl.ds(s * toks, toks)
        grads = jnp.where(is_mine, mine_ref[here, :], theirs_ref[here, :])
        rhs_ref[pl.ds(s * LANES, toks), :] = grads
        rhs_ref[pl.ds(s * LANES + toks, toks), :] = grads
    out_ref[...] = acc_in_ref[...] + jnp.dot(lhs_ref[...], rhs_ref[...], preferred_element_type=jnp.float32)


def weight_grad(sources, received, mine, theirs, chunk, acc):
    nsrc, rows, _ = received.shape
    wide = mine.shape[1]
    return pl.pallas_call(
        functools.partial(weight_grad_kernel, nsrc, rows, chunk),
        grid=(1,),
        out_shape=jax.ShapeDtypeStruct((2 * rows, wide), jnp.float32),
        in_specs=[SM, VM, VM, VM, VM],
        out_specs=VM,
        scratch_shapes=[
            pltpu.VMEM((2 * rows, nsrc * LANES), jnp.bfloat16),
            pltpu.VMEM((nsrc * LANES, wide), jnp.bfloat16),
        ],
        compiler_params=params(40),
        cost_estimate=cost(8 * rows * nsrc * LANES * wide, 2 * nsrc * LANES * (rows + wide)),
        name="weight_grad",
    )(sources, received, mine, theirs, acc)


def gather_ring(value):
    nx, nz = lax.axis_size("x"), lax.axis_size("z")
    up, down = shift(value, "x", 1), shift(value, "x", nx - 1)
    far = shift(value, "x", 2)
    here = jnp.concatenate([value, up, far, down], axis=0)
    blocks = [None] * nz
    blocks[0] = here
    forth = back_ = here
    for step in range(1, nz // 2 + 1):
        forth = shift(forth, "z", 1)
        blocks[step] = forth
        if step < nz // 2:
            back_ = shift(back_, "z", nz - 1)
            blocks[nz - step] = back_
    return jnp.concatenate(blocks, axis=0)


def relative_sources():
    nx, nz = lax.axis_size("x"), lax.axis_size("z")
    z, x = lax.axis_index("z"), lax.axis_index("x")
    dz, dx = jnp.arange(nz)[:, None], jnp.arange(nx)[None, :]
    return (((z - dz) % nz) * nx + (x - dx) % nx).reshape(-1)


def exchange_zx(quant_t):
    nsrc = lax.axis_size("z") * lax.axis_size("x")
    blocks = quant_t.reshape(nsrc, -1, quant_t.shape[1])
    return lax.all_to_all(blocks, ("z", "x"), 0, 0, tiled=True)


def local(hidden, sign_bits, exponents, down_weight, grad_out):
    tok_count, ff_local = hidden.shape
    n_tensor = lax.axis_size("yl") * lax.axis_size("core")
    n_data = lax.axis_size("yh") * lax.axis_size("z") * lax.axis_size("x")
    norm = 1.0 / math.sqrt(ff_local * n_tensor)
    half = tok_count // 2
    table = jnp.asarray(block_table(), jnp.bfloat16)
    sign_bits = sign_bits.reshape(1, ff_local)
    core, yl, yh = lax.axis_index("core"), lax.axis_index("yl"), lax.axis_index("yh")
    so_core = (1 - 2 * core).astype(jnp.float32)
    so_y = (1 - 2 * yl).astype(jnp.float32)
    sgn_c, sgn_y, sgn = so_core[None], so_y[None], jnp.stack([so_core, so_y])
    bound = 448.0 * jnp.exp2(exponents.astype(jnp.float32))

    flip0 = flip(hidden, sign_bits, 0, half)
    far0 = swap(flip0, "yl")
    flip1 = flip(hidden, sign_bits, 1, half, after=(flip0,))
    near1 = swap(flip1, "core")
    near0 = swap(flip0, "core")
    both1 = fold(sgn_c, flip1, near1)
    far1 = swap(both1, "yl")
    gq = back(grad_out, down_weight, after=(both1,))

    mine = gather_ring(lax.dynamic_slice_in_dim(grad_out, core * half, half, 0))
    theirs = swap(mine, "core")
    sources = jnp.concatenate([relative_sources(), core[None]]).astype(jnp.int32)

    q0, qt0, s0 = turn(sgn, (flip0, near0, far0, swap(far0, "core")), table, bound, gq, 0, norm)
    sent0 = swap(s0, "core")
    got0 = exchange_zx(qt0)
    fold0 = fold(sgn_c, s0, sent0)
    cross0 = swap(fold0, "yl")

    q1, qt1, s1 = turn(sgn, (both1, far1), table, bound, gq, 1, norm, after=(fold0,))
    sent1 = swap(s1, "core")
    got1 = exchange_zx(qt1)
    fold1 = fold(sgn_c, s1, sent1)
    cross1 = swap(fold1, "yl")

    out_all = project((q0, q1), down_weight, after=(fold1,)).reshape(2, 2, -1, down_weight.shape[1])
    keep = lax.dynamic_index_in_dim(out_all, yl, 0, keepdims=False)
    give = lax.dynamic_index_in_dim(out_all, 1 - yl, 0, keepdims=False)
    summed = keep.astype(jnp.float32) + swap(give, "yl").astype(jnp.float32)
    keep = lax.dynamic_index_in_dim(summed, core, 0, keepdims=False)
    give = lax.dynamic_index_in_dim(summed, 1 - core, 0, keepdims=False).astype(jnp.bfloat16)
    output = (keep + swap(give, "core").astype(jnp.float32)).astype(jnp.bfloat16)

    acc = jnp.zeros((2 * got0.shape[1], grad_out.shape[1]), jnp.float32)
    acc = weight_grad(sources, got0, mine, theirs, 0, acc)
    acc = weight_grad(sources, got1, mine, theirs, 1, acc)
    acc = acc.reshape(2, -1, grad_out.shape[1])
    keep = lax.dynamic_index_in_dim(acc, yh, 0, keepdims=False)
    give = lax.dynamic_index_in_dim(acc, 1 - yh, 0, keepdims=False).astype(jnp.bfloat16)
    inv_root = 1.0 / math.sqrt(tok_count * n_data)
    grad_weight = (keep + swap(give, "yh").astype(jnp.float32)) * inv_root

    grad_hidden = finish(sgn_y, fold0, cross0, sign_bits, 0)
    grad_hidden = finish(sgn_y, fold1, cross1, sign_bits, 1, into=grad_hidden)
    return (output, grad_hidden, grad_weight)


def solution(mesh):
    fine = Mesh(mesh.devices.reshape(2, 8, 4, 2, 2), AXES)
    dp, tensor = ("yh", "z", "x"), ("yl", "core")
    return jax.shard_map(
        local,
        mesh=fine,
        in_specs=(P(dp, tensor), P(tensor), P(dp, tensor), P(tensor, None), P(dp, None)),
        out_specs=(P(dp + tensor, None), P(dp, tensor), P(tensor + dp, None)),
        check_vma=False,
    )
```

time: 195 us -> 188 us (0.964)
  local copies, waits for them, and re-layouts: 10.1 us -> 34.4 us
  waiting for transfers between devices: 85 us -> 67 us
  between operations: 14.2 us -> 0.96 us
  other arithmetic: 14.3 us -> 2.35 us
  starting transfers between devices: 41.6 us -> 49.4 us
  Pallas kernels: 28.1 us -> 33.1 us
    unnamed x26 -> x68, local copies, waits for them, and re-layouts: 9.89 us -> 33.3 us
    all_to_all x2, waiting for transfers between devices: 16.9 us -> 0.01 us  [exchange_zx(): return lax.all_to_all(blocks, ('z', 'x'), 0, 0, tiled=True)]
    ppermute x13 -> x23, starting transfers between devices: 20.9 us -> 33.9 us  [the longest x13 18.1 us: swap(): return lax.ppermute(value, axis, [(0, 1), (1, 0)])]
    mul x3 -> x2, other arithmetic: 7.26 us -> 0.73 us  [the longest x1 0.72 us: local(): grad_weight = (keep + swap(give, 'yh').astype(jnp.float32)) * inv_root]
    all_to_all x2, starting transfers between devices: 20.6 us -> 15.5 us  [exchange_zx(): return lax.all_to_all(blocks, ('z', 'x'), 0, 0, tiled=True)]
    pallas_call x6 -> x13, Pallas kernels: 28.1 us -> 33.1 us  [the longest x2 9.51 us: turn(): pl.pallas_call(functools.partial(turn_kernel, nblk, norm, len(ins)), grid...]
    convert_element_type x3 -> x0, other arithmetic: 4.94 us -> none  [the longest x2 4.19 us: local(): (so_core * spun.astype(jnp.float32) + partner.astype(jnp.float32)).astype...]
    ppermute x13 -> x23, waiting for transfers between devices: 68.1 us -> 67 us  [the longest x13 38 us: swap(): return lax.ppermute(value, axis, [(0, 1), (1, 0)])]
  transfers between devices with their start and end apart: 16 -> 25, of which waited for: 5 -> 9; matrix products, arithmetic and copies ran while one was open for 5% -> 8% of each run, Pallas kernels for 14% -> 17%
where the time goes in v2:
time: 188 us; the launch traced here: 187 us
  waiting for transfers between devices  67 us (36%)
  starting transfers between devices  49.4 us (26%)
  local copies, waits for them, and re-layouts  34.4 us (18%)
  Pallas kernels  33.1 us (18%)
  other arithmetic  2.35 us (1%)
    ppermute x13, waiting for transfers between devices, swap(): return lax.ppermute(value, axis, [(0, 1), (1, 0)])  38 us
    unnamed x68, local copies, waits for them, and re-layouts  33.3 us
    ppermute x10, waiting for transfers between devices, shift(): lax.ppermute(value, axis, [(i, (i + by) % size) for i in range(size)])  29 us
    ppermute x13, starting transfers between devices, swap(): return lax.ppermute(value, axis, [(0, 1), (1, 0)])  18.1 us
    ppermute x10, starting transfers between devices, shift(): lax.ppermute(value, axis, [(i, (i + by) % size) for i in range(size)])  15.8 us
    all_to_all x2, starting transfers between devices, exchange_zx(): return lax.all_to_all(blocks, ('z', 'x'), 0, 0, tiled=True)  15.5 us
    pallas_call x2, Pallas kernels, turn(): pl.pallas_call(functools.partial(turn_kernel, nblk, norm, len(ins)), grid...  9.51 us
    pallas_call x2, Pallas kernels, finish(): pl.pallas_call(finish_kernel, grid=(cols // wide,), out_shape=jax.ShapeDt...  6.97 us
  transfers between devices with their start and end apart: 25, of which 9 were waited for; matrix products, arithmetic and copies ran while one was open for 8% of the time, Pallas kernels for 17%

profile of v2, /device:TPU:1, one launch (start us, length us, event | category | flops | bytes accessed | tf_op | source)
XLA Modules:
  0.0 187.2 jit_solution(17675220684448752157)
XLA Ops:
  3.3 2.2 %collective-permute-start.1 = (bf16[64,7168]{1,0:T(8,128)(2,1)S(1)}, bf16[64,7168]{1,0:T(8,128)(2,1)}, u32[]{:S(2)}, u32[]{:S(2)}) collective-permute-start(bf16[64,7168]{1,0:T(8,128)(2,1)S(1)} %flip.2.rest_0_.refs_0_), channel_id=1, source_target_pairs={{0,2},{2,0},{1,3},{3,1},{4,6},{6,4},{5,7},{7,5},{8,10},{10,8},{9,1... | collective-permute-start | bytes 2752520 | tf_op jit(solution)/shard_map/ppermute | solution.py:49
  9.1 15.2 %collective-permute-done.1.refs_2_ = bf16[64,7168]{1,0:T(8,128)(2,1)} collective-permute-done((bf16[64,7168]{1,0:T(8,128)(2,1)S(1)}, bf16[64,7168]{1,0:T(8,128)(2,1)}, u32[]{:S(2)}, u32[]{:S(2)}) %collective-permute-start.1) | collective-permute-done | bytes 917536 | tf_op jit(solution)/shard_map/ppermute | solution.py:49
  24.3 2.6 %collective-permute-start.2 = (bf16[64,7168]{1,0:T(8,128)(2,1)}, bf16[64,7168]{1,0:T(8,128)(2,1)}, u32[]{:S(2)}, u32[]{:S(2)}) collective-permute-start(bf16[64,7168]{1,0:T(8,128)(2,1)} %collective-permute-done.1.refs_2_), channel_id=1, source_target_pairs={{0,1},{1,0},{2,3},{3,2},{4,5},{5,4},{6,7},{7,6},{8,9},{9,8},{10,11... | collective-permute-start | bytes 2752520 | tf_op jit(solution)/shard_map/ppermute | solution.py:49
  26.9 2.9 %collective-permute-start.12 = (bf16[64,512]{1,0:T(8,128)(2,1)S(1)}, bf16[64,512]{1,0:T(8,128)(2,1)S(1)}, u32[]{:S(2)}, u32[]{:S(2)}) collective-permute-start(bf16[64,512]{1,0:T(8,128)(2,1)S(1)} %get-tuple-element.16), channel_id=1, source_target_pairs={{0,8},{4,12},{8,0},{12,4},{1,9},{5,13},{9,1},{13,5},{2,10},{6,14},... | collective-permute-start | bytes 196616 | tf_op jit(solution)/shard_map/ppermute | solution.py:54
  34.4 1.6 collective-permute-start.14
  36.2 4.0 %collective-permute-start.18 = (bf16[256,512]{1,0:T(8,128)(2,1)}, bf16[256,512]{1,0:T(8,128)(2,1)S(1)}, u32[]{:S(2)}, u32[]{:S(2)}) collective-permute-start(bf16[256,512]{1,0:T(8,128)(2,1)} %pad_maximum_fusion), channel_id=1, source_target_pairs={{0,112},{16,0},{32,16},{48,32},{64,48},{80,64},{96,80},{112,96},{1... | collective-permute-start | bytes 786440 | tf_op jit(solution)/shard_map/ppermute | solution.py:54
  40.2 5.8 %collective-permute-done.14 = bf16[256,512]{1,0:T(8,128)(2,1)S(1)} collective-permute-done((bf16[256,512]{1,0:T(8,128)(2,1)}, bf16[256,512]{1,0:T(8,128)(2,1)S(1)}, u32[]{:S(2)}, u32[]{:S(2)}) %collective-permute-start.14) | collective-permute-done | bytes 262176 | tf_op jit(solution)/shard_map/ppermute | solution.py:54
  49.1 2.7 %collective-permute-start.19 = (bf16[256,512]{1,0:T(8,128)(2,1)S(1)}, bf16[256,512]{1,0:T(8,128)(2,1)}, u32[]{:S(2)}, u32[]{:S(2)}) collective-permute-start(bf16[256,512]{1,0:T(8,128)(2,1)S(1)} %collective-permute-done.18), channel_id=1, source_target_pairs={{0,112},{16,0},{32,16},{48,32},{64,48},{80,64},{96,80},{112,96},{1... | collective-permute-start | bytes 786440 | tf_op jit(solution)/shard_map/ppermute | solution.py:54
  51.7 2.0 %collective-permute-done.15 = bf16[256,512]{1,0:T(8,128)(2,1)} collective-permute-done((bf16[256,512]{1,0:T(8,128)(2,1)S(1)}, bf16[256,512]{1,0:T(8,128)(2,1)}, u32[]{:S(2)}, u32[]{:S(2)}) %collective-permute-start.15) | collective-permute-done | bytes 262176 | tf_op jit(solution)/shard_map/ppermute | solution.py:54
  56.4 3.1 %copy-done.1 = bf16[7168,512]{1,0:T(8,128)(2,1)S(1)} copy-done((bf16[7168,512]{1,0:T(8,128)(2,1)S(1)}, bf16[7168,512]{1,0:T(8,128)(2,1)}, u32[]{:S(2)}) %copy-start.1) | copy-done | bytes 7340056
  59.5 3.8 %back.1.refs_6_.refs_4_ = f32[128,7168]{1,0:T(8,128)S(1)} custom-call(bf16[128,512]{1,0:T(8,128)(2,1)S(1)} %copy-done.23, bf16[7168,512]{1,0:T(8,128)(2,1)S(1)} %copy-done.1, bf16[64,7168]{1,0:T(8,128)(2,1)S(1)} %fold.3.rest_0_.refs_0_), custom_call_target="tpu_custom_call" | custom-call | flops 939524096 | bytes 11010048 | tf_op jit(solution)/shard_map/back/pallas_call | solution.py:158
  63.3 1.8 copy-done
  65.1 5.3 %turn.2 = (bf16[64,7168]{1,0:T(8,128)(2,1)S(1)}, bf16[3584,128]{1,0:T(8,128)(2,1)S(1)}, bf16[64,7168]{1,0:T(8,128)(2,1)S(1)}) custom-call(f32[2]{0:T(128)S(1)} %pad_maximum_fusion.1.sgn_ref, bf16[64,7168]{1,0:T(8,128)(2,1)S(1)} %flip.2.rest_0_.refs_0_, bf16[64,7168]{1,0:T(8,128)(2,1)} %collective-permute-done.refs_1_, ...), custom_call_target="tpu_custom_call" | custom-call | flops 1644167168 | bytes 8257536 | tf_op jit(solution)/shard_map/turn/pallas_call | solution.py:251
  73.2 8.3 %all-to-all-start.1 = ((bf16[32,112,128]{2,1,0:T(8,128)(2,1)}), bf16[32,112,128]{2,1,0:T(8,128)(2,1)S(1)}, u32[]{:S(2)}, u32[]{:S(2)}) async-start(bf16[32,112,128]{2,1,0:T(8,128)(2,1)} %bitcast.26), calls=%async_computation.1 | async-start | bytes 1835008 | tf_op jit(solution)/shard_map/all_to_all | solution.py:340
  85.5 1.7 constant_dynamic-update-slice_fusion.5
  87.2 1.7 constant_dynamic-update-slice_fusion.4
  90.2 18.2 %collective-permute-done.17 = bf16[256,512]{1,0:T(8,128)(2,1)S(1)} collective-permute-done((bf16[256,512]{1,0:T(8,128)(2,1)}, bf16[256,512]{1,0:T(8,128)(2,1)S(1)}, u32[]{:S(2)}, u32[]{:S(2)}) %collective-permute-start.17) | collective-permute-done | bytes 262176 | tf_op jit(solution)/shard_map/ppermute | solution.py:54
  109.8 2.7 %collective-permute-start.5 = (bf16[64,7168]{1,0:T(8,128)(2,1)S(1)}, bf16[64,7168]{1,0:T(8,128)(2,1)S(1)}, u32[]{:S(2)}, u32[]{:S(2)}) collective-permute-start(bf16[64,7168]{1,0:T(8,128)(2,1)S(1)} %copy-done.19), channel_id=1, source_target_pairs={{0,1},{1,0},{2,3},{3,2},{4,5},{5,4},{6,7},{7,6},{8,9},{9,8},{10,11... | collective-permute-start | bytes 2752520 | tf_op jit(solution)/shard_map/ppermute | solution.py:49
  112.5 1.7 constant_dynamic-update-slice_fusion.1
  115.5 4.2 %turn.3 = (bf16[64,7168]{1,0:T(8,128)(2,1)S(1)}, bf16[3584,128]{1,0:T(8,128)(2,1)S(1)}, bf16[64,7168]{1,0:T(8,128)(2,1)S(1)}) custom-call(f32[2]{0:T(128)S(1)} %pad_maximum_fusion.1.sgn_ref, bf16[64,7168]{1,0:T(8,128)(2,1)S(1)} %fold.3.rest_0_.refs_0_, bf16[64,7168]{1,0:T(8,128)(2,1)S(1)} %collective-permute-done.4.refs_1_, bf16[896,896]{1,0:T(8,128)(2,1)S(1)} %copy-done.5, ...), custom_call_target="tpu_custom_call" | custom-call | flops 1644167168 | bytes 6422528 | tf_op jit(solution)/shard_map/turn/pallas_call | solution.py:251
  122.6 7.2 %all-to-all-start = ((bf16[32,112,128]{2,1,0:T(8,128)(2,1)}), bf16[32,112,128]{2,1,0:T(8,128)(2,1)}, u32[]{:S(2)}, u32[]{:S(2)}) async-start(bf16[32,112,128]{2,1,0:T(8,128)(2,1)} %bitcast.25), calls=%async_computation | async-start | bytes 1835008 | tf_op jit(solution)/shard_map/all_to_all | solution.py:340
  134.3 2.2 %fold.5.rest_0_.a_ref = bf16[64,7168]{1,0:T(8,128)(2,1)S(1)} custom-call(f32[1]{0:T(128)} %bitcast.sgn_ref, bf16[64,7168]{1,0:T(8,128)(2,1)S(1)} %copy-done.17, bf16[64,7168]{1,0:T(8,128)(2,1)} %collective-permute-done.6.b_ref), custom_call_target="tpu_custom_call" | custom-call | flops 917504 | bytes 2752512 | tf_op jit(solution)/shard_map/fold/pallas_call | solution.py:112
  137.9 3.1 %copy-done.2 = bf16[7168,512]{1,0:T(8,128)(2,1)S(1)} copy-done((bf16[7168,512]{1,0:T(8,128)(2,1)S(1)}, bf16[7168,512]{1,0:T(8,128)(2,1)}, u32[]{:S(2)}) %copy-start.2) | copy-done | bytes 7340056
  142.2 3.0 %project.1 = bf16[128,512]{1,0:T(8,128)(2,1)S(1)} custom-call(bf16[64,7168]{1,0:T(8,128)(2,1)S(1)} %copy-done.7, bf16[64,7168]{1,0:T(8,128)(2,1)S(1)} %copy-done.9, bf16[7168,512]{1,0:T(8,128)(2,1)S(1)} %copy-done.2, bf16[64,7168]{1,0:T(8,128)(2,1)S(1)} %fold.5.rest_0_.a_ref), custom_call_target="tpu_custom_call" | custom-call | flops 939524096 | bytes 7340032 | tf_op jit(solution)/shard_map/project/pallas_call | solution.py:197
  145.5 2.8 %weight_grad.2.acc_in_ref = f32[224,512]{1,0:T(8,128)S(1)} custom-call(s32[33]{0:T(128)S(1)} %pad_add_fusion.src_ref, bf16[32,112,128]{2,1,0:T(8,128)(2,1)S(1)} %copy-done.11, bf16[2048,512]{1,0:T(8,128)(2,1)S(1)} %copy-done.24, bf16[2048,512]{1,0:T(8,128)(2,1)} %collective-permute-done.21.theirs_ref, f32[224,512]{1,0:T(8,128)S(1)} %broadcast_in_dim.5.acc_in_ref), custom_call_target="tpu_custom_call" | custom-call | flops 1879048192 | bytes 5111808 | tf_op jit(solution)/shard_map/weight_grad/pallas_call | solution.py:297
  148.3 4.4 %collective-permute-done.10.b_ref = bf16[64,7168]{1,0:T(8,128)(2,1)} collective-permute-done((bf16[64,7168]{1,0:T(8,128)(2,1)S(1)}, bf16[64,7168]{1,0:T(8,128)(2,1)}, u32[]{:S(2)}, u32[]{:S(2)}) %collective-permute-start.10) | collective-permute-done | bytes 917536 | tf_op jit(solution)/shard_map/ppermute | solution.py:49
  152.7 3.5 %finish.2.rest_0_ = bf16[128,7168]{1,0:T(8,128)(2,1)} custom-call(f32[1]{0:T(128)} %bitcast.1.sgn_ref, bf16[64,7168]{1,0:T(8,128)(2,1)S(1)} %fold.4.refs_5_.a_ref, bf16[64,7168]{1,0:T(8,128)(2,1)} %collective-permute-done.10.b_ref, s32[1,7168]{1,0:T(1,128)S(1)} %bitcast.31), custom_call_target="tpu_custom_call" | custom-call | flops 917504 | bytes 2752512 | tf_op jit(solution)/shard_map/finish/pallas_call | solution.py:136
  156.2 17.5 %collective-permute-done.7 = bf16[2,32,512]{2,1,0:T(8,128)(2,1)S(1)} collective-permute-done((bf16[2,32,512]{2,1,0:T(8,128)(2,1)S(1)}, bf16[2,32,512]{2,1,0:T(8,128)(2,1)S(1)}, u32[]{:S(2)}, u32[]{:S(2)}) %collective-permute-start.7) | collective-permute-done | bytes 65568 | tf_op jit(solution)/shard_map/ppermute | solution.py:49
  174.7 1.6 copy-done.25
  176.3 3.0 %weight_grad.3 = f32[224,512]{1,0:T(8,128)S(1)} custom-call(s32[33]{0:T(128)S(1)} %pad_add_fusion.src_ref, bf16[32,112,128]{2,1,0:T(8,128)(2,1)} %all-to-all-done.r_ref, bf16[2048,512]{1,0:T(8,128)(2,1)S(1)} %copy-done.25, bf16[2048,512]{1,0:T(8,128)(2,1)} %collective-permute-done.21.theirs_ref, f32[224,512]{1,0:T(8,128)S(1)} %weight_grad.2.acc_in_ref), custom_call_target="tpu_custom_call" | custom-call | flops 1879048192 | bytes 5111808 | tf_op jit(solution)/shard_map/weight_grad/pallas_call | solution.py:297
  179.3 3.0 %collective-permute-start.22 = (bf16[112,512]{1,0:T(8,128)(2,1)S(1)}, bf16[112,512]{1,0:T(8,128)(2,1)S(1)}, u32[]{:S(2)}, u32[]{:S(2)}) collective-permute-start(bf16[112,512]{1,0:T(8,128)(2,1)S(1)} %fusion.1), channel_id=1, source_target_pairs={{0,128},{128,0},{1,129},{129,1},{2,130},{130,2},{3,131},{131,3},{4... | collective-permute-start | bytes 344072 | tf_op jit(solution)/shard_map/ppermute | solution.py:49
  183.0 3.5 %finish.3 = bf16[128,7168]{1,0:T(8,128)(2,1)} custom-call(f32[1]{0:T(128)} %bitcast.1.sgn_ref, bf16[64,7168]{1,0:T(8,128)(2,1)S(1)} %fold.5.rest_0_.a_ref, bf16[64,7168]{1,0:T(8,128)(2,1)} %collective-permute-done.9.b_ref, s32[1,7168]{1,0:T(1,128)S(1)} %bitcast.32, bf16[128,7168]{1,0:T(8,128)(2,1)} %finish.2.rest_0_), custom_call_target="tpu_custom_call", output_to_operand_aliasing={{}: (4, {})} | custom-call | flops 917504 | bytes 2752512 | tf_op jit(solution)/shard_map/finish/pallas_call | solution.py:136
  (117 shorter events, 40.1 us)
Async XLA Ops:
  3.3 32.8 %copy-start.28 = (s32[128,56]{0,1:T(8,128)S(1)}, s32[128,56]{0,1:T(8,128)}, u32[]{:S(2)}) copy-start(s32[128,56]{0,1:T(8,128)} %param.8) | copy-start | bytes 86020
  3.3 21.0 %collective-permute-start.1 = (bf16[64,7168]{1,0:T(8,128)(2,1)S(1)}, bf16[64,7168]{1,0:T(8,128)(2,1)}, u32[]{:S(2)}, u32[]{:S(2)}) collective-permute-start(bf16[64,7168]{1,0:T(8,128)(2,1)S(1)} %flip.2.rest_0_.refs_0_), channel_id=1, source_target_pairs={{0,2},{2,0},{1,3},{3,1},{4,6},{6,4},{5,7},{7,5},{8,10},{10,8},{9,1... | collective-permute-start | bytes 2752520 | tf_op jit(solution)/shard_map/ppermute | solution.py:49
  5.9 47.9 %collective-permute-start.3 = (bf16[64,7168]{1,0:T(8,128)(2,1)S(1)}, bf16[64,7168]{1,0:T(8,128)(2,1)S(1)}, u32[]{:S(2)}, u32[]{:S(2)}) collective-permute-start(bf16[64,7168]{1,0:T(8,128)(2,1)S(1)} %flip.3.a_ref), channel_id=1, source_target_pairs={{0,1},{1,0},{2,3},{3,2},{4,5},{5,4},{6,7},{7,6},{8,9},{9,8},{10,11... | collective-permute-start | bytes 2752520 | tf_op jit(solution)/shard_map/ppermute | solution.py:49
  7.7 22.1 %collective-permute-start.11 = (bf16[64,512]{1,0:T(8,128)(2,1)S(1)}, bf16[64,512]{1,0:T(8,128)(2,1)S(1)}, u32[]{:S(2)}, u32[]{:S(2)}) collective-permute-start(bf16[64,512]{1,0:T(8,128)(2,1)S(1)} %get-tuple-element.16), channel_id=1, source_target_pairs={{0,4},{4,8},{8,12},{12,0},{1,5},{5,9},{9,13},{13,1},{2,6},{6,10},{... | collective-permute-start | bytes 196616 | tf_op jit(solution)/shard_map/ppermute | solution.py:54
  8.8 56.3 %collective-permute-start = (bf16[64,7168]{1,0:T(8,128)(2,1)S(1)}, bf16[64,7168]{1,0:T(8,128)(2,1)}, u32[]{:S(2)}, u32[]{:S(2)}) collective-permute-start(bf16[64,7168]{1,0:T(8,128)(2,1)S(1)} %flip.2.rest_0_.refs_0_), channel_id=1, source_target_pairs={{0,1},{1,0},{2,3},{3,2},{4,5},{5,4},{6,7},{7,6},{8,9},{9,8},{10,11... | collective-permute-start | bytes 2752520 | tf_op jit(solution)/shard_map/ppermute | solution.py:49
  24.3 40.7 %collective-permute-start.2 = (bf16[64,7168]{1,0:T(8,128)(2,1)}, bf16[64,7168]{1,0:T(8,128)(2,1)}, u32[]{:S(2)}, u32[]{:S(2)}) collective-permute-start(bf16[64,7168]{1,0:T(8,128)(2,1)} %collective-permute-done.1.refs_2_), channel_id=1, source_target_pairs={{0,1},{1,0},{2,3},{3,2},{4,5},{5,4},{6,7},{7,6},{8,9},{9,8},{10,11... | collective-permute-start | bytes 2752520 | tf_op jit(solution)/shard_map/ppermute | solution.py:49
  26.9 5.2 %collective-permute-start.12 = (bf16[64,512]{1,0:T(8,128)(2,1)S(1)}, bf16[64,512]{1,0:T(8,128)(2,1)S(1)}, u32[]{:S(2)}, u32[]{:S(2)}) collective-permute-start(bf16[64,512]{1,0:T(8,128)(2,1)S(1)} %get-tuple-element.16), channel_id=1, source_target_pairs={{0,8},{4,12},{8,0},{12,4},{1,9},{5,13},{9,1},{13,5},{2,10},{6,14},... | collective-permute-start | bytes 196616 | tf_op jit(solution)/shard_map/ppermute | solution.py:54
  29.8 3.9 %collective-permute-start.13 = (bf16[64,512]{1,0:T(8,128)(2,1)S(1)}, bf16[64,512]{1,0:T(8,128)(2,1)S(1)}, u32[]{:S(2)}, u32[]{:S(2)}) collective-permute-start(bf16[64,512]{1,0:T(8,128)(2,1)S(1)} %get-tuple-element.16), channel_id=1, source_target_pairs={{0,12},{4,0},{8,4},{12,8},{1,13},{5,1},{9,5},{13,9},{2,14},{6,2},{... | collective-permute-start | bytes 196616 | tf_op jit(solution)/shard_map/ppermute | solution.py:54
  34.4 11.6 %collective-permute-start.14 = (bf16[256,512]{1,0:T(8,128)(2,1)}, bf16[256,512]{1,0:T(8,128)(2,1)S(1)}, u32[]{:S(2)}, u32[]{:S(2)}) collective-permute-start(bf16[256,512]{1,0:T(8,128)(2,1)} %pad_maximum_fusion), channel_id=1, source_target_pairs={{0,16},{16,32},{32,48},{48,64},{64,80},{80,96},{96,112},{112,0},{1... | collective-permute-start | bytes 786440 | tf_op jit(solution)/shard_map/ppermute | solution.py:54
  36.2 12.8 %collective-permute-start.18 = (bf16[256,512]{1,0:T(8,128)(2,1)}, bf16[256,512]{1,0:T(8,128)(2,1)S(1)}, u32[]{:S(2)}, u32[]{:S(2)}) collective-permute-start(bf16[256,512]{1,0:T(8,128)(2,1)} %pad_maximum_fusion), channel_id=1, source_target_pairs={{0,112},{16,0},{32,16},{48,32},{64,48},{80,64},{96,80},{112,96},{1... | collective-permute-start | bytes 786440 | tf_op jit(solution)/shard_map/ppermute | solution.py:54
  46.0 7.7 %collective-permute-start.15 = (bf16[256,512]{1,0:T(8,128)(2,1)S(1)}, bf16[256,512]{1,0:T(8,128)(2,1)}, u32[]{:S(2)}, u32[]{:S(2)}) collective-permute-start(bf16[256,512]{1,0:T(8,128)(2,1)S(1)} %collective-permute-done.14), channel_id=1, source_target_pairs={{0,16},{16,32},{32,48},{48,64},{64,80},{80,96},{96,112},{112,0},{1... | collective-permute-start | bytes 786440 | tf_op jit(solution)/shard_map/ppermute | solution.py:54
  49.1 35.0 %collective-permute-start.19 = (bf16[256,512]{1,0:T(8,128)(2,1)S(1)}, bf16[256,512]{1,0:T(8,128)(2,1)}, u32[]{:S(2)}, u32[]{:S(2)}) collective-permute-start(bf16[256,512]{1,0:T(8,128)(2,1)S(1)} %collective-permute-done.18), channel_id=1, source_target_pairs={{0,112},{16,0},{32,16},{48,32},{64,48},{80,64},{96,80},{112,96},{1... | collective-permute-start | bytes 786440 | tf_op jit(solution)/shard_map/ppermute | solution.py:54
  53.7 28.4 %collective-permute-start.16 = (bf16[256,512]{1,0:T(8,128)(2,1)}, bf16[256,512]{1,0:T(8,128)(2,1)}, u32[]{:S(2)}, u32[]{:S(2)}) collective-permute-start(bf16[256,512]{1,0:T(8,128)(2,1)} %collective-permute-done.15), channel_id=1, source_target_pairs={{0,16},{16,32},{32,48},{48,64},{64,80},{80,96},{96,112},{112,0},{1... | collective-permute-start | bytes 786440 | tf_op jit(solution)/shard_map/ppermute | solution.py:54
  73.2 36.6 %copy-start.19 = (bf16[64,7168]{1,0:T(8,128)(2,1)S(1)}, bf16[64,7168]{1,0:T(8,128)(2,1)}, u32[]{:S(2)}) copy-start(bf16[64,7168]{1,0:T(8,128)(2,1)} %copy-done.18) | copy-start | bytes 2752516
  73.2 49.4 %all-to-all-start.1 = ((bf16[32,112,128]{2,1,0:T(8,128)(2,1)}), bf16[32,112,128]{2,1,0:T(8,128)(2,1)S(1)}, u32[]{:S(2)}, u32[]{:S(2)}) async-start(bf16[32,112,128]{2,1,0:T(8,128)(2,1)} %bitcast.26), calls=%async_computation.1 | async-start | bytes 1835008 | tf_op jit(solution)/shard_map/all_to_all | solution.py:340
  81.5 33.5 %copy-start.20 = (bf16[64,7168]{1,0:T(8,128)(2,1)S(1)}, bf16[64,7168]{1,0:T(8,128)(2,1)}, u32[]{:S(2)}) copy-start(bf16[64,7168]{1,0:T(8,128)(2,1)} %copy-done.18) | copy-start | bytes 2752516
  82.1 26.2 %collective-permute-start.17 = (bf16[256,512]{1,0:T(8,128)(2,1)}, bf16[256,512]{1,0:T(8,128)(2,1)S(1)}, u32[]{:S(2)}, u32[]{:S(2)}) collective-permute-start(bf16[256,512]{1,0:T(8,128)(2,1)} %collective-permute-done.16), channel_id=1, source_target_pairs={{0,16},{16,32},{32,48},{48,64},{64,80},{80,96},{96,112},{112,0},{1... | collective-permute-start | bytes 786440 | tf_op jit(solution)/shard_map/ppermute | solution.py:54
  84.1 25.0 %collective-permute-start.20 = (bf16[256,512]{1,0:T(8,128)(2,1)}, bf16[256,512]{1,0:T(8,128)(2,1)S(1)}, u32[]{:S(2)}, u32[]{:S(2)}) collective-permute-start(bf16[256,512]{1,0:T(8,128)(2,1)} %collective-permute-done.19), channel_id=1, source_target_pairs={{0,112},{16,0},{32,16},{48,32},{64,48},{80,64},{96,80},{112,96},{1... | collective-permute-start | bytes 786440 | tf_op jit(solution)/shard_map/ppermute | solution.py:54
  88.9 26.7 %collective-permute-start.4 = (bf16[64,7168]{1,0:T(8,128)(2,1)S(1)}, bf16[64,7168]{1,0:T(8,128)(2,1)S(1)}, u32[]{:S(2)}, u32[]{:S(2)}) collective-permute-start(bf16[64,7168]{1,0:T(8,128)(2,1)S(1)} %fold.3.rest_0_.refs_0_), channel_id=1, source_target_pairs={{0,2},{2,0},{1,3},{3,1},{4,6},{6,4},{5,7},{7,5},{8,10},{10,8},{9,1... | collective-permute-start | bytes 2752520 | tf_op jit(solution)/shard_map/ppermute | solution.py:49
  109.1 6.5 %copy-start.5 = (bf16[896,896]{1,0:T(8,128)(2,1)S(1)}, bf16[896,896]{1,0:T(8,128)(2,1)}, u32[]{:S(2)}) copy-start(bf16[896,896]{1,0:T(8,128)(2,1)} %constant.90.clone.refs_4_.refs_2_) | copy-start | bytes 4816900
  109.8 5.2 %collective-permute-start.5 = (bf16[64,7168]{1,0:T(8,128)(2,1)S(1)}, bf16[64,7168]{1,0:T(8,128)(2,1)S(1)}, u32[]{:S(2)}, u32[]{:S(2)}) collective-permute-start(bf16[64,7168]{1,0:T(8,128)(2,1)S(1)} %copy-done.19), channel_id=1, source_target_pairs={{0,1},{1,0},{2,3},{3,2},{4,5},{5,4},{6,7},{7,6},{8,9},{9,8},{10,11... | collective-permute-start | bytes 2752520 | tf_op jit(solution)/shard_map/ppermute | solution.py:49
  114.9 30.5 %collective-permute-start.21 = (bf16[2048,512]{1,0:T(8,128)(2,1)}, bf16[2048,512]{1,0:T(8,128)(2,1)}, u32[]{:S(2)}, u32[]{:S(2)}) collective-permute-start(bf16[2048,512]{1,0:T(8,128)(2,1)} %constant_dynamic-update-slice_fusion.mine_ref), channel_id=1, source_target_pairs={{0,1},{1,0},{2,3},{3,2},{4,5},{5,4},{6,7},{7,6},{8,9},{9,8},{10,11... | collective-permute-start | bytes 6291464 | tf_op jit(solution)/shard_map/ppermute | solution.py:49
  122.6 9.7 %copy-start.10 = (bf16[32,112,128]{2,1,0:T(8,128)(2,1)}, bf16[32,112,128]{2,1,0:T(8,128)(2,1)S(1)}, u32[]{:S(2)}) copy-start(bf16[32,112,128]{2,1,0:T(8,128)(2,1)S(1)} %all-to-all-done.1.r_ref) | copy-start | bytes 2752516
  122.6 15.4 %copy-start.7 = (bf16[64,7168]{1,0:T(8,128)(2,1)S(1)}, bf16[64,7168]{1,0:T(8,128)(2,1)}, u32[]{:S(2)}) copy-start(bf16[64,7168]{1,0:T(8,128)(2,1)} %copy-done.6) | copy-start | bytes 2752516
  122.6 52.1 %all-to-all-start = ((bf16[32,112,128]{2,1,0:T(8,128)(2,1)}), bf16[32,112,128]{2,1,0:T(8,128)(2,1)}, u32[]{:S(2)}, u32[]{:S(2)}) async-start(bf16[32,112,128]{2,1,0:T(8,128)(2,1)} %bitcast.25), calls=%async_computation | async-start | bytes 1835008 | tf_op jit(solution)/shard_map/all_to_all | solution.py:340
  129.8 3.3 %collective-permute-start.6 = (bf16[64,7168]{1,0:T(8,128)(2,1)}, bf16[64,7168]{1,0:T(8,128)(2,1)}, u32[]{:S(2)}, u32[]{:S(2)}) collective-permute-start(bf16[64,7168]{1,0:T(8,128)(2,1)} %copy-done.16), channel_id=1, source_target_pairs={{0,1},{1,0},{2,3},{3,2},{4,5},{5,4},{6,7},{7,6},{8,9},{9,8},{10,11... | collective-permute-start | bytes 2752520 | tf_op jit(solution)/shard_map/ppermute | solution.py:49
  130.7 22.0 %collective-permute-start.10 = (bf16[64,7168]{1,0:T(8,128)(2,1)S(1)}, bf16[64,7168]{1,0:T(8,128)(2,1)}, u32[]{:S(2)}, u32[]{:S(2)}) collective-permute-start(bf16[64,7168]{1,0:T(8,128)(2,1)S(1)} %fold.4.refs_5_.a_ref), channel_id=1, source_target_pairs={{0,2},{2,0},{1,3},{3,1},{4,6},{6,4},{5,7},{7,5},{8,10},{10,8},{9,1... | collective-permute-start | bytes 2752520 | tf_op jit(solution)/shard_map/ppermute | solution.py:49
  136.5 46.4 %collective-permute-start.9 = (bf16[64,7168]{1,0:T(8,128)(2,1)S(1)}, bf16[64,7168]{1,0:T(8,128)(2,1)}, u32[]{:S(2)}, u32[]{:S(2)}) collective-permute-start(bf16[64,7168]{1,0:T(8,128)(2,1)S(1)} %fold.5.rest_0_.a_ref), channel_id=1, source_target_pairs={{0,2},{2,0},{1,3},{3,1},{4,6},{6,4},{5,7},{7,5},{8,10},{10,8},{9,1... | collective-permute-start | bytes 2752520 | tf_op jit(solution)/shard_map/ppermute | solution.py:49
  145.2 28.4 %collective-permute-start.7 = (bf16[2,32,512]{2,1,0:T(8,128)(2,1)S(1)}, bf16[2,32,512]{2,1,0:T(8,128)(2,1)S(1)}, u32[]{:S(2)}, u32[]{:S(2)}) collective-permute-start(bf16[2,32,512]{2,1,0:T(8,128)(2,1)S(1)} %dynamic-slice_bitcast_fusion), channel_id=1, source_target_pairs={{0,2},{2,0},{1,3},{3,1},{4,6},{6,4},{5,7},{7,5},{8,10},{10,8},{9,1... | collective-permute-start | bytes 196616 | tf_op jit(solution)/shard_map/ppermute | solution.py:49
  145.5 7.2 %copy-start.22 = (s32[7168]{0:T(1024)S(1)}, s32[7168]{0:T(1024)}, u32[]{:S(2)}) copy-start(s32[7168]{0:T(1024)} %param.7) | copy-start | bytes 86020
  173.7 8.6 %collective-permute-start.8 = (bf16[32,512]{1,0:T(8,128)(2,1)S(1)}, bf16[32,512]{1,0:T(8,128)(2,1)S(1)}, u32[]{:S(2)}, u32[]{:S(2)}) collective-permute-start(bf16[32,512]{1,0:T(8,128)(2,1)S(1)} %fusion.3), channel_id=1, source_target_pairs={{0,1},{1,0},{2,3},{3,2},{4,5},{5,4},{6,7},{7,6},{8,9},{9,8},{10,11... | collective-permute-start | bytes 98312 | tf_op jit(solution)/shard_map/ppermute | solution.py:49
  179.3 7.1 %collective-permute-start.22 = (bf16[112,512]{1,0:T(8,128)(2,1)S(1)}, bf16[112,512]{1,0:T(8,128)(2,1)S(1)}, u32[]{:S(2)}, u32[]{:S(2)}) collective-permute-start(bf16[112,512]{1,0:T(8,128)(2,1)S(1)} %fusion.1), channel_id=1, source_target_pairs={{0,128},{128,0},{1,129},{129,1},{2,130},{130,2},{3,131},{131,3},{4... | collective-permute-start | bytes 344072 | tf_op jit(solution)/shard_map/ppermute | solution.py:49
  (22 other events, 48.2 us)

commit v3 on v0

v3 whole, which is shorter than its diff:
```python
import functools
import math

import jax
import jax.numpy as jnp
import numpy as np
from jax import lax
from jax.experimental import pallas as pl
from jax.experimental.pallas import tpu as pltpu
from jax.sharding import Mesh
from jax.sharding import PartitionSpec as P

AXES = ("yh", "z", "x", "yl", "core")
BLOCK = 896
LANES = 128
VM = pl.BlockSpec(memory_space=pltpu.VMEM)
SM = pl.BlockSpec(memory_space=pltpu.SMEM)
ANY = pl.BlockSpec(memory_space=pl.ANY)


def paley_table():
    squares_set = set((factor * factor % 13 for factor in range(1, 13)))
    core_matrix = np.zeros((14, 14))
    core_matrix[0, 1:] = 1.0
    core_matrix[1:, 0] = 1.0
    for row_idx in range(13):
        for col_idx in range(13):
            offset = (col_idx - row_idx) % 13
            if offset != 0:
                core_matrix[row_idx + 1, col_idx + 1] = 1.0 if offset in squares_set else -1.0
    first_pat = np.array([[1.0, -1.0], [-1.0, -1.0]])
    second_pat = np.array([[1.0, 1.0], [1.0, -1.0]])
    return np.kron(core_matrix, first_pat) + np.kron(np.eye(14), second_pat)


def sylvester_table(order):
    result = np.ones((1, 1))
    base_pat = np.array([[1.0, 1.0], [1.0, -1.0]])
    while result.shape[0] < order:
        result = np.kron(base_pat, result)
    return result


def block_table():
    return np.kron(sylvester_table(BLOCK // 28), paley_table())


def swap(value, axis):
    return lax.ppermute(value, axis, [(0, 1), (1, 0)])


def xor(value, axes, by):
    size = math.prod(lax.axis_size(a) for a in axes)
    return lax.ppermute(value, axes, [(i, i ^ by) for i in range(size)])


def shift(value, axis, by):
    size = lax.axis_size(axis)
    return lax.ppermute(value, axis, [(i, (i + by) % size) for i in range(size)])


def params(mib):
    return pltpu.CompilerParams(vmem_limit_bytes=mib * 2**20)


def cost(flops, nbytes):
    return pl.CostEstimate(flops=flops, bytes_accessed=nbytes, transcendentals=0)


def butterfly(parts):
    parts = list(parts)
    step = 1
    while step < len(parts):
        for base in range(len(parts)):
            if base & step == 0:
                a, b = parts[base], parts[base + step]
                parts[base], parts[base + step] = a + b, a - b
        step *= 2
    return parts


def flip_kernel(idx_ref, m_ref, p_ref, sign_ref, *rest):
    mo_ref, po_ref = rest[-2:]
    sign = (2 * sign_ref[...] - 1).astype(jnp.float32)
    mo_ref[...] = (m_ref[...].astype(jnp.float32) * sign).astype(jnp.bfloat16)
    po_ref[...] = (p_ref[...].astype(jnp.float32) * sign).astype(jnp.bfloat16)


def flip(idx, hidden, sign_bits, rows, after=()):
    cols = hidden.shape[1]
    wide = 2 * BLOCK
    block = pl.BlockSpec((rows, wide), lambda j, idx: (0, j))
    return pl.pallas_call(
        flip_kernel,
        grid_spec=pltpu.PrefetchScalarGridSpec(
            num_scalar_prefetch=1,
            grid=(cols // wide,),
            in_specs=[
                pl.BlockSpec((rows, wide), lambda j, idx: (idx[0], j)),
                pl.BlockSpec((rows, wide), lambda j, idx: (idx[1], j)),
                pl.BlockSpec((1, wide), lambda j, idx: (0, j)),
            ]
            + [ANY] * len(after),
            out_specs=(block, block),
        ),
        out_shape=(pltpu.HBM((rows, cols), jnp.bfloat16),) * 2,
        compiler_params=params(16),
        cost_estimate=cost(2 * rows * cols, 8 * rows * cols),
        name="flip",
    )(idx, hidden, hidden, sign_bits, *after)


def finish_kernel(idx_ref, sgn_ref, a_ref, b_ref, c_ref, d_ref, sign_ref, out_ref):
    rows, cols = a_ref.shape
    for at in range(0, cols, BLOCK):
        here = pl.ds(at, BLOCK)
        sign = (2 * sign_ref[:, here] - 1).astype(jnp.float32)
        for i, (own, other) in enumerate(((a_ref, b_ref), (c_ref, d_ref))):
            total = sgn_ref[0] * own[:, here].astype(jnp.float32) + other[:, here].astype(jnp.float32)
            start = pl.multiple_of(idx_ref[i] * rows, rows)
            out_ref[pl.ds(start, rows), here] = (total * sign).astype(jnp.bfloat16)


def finish(idx, sgn, mine, part, sign_bits):
    rows, cols = mine[0].shape
    return pl.pallas_call(
        finish_kernel,
        out_shape=jax.ShapeDtypeStruct((2 * rows, cols), jnp.bfloat16),
        in_specs=[SM, SM] + [VM] * 5,
        out_specs=VM,
        compiler_params=params(16),
        cost_estimate=cost(4 * rows * cols, 12 * rows * cols),
        name="finish",
    )(idx, sgn, *mine, *part, sign_bits)


def back_kernel(m_ref, p_ref, w_ref, *rest):
    mo_ref, po_ref = rest[-2:]
    rows = m_ref.shape[0]
    grads = jnp.concatenate([m_ref[...], p_ref[...]], axis=0)
    grad = lax.dot_general(grads, w_ref[...], (((1,), (1,)), ((), ())), preferred_element_type=jnp.float32)
    grad = grad.astype(jnp.bfloat16)
    mo_ref[...] = grad[:rows]
    po_ref[...] = grad[rows:]


def back(mine, part, weight, after=()):
    rows, wide = mine.shape
    cols = weight.shape[0]
    whole = pl.BlockSpec((rows, wide), lambda j: (0, 0))
    block = pl.BlockSpec((rows, BLOCK), lambda j: (0, j))
    return pl.pallas_call(
        back_kernel,
        grid=(cols // BLOCK,),
        out_shape=(pltpu.HBM((rows, cols), jnp.bfloat16),) * 2,
        in_specs=[whole, whole, pl.BlockSpec((BLOCK, wide), lambda j: (j, 0))] + [ANY] * len(after),
        out_specs=(block, block),
        compiler_params=params(24),
        cost_estimate=cost(4 * rows * cols * wide, 2 * cols * wide + 4 * rows * cols),
        name="back",
    )(mine, part, weight, *after)


def project_kernel(n, *refs):
    w_ref, out_ref, acc_ref = refs[n], refs[-2], refs[-1]
    j = pl.program_id(0)
    quant = jnp.concatenate([r[...] for r in refs[:n]], axis=0)
    part = jnp.dot(quant, w_ref[...], preferred_element_type=jnp.float32)

    @pl.when(j == 0)
    def _():
        acc_ref[...] = part

    @pl.when(j > 0)
    def _():
        acc_ref[...] += part

    @pl.when(j == pl.num_programs(0) - 1)
    def _():
        out_ref[...] = acc_ref[...].astype(out_ref.dtype)


def project(quants, weight, after=()):
    rows, cols = quants[0].shape
    n, wide = len(quants), weight.shape[1]
    block = pl.BlockSpec((rows, BLOCK), lambda j: (0, j))
    return pl.pallas_call(
        functools.partial(project_kernel, n),
        grid=(cols // BLOCK,),
        out_shape=jax.ShapeDtypeStruct((n * rows, wide), jnp.bfloat16),
        in_specs=[block] * n + [pl.BlockSpec((BLOCK, wide), lambda j: (j, 0))] + [ANY] * len(after),
        out_specs=pl.BlockSpec((n * rows, wide), lambda j: (0, 0)),
        scratch_shapes=[pltpu.VMEM((n * rows, wide), jnp.float32)],
        compiler_params=params(24),
        cost_estimate=cost(2 * n * rows * cols * wide, 2 * cols * wide),
        name="project",
    )(*quants, weight, *after)


SUB = 32


def turn_kernel(nblk, norm, sgn_ref, core_ref, own_ref, near_ref, far_ref, diag_ref, table_ref, *refs):
    bounds, (gq_here_ref, gq_there_ref) = refs[:2], refs[2:4]
    q_here_ref, q_there_ref, qt_ref, u_ref, w_ref, spun_ref = refs[-6:]
    rows = own_ref.shape[0]
    so_core, so_y = sgn_ref[0], sgn_ref[1]
    core = core_ref[0]
    span = nblk * rows
    per = BLOCK // LANES
    slabs = LANES // rows
    each = nblk // slabs
    n_dest, dest_rows = qt_ref.shape[0] // 2, qt_ref.shape[1]
    for j in range(nblk):
        cols = pl.ds(j * BLOCK, BLOCK)
        own, near, far, diag = (r[:, cols].astype(jnp.float32) for r in (own_ref, near_ref, far_ref, diag_ref))
        here = so_y * (so_core * own + near) + (so_core * far + diag)
        there = so_y * (own - so_core * near) + (far - so_core * diag)
        w_ref[pl.ds(j * rows, rows), :] = here.astype(jnp.bfloat16)
        w_ref[pl.ds(span + j * rows, rows), :] = there.astype(jnp.bfloat16)
    spun_ref[...] = jnp.dot(w_ref[...], table_ref[...], preferred_element_type=jnp.float32)

    def side(which, sub, lane, q_ref):
        toks = pl.ds(sub * SUB, SUB)
        lcols = pl.ds(lane * LANES, LANES)
        parts = butterfly([spun_ref[pl.ds(which * span + j * rows + sub * SUB, SUB), lcols] for j in range(nblk)])
        grads = []
        for j in range(nblk):
            bound = bounds[which][toks, j * per + lane : j * per + lane + 1]
            ratio = jnp.tanh(parts[j] * (norm / bound))
            cols = pl.ds(j * BLOCK + lane * LANES, LANES)
            q_ref[toks, cols] = (bound * ratio).astype(jnp.bfloat16)
            if which == 0:
                grad = gq_here_ref[toks, cols]
            else:
                grad = gq_there_ref[toks, cols]
            grads.append(grad.astype(jnp.float32) * (1.0 - ratio * ratio))
        return grads

    def transpose(lane, q_ref, slot):
        for part in range(each):
            cols = [pl.ds((slab * each + part) * BLOCK + lane * LANES, LANES) for slab in range(slabs)]
            both = jnp.concatenate([q_ref[:, c].astype(jnp.float32) for c in cols], axis=0)
            both = both.T.astype(jnp.bfloat16)
            start, done = (part * per + lane) * LANES, 0
            while done < LANES:
                dest, off = divmod(start + done, dest_rows)
                n = min(LANES - done, dest_rows - off)
                qt_ref[slot * n_dest + dest, off : off + n, :] = both[done : done + n]
                done += n

    for lane in range(per):
        lcols = pl.ds(lane * LANES, LANES)
        for sub in range(rows // SUB):
            here = side(0, sub, lane, q_here_ref)
            there = side(1, sub, lane, q_there_ref)
            for j in range(nblk):
                at = j * rows + sub * SUB
                u_ref[pl.ds(at, SUB), lcols] = (so_core * here[j] + there[j]).astype(jnp.bfloat16)
                u_ref[pl.ds(span + at, SUB), lcols] = (here[j] - so_core * there[j]).astype(jnp.bfloat16)
        transpose(lane, q_here_ref, core)
        transpose(lane, q_there_ref, 1 - core)


def turn(sgn, core, ins, table, bounds, gqs, norm, n_dest):
    rows, cols = ins[0].shape
    nblk = cols // BLOCK
    deep = 2 * nblk * rows
    flat = pltpu.HBM((rows, cols), jnp.bfloat16)
    qt = pltpu.HBM((n_dest, 2 * cols * rows // LANES // n_dest, LANES), jnp.bfloat16)
    return pl.pallas_call(
        functools.partial(turn_kernel, nblk, norm),
        out_shape=(flat, flat, qt, pltpu.HBM((deep, BLOCK), jnp.bfloat16)),
        in_specs=[SM, SM] + [VM] * 9,
        out_specs=(VM,) * 4,
        scratch_shapes=[pltpu.VMEM((deep, BLOCK), jnp.bfloat16), pltpu.VMEM((deep, BLOCK), jnp.float32)],
        compiler_params=params(32),
        cost_estimate=cost(2 * deep * BLOCK * BLOCK, 2 * rows * cols * 10),
        name="turn",
    )(sgn, core, *ins, table, *bounds, *gqs)


def return_kernel(nblk, norm, u_ref, table_ref, here_ref, there_ref, spun_ref):
    rows = here_ref.shape[0]
    span = nblk * rows
    spun_ref[...] = jnp.dot(u_ref[...], table_ref[...], preferred_element_type=jnp.float32)
    for which, v_ref in enumerate((here_ref, there_ref)):
        for sub in range(rows // SUB):
            for lane in range(BLOCK // LANES):
                lcols = pl.ds(lane * LANES, LANES)
                parts = butterfly(
                    [spun_ref[pl.ds(which * span + j * rows + sub * SUB, SUB), lcols] for j in range(nblk)]
                )
                for j in range(nblk):
                    cols = pl.ds(j * BLOCK + lane * LANES, LANES)
                    v_ref[pl.ds(sub * SUB, SUB), cols] = (parts[j] * norm).astype(jnp.bfloat16)


def turn_back(grads, table, rows, cols, norm):
    deep = grads.shape[0]
    flat = pltpu.HBM((rows, cols), jnp.bfloat16)
    return pl.pallas_call(
        functools.partial(return_kernel, cols // BLOCK, norm),
        out_shape=(flat, flat),
        in_specs=[VM, VM],
        out_specs=(VM, VM),
        scratch_shapes=[pltpu.VMEM((deep, BLOCK), jnp.float32)],
        compiler_params=params(24),
        cost_estimate=cost(2 * deep * BLOCK * BLOCK, 4 * rows * cols * 2),
        name="turn_back",
    )(grads, table)


def weight_grad_kernel(rows, toks, at_ref, r_ref, *refs):
    grad_refs, (out_ref, lhs_ref, rhs_ref) = refs[:-3], refs[-3:]
    slabs = LANES // toks
    slab = lax.broadcasted_iota(jnp.int32, (rows, LANES), 1) // toks
    blocks = [(ref, at) for ref in grad_refs for at in range(0, ref.shape[0], toks)]
    for place, (ref, start) in enumerate(blocks):
        value = r_ref[at_ref[place]]
        zero = jnp.zeros_like(value)
        at = place * LANES
        grads = ref[pl.ds(start, toks), :]
        for i in range(slabs):
            lhs_ref[i * rows : (i + 1) * rows, pl.ds(at, LANES)] = jnp.where(slab == i, value, zero)
            rhs_ref[pl.ds(at + i * toks, toks), :] = grads
    out_ref[...] = jnp.dot(lhs_ref[...], rhs_ref[...], preferred_element_type=jnp.float32)


def weight_grad(places, received, grads, toks):
    nsrc, rows, _ = received.shape
    wide = grads[0].shape[1]
    slabs = LANES // toks
    return pl.pallas_call(
        functools.partial(weight_grad_kernel, rows, toks),
        out_shape=jax.ShapeDtypeStruct((slabs * rows, wide), jnp.float32),
        in_specs=[SM] + [VM] * (1 + len(grads)),
        out_specs=VM,
        scratch_shapes=[
            pltpu.VMEM((slabs * rows, nsrc * LANES), jnp.bfloat16),
            pltpu.VMEM((nsrc * LANES, wide), jnp.bfloat16),
        ],
        compiler_params=params(40),
        cost_estimate=cost(2 * slabs * rows * nsrc * LANES * wide, 2 * nsrc * LANES * (rows + wide)),
        name="weight_grad",
    )(places, received, *grads)


def gather_z(value, *gates):
    two = after(jnp.concatenate([value, xor(value, ("z",), 4)], axis=0), *gates)
    return jnp.concatenate([two] + [xor(two, ("z",), d) for d in (1, 2, 3)], axis=0)


def gather_x(line):
    half = line.shape[0] // 2
    below, above = shift(line, "x", 1), shift(line, "x", -1)
    return [line, below, above, shift(below[:half], "x", 1), shift(above[half:], "x", -1)]


def source_places():
    nz, nx = lax.axis_size("z"), lax.axis_size("x")
    core = (lax.axis_index("core") ^ jnp.arange(2))[:, None, None]
    z = (lax.axis_index("z") ^ jnp.asarray([0, 4, 1, 5, 2, 6, 3, 7]))[None, None, :]
    x = ((lax.axis_index("x") - jnp.asarray([0, 1, -1, -2])) & (nx - 1))[None, :, None]
    return ((core * nz + z) * nx + x).reshape(-1).astype(jnp.int32)


def after(value, *others):
    return lax.optimization_barrier((value,) + others)[0]


def local(hidden, sign_bits, exponents, down_weight, grad_out):
    tok_count, ff_local = hidden.shape
    d_out = grad_out.shape[1]
    n_tensor = lax.axis_size("yl") * lax.axis_size("core")
    n_data = math.prod(lax.axis_size(a) for a in ("yh", "z", "x"))
    norm = 1.0 / math.sqrt(ff_local * n_tensor)
    half, quarter = tok_count // 2, tok_count // 4
    table = jnp.asarray(block_table(), jnp.bfloat16)
    sign_bits = sign_bits.reshape(1, ff_local)
    core, yl, yh = (lax.axis_index(a) for a in ("core", "yl", "yh"))
    so_core = (1 - 2 * core).astype(jnp.float32)
    so_y = (1 - 2 * yl).astype(jnp.float32)
    sgn_y, sgn = so_y[None], jnp.stack([so_core, so_y])
    core_at = core[None].astype(jnp.int32)
    idx = jnp.stack([core, 1 - core]).astype(jnp.int32)

    def of_mine(value):
        return lax.dynamic_slice_in_dim(value, core * half, half, 0)

    def of_part(value):
        return lax.dynamic_slice_in_dim(value, (1 - core) * half, half, 0)

    def diagonal(value):
        return xor(value, ("yl", "core"), 3)

    own, part = flip(idx, hidden, sign_bits, half)
    far, diag, near = swap(own, "yl"), diagonal(part), swap(part, "core")

    go_mine, go_part = of_mine(grad_out), of_part(grad_out)
    line = gather_z(after(go_mine, own))
    gq_here, gq_give = back(go_mine, go_part, down_weight, after=(own,))
    gq_there = swap(gq_give, "core")
    bound = 448.0 * jnp.exp2(exponents.astype(jnp.float32))
    bounds = (of_mine(bound), swap(of_part(bound), "core"))
    pieces = gather_x(after(line, far, gq_here))

    q_here, q_there, qt, grads = turn(
        sgn, core_at, (own, near, far, diag), table, bounds, (gq_here, gq_there), norm, 64
    )
    got = lax.all_to_all(after(qt, *pieces), ("core", "z", "x"), 0, 0, tiled=True)
    v_here, v_there = turn_back(grads, table, half, ff_local, norm)
    cross, dcross, ncross = swap(v_here, "yl"), diagonal(v_there), swap(v_there, "core")
    out_all = project((q_here, swap(q_there, "core")), down_weight, after=(v_here,)).reshape(2, 2, quarter, d_out)
    keep = lax.dynamic_index_in_dim(out_all, yl ^ core, 0, keepdims=False)
    give = lax.dynamic_index_in_dim(out_all, 1 - (yl ^ core), 0, keepdims=False)
    summed = keep.astype(jnp.float32) + swap(give, "yl").astype(jnp.float32)
    keep = lax.dynamic_index_in_dim(summed, core, 0, keepdims=False)
    give = lax.dynamic_index_in_dim(summed, 1 - core, 0, keepdims=False).astype(jnp.bfloat16)
    output = (keep + swap(give, "core").astype(jnp.float32)).astype(jnp.bfloat16)

    grad_hidden = finish(idx, sgn_y, (v_here, cross), (ncross, dcross), sign_bits)

    grads_all = pieces + [swap(p, "core") for p in pieces]
    acc = weight_grad(source_places(), got, grads_all, half)
    acc = acc.reshape(2, -1, d_out)
    keep = lax.dynamic_index_in_dim(acc, yh, 0, keepdims=False)
    give = lax.dynamic_index_in_dim(acc, 1 - yh, 0, keepdims=False).astype(jnp.bfloat16)
    grad_weight = (keep + swap(give, "yh").astype(jnp.float32)) * (1.0 / math.sqrt(tok_count * n_data))
    return (output, grad_hidden, grad_weight)


def solution(mesh):
    fine = Mesh(mesh.devices.reshape(2, 8, 4, 2, 2), AXES)
    dp, tensor = ("yh", "z", "x"), ("yl", "core")
    return jax.shard_map(
        local,
        mesh=fine,
        in_specs=(P(dp, tensor), P(tensor), P(dp, tensor), P(tensor, None), P(dp, None)),
        out_specs=(P(dp + tensor, None), P(dp, tensor), P(tensor + dp, None)),
        check_vma=False,
    )
```

time: 537 us -> 145 us (0.27)
  the two profiles are of different devices: /device:TPU:0 before, /device:TPU:1 now
where the time goes in v3:
time: 145 us; the launch traced here: 144 us
  waiting for transfers between devices  45.9 us (32%)
  starting transfers between devices  41.8 us (29%)
  Pallas kernels  30.4 us (21%)
  local copies, waits for them, and re-layouts  22 us (15%)
  other arithmetic  3.4 us (2%)
    ppermute x6, waiting for transfers between devices, xor(): return lax.ppermute(value, axes, [(i, i ^ by) for i in range(size)])  23.2 us
    unnamed x44, local copies, waits for them, and re-layouts  19.8 us
    ppermute x15, starting transfers between devices, swap(): return lax.ppermute(value, axis, [(0, 1), (1, 0)])  15.9 us
    ppermute x4, waiting for transfers between devices, shift(): lax.ppermute(value, axis, [(i, (i + by) % size) for i in range(size)])  11.4 us
    ppermute x15, waiting for transfers between devices, swap(): return lax.ppermute(value, axis, [(0, 1), (1, 0)])  11.3 us
    ppermute x6, starting transfers between devices, xor(): return lax.ppermute(value, axes, [(i, i ^ by) for i in range(size)])  11.2 us
    all_to_all x1, starting transfers between devices, local(): lax.all_to_all(after(qt, *pieces), ('core', 'z', 'x'), 0, 0, tiled=True)  9 us
    pallas_call x1, Pallas kernels, turn(): pl.pallas_call(functools.partial(turn_kernel, nblk, norm), out_shape=(fla...  8.49 us
  transfers between devices with their start and end apart: 26, of which 6 were waited for; matrix products, arithmetic and copies ran while one was open for 3% of the time, Pallas kernels for 19%

profile of v3, /device:TPU:1, one launch (start us, length us, event | category | flops | bytes accessed | tf_op | source)
XLA Modules:
  0.0 144.3 jit_solution(931307847429192359)
XLA Ops:
  0.7 1.5 %copy-done.2 = bf16[128,7168]{1,0:T(8,128)(2,1)S(1)} copy-done((bf16[128,7168]{1,0:T(8,128)(2,1)S(1)}, bf16[128,7168]{1,0:T(8,128)(2,1)}, u32[]{:S(2)}) %copy-start.2) | copy-done | bytes 1835032
  3.0 2.5 %flip.1 = (bf16[64,7168]{1,0:T(8,128)(2,1)}, bf16[64,7168]{1,0:T(8,128)(2,1)}) custom-call(s32[2]{0:T(128)S(1)} %pad_add_fusion.idx_ref, bf16[128,7168]{1,0:T(8,128)(2,1)S(1)} %copy-done.2, bf16[128,7168]{1,0:T(8,128)(2,1)S(1)} %copy-done.2, s32[1,7168]{1,0:T(1,128)S(1)} %bitcast.28), custom_call_target="tpu_custom_call" | custom-call | flops 917504 | bytes 3670016 | tf_op jit(solution)/shard_map/flip/pallas_call | solution.py:93
  5.5 2.1 %collective-permute-start.1 = (bf16[64,7168]{1,0:T(8,128)(2,1)}, bf16[64,7168]{1,0:T(8,128)(2,1)S(1)}, u32[]{:S(2)}, u32[]{:S(2)}) collective-permute-start(bf16[64,7168]{1,0:T(8,128)(2,1)} %get-tuple-element.16.rest_0_.own_ref), channel_id=1, source_target_pairs={{0,2},{2,0},{1,3},{3,1},{4,6},{6,4},{5,7},{7,5},{8,10},{10,8},{9,1... | collective-permute-start | bytes 2752520 | tf_op jit(solution)/shard_map/ppermute | solution.py:49
  7.6 7.0 %collective-permute-start.11 = (bf16[64,512]{1,0:T(8,128)(2,1)S(1)}, bf16[64,512]{1,0:T(8,128)(2,1)S(1)}, u32[]{:S(2)}, u32[]{:S(2)}) collective-permute-start(bf16[64,512]{1,0:T(8,128)(2,1)S(1)} %get-tuple-element.26.m_ref), channel_id=1, source_target_pairs={{0,64},{16,80},{32,96},{48,112},{64,0},{80,16},{96,32},{112,48},{1... | collective-permute-start | bytes 196616 | tf_op jit(solution)/shard_map/ppermute | solution.py:54
  14.6 1.7 %collective-permute-done.11 = bf16[64,512]{1,0:T(8,128)(2,1)S(1)} collective-permute-done((bf16[64,512]{1,0:T(8,128)(2,1)S(1)}, bf16[64,512]{1,0:T(8,128)(2,1)S(1)}, u32[]{:S(2)}, u32[]{:S(2)}) %collective-permute-start.11) | collective-permute-done | bytes 65568 | tf_op jit(solution)/shard_map/ppermute | solution.py:54
  16.4 2.8 %collective-permute-start.14 = (bf16[128,512]{1,0:T(8,128)(2,1)S(1)}, bf16[128,512]{1,0:T(8,128)(2,1)S(1)}, u32[]{:S(2)}, u32[]{:S(2)}) collective-permute-start(bf16[128,512]{1,0:T(8,128)(2,1)S(1)} %pad_maximum_fusion.1), channel_id=1, source_target_pairs={{0,48},{16,32},{32,16},{48,0},{64,112},{80,96},{96,80},{112,64},{1... | collective-permute-start | bytes 393224 | tf_op jit(solution)/shard_map/ppermute | solution.py:54
  19.2 2.4 %collective-permute-start = (bf16[64,7168]{1,0:T(8,128)(2,1)}, bf16[64,7168]{1,0:T(8,128)(2,1)}, u32[]{:S(2)}, u32[]{:S(2)}) collective-permute-start(bf16[64,7168]{1,0:T(8,128)(2,1)} %get-tuple-element.17), channel_id=1, source_target_pairs={{0,1},{1,0},{2,3},{3,2},{4,5},{5,4},{6,7},{7,6},{8,9},{9,8},{10,11... | collective-permute-start | bytes 2752520 | tf_op jit(solution)/shard_map/ppermute | solution.py:49
  21.7 3.1 %copy-done = bf16[7168,512]{1,0:T(8,128)(2,1)S(1)} copy-done((bf16[7168,512]{1,0:T(8,128)(2,1)S(1)}, bf16[7168,512]{1,0:T(8,128)(2,1)}, u32[]{:S(2)}) %copy-start) | copy-done | bytes 7340056
  26.0 5.1 %back.1 = (bf16[64,7168]{1,0:T(8,128)(2,1)}, bf16[64,7168]{1,0:T(8,128)(2,1)}) custom-call(bf16[64,512]{1,0:T(8,128)(2,1)S(1)} %get-tuple-element.26.m_ref, bf16[64,512]{1,0:T(8,128)(2,1)S(1)} %get-tuple-element.29.p_ref, bf16[7168,512]{1,0:T(8,128)(2,1)S(1)} %copy-done, bf16[64,7168]{1,0:T(8,128)(2,1)S(1)} %copy-done.5), custom_call_target="tpu_custom_call" | custom-call | flops 939524096 | bytes 9175040 | tf_op jit(solution)/shard_map/back/pallas_call | solution.py:152
  31.7 1.2 collective-permute-start.12
  32.9 4.0 %collective-permute-done.12 = bf16[128,512]{1,0:T(8,128)(2,1)S(1)} collective-permute-done((bf16[128,512]{1,0:T(8,128)(2,1)S(1)}, bf16[128,512]{1,0:T(8,128)(2,1)S(1)}, u32[]{:S(2)}, u32[]{:S(2)}) %collective-permute-start.12) | collective-permute-done | bytes 131104 | tf_op jit(solution)/shard_map/ppermute | solution.py:54
  37.7 1.2 collective-permute-start.15
  38.9 1.5 %collective-permute-start.16 = (bf16[512,512]{1,0:T(8,128)(2,1)}, bf16[512,512]{1,0:T(8,128)(2,1)}, u32[]{:S(2)}, u32[]{:S(2)}) collective-permute-start(bf16[512,512]{1,0:T(8,128)(2,1)} %pad_maximum_fusion.refs_0_), channel_id=1, source_target_pairs={{0,12},{4,0},{8,4},{12,8},{1,13},{5,1},{9,5},{13,9},{2,14},{6,2},{... | collective-permute-start | bytes 1572872 | tf_op jit(solution)/shard_map/ppermute | solution.py:59
  40.6 11.4 %collective-permute-done.15.refs_1_ = bf16[512,512]{1,0:T(8,128)(2,1)} collective-permute-done((bf16[512,512]{1,0:T(8,128)(2,1)}, bf16[512,512]{1,0:T(8,128)(2,1)}, u32[]{:S(2)}, u32[]{:S(2)}) %collective-permute-start.15) | collective-permute-done | bytes 524320 | tf_op jit(solution)/shard_map/ppermute | solution.py:59
  51.9 1.7 %collective-permute-start.3 = (f32[64,56]{1,0:T(8,128)S(1)}, f32[64,56]{1,0:T(8,128)S(1)}, u32[]{:S(2)}, u32[]{:S(2)}) collective-permute-start(f32[64,56]{1,0:T(8,128)S(1)} %get-tuple-element.31), channel_id=1, source_target_pairs={{0,1},{1,0},{2,3},{3,2},{4,5},{5,4},{6,7},{7,6},{8,9},{9,8},{10,11... | collective-permute-start | bytes 43016 | tf_op jit(solution)/shard_map/ppermute | solution.py:49
  55.7 2.9 %collective-permute-start.18 = (bf16[256,512]{1,0:T(8,128)(2,1)S(1)}, bf16[256,512]{1,0:T(8,128)(2,1)}, u32[]{:S(2)}, u32[]{:S(2)}) collective-permute-start(bf16[256,512]{1,0:T(8,128)(2,1)S(1)} %slice.9), channel_id=1, source_target_pairs={{0,12},{4,0},{8,4},{12,8},{1,13},{5,1},{9,5},{13,9},{2,14},{6,2},{... | collective-permute-start | bytes 786440 | tf_op jit(solution)/shard_map/ppermute | solution.py:59
  59.9 8.5 %turn.1 = (bf16[64,7168]{1,0:T(8,128)(2,1)}, bf16[64,7168]{1,0:T(8,128)(2,1)}, bf16[64,112,128]{2,1,0:T(8,128)(2,1)}, bf16[1024,896]{1,0:T(8,128)(2,1)}) custom-call(f32[2]{0:T(128)S(1)} %pad_maximum_fusion.2.sgn_ref, s32[1]{0:T(128)} %bitcast.2.core_ref, bf16[64,7168]{1,0:T(8,128)(2,1)S(1)} %copy-done.6, bf16[64,7168]{1,0:T(8,128)(2,1)} %collective-permute-done.near_ref, ...), custom_call_target="tpu_custom_call" | custom-call | flops 1644167168 | bytes 9175040 | tf_op jit(solution)/shard_map/turn/pallas_call | solution.py:271
  68.4 9.0 %all-to-all-start = ((bf16[64,112,128]{2,1,0:T(8,128)(2,1)}), bf16[64,112,128]{2,1,0:T(8,128)(2,1)S(1)}, u32[]{:S(2)}, u32[]{:S(2)}) async-start(bf16[64,112,128]{2,1,0:T(8,128)(2,1)} %get-tuple-element.28), calls=%async_computation | async-start | bytes 3670016 | tf_op jit(solution)/shard_map/all_to_all | solution.py:411
  77.8 1.4 copy-done.8
  79.2 1.5 %copy-done.15 = bf16[1024,896]{1,0:T(8,128)(2,1)S(1)} copy-done((bf16[1024,896]{1,0:T(8,128)(2,1)S(1)}, bf16[1024,896]{1,0:T(8,128)(2,1)}, u32[]{:S(2)}) %copy-start.15) | copy-done | bytes 1835032
  80.7 3.6 %turn_back.1 = (bf16[64,7168]{1,0:T(8,128)(2,1)}, bf16[64,7168]{1,0:T(8,128)(2,1)}) custom-call(bf16[1024,896]{1,0:T(8,128)(2,1)S(1)} %copy-done.15, bf16[896,896]{1,0:T(8,128)(2,1)S(1)} %copy-done.8), custom_call_target="tpu_custom_call" | custom-call | flops 1644167168 | bytes 3670016 | tf_op jit(solution)/shard_map/turn_back/pallas_call | solution.py:302
  84.3 1.3 collective-permute-start.8
  87.8 3.1 %copy-done.1 = bf16[7168,512]{1,0:T(8,128)(2,1)S(1)} copy-done((bf16[7168,512]{1,0:T(8,128)(2,1)S(1)}, bf16[7168,512]{1,0:T(8,128)(2,1)}, u32[]{:S(2)}) %copy-start.1) | copy-done | bytes 7340056
  94.4 3.0 %project.1 = bf16[128,512]{1,0:T(8,128)(2,1)S(1)} custom-call(bf16[64,7168]{1,0:T(8,128)(2,1)S(1)} %copy-done.9, bf16[64,7168]{1,0:T(8,128)(2,1)S(1)} %copy-done.11, bf16[7168,512]{1,0:T(8,128)(2,1)S(1)} %copy-done.1, bf16[64,7168]{1,0:T(8,128)(2,1)S(1)} %copy-done.3), custom_call_target="tpu_custom_call" | custom-call | flops 939524096 | bytes 7340032 | tf_op jit(solution)/shard_map/project/pallas_call | solution.py:187
  97.4 9.0 %collective-permute-done.8.b_ref = bf16[64,7168]{1,0:T(8,128)(2,1)} collective-permute-done((bf16[64,7168]{1,0:T(8,128)(2,1)}, bf16[64,7168]{1,0:T(8,128)(2,1)}, u32[]{:S(2)}, u32[]{:S(2)}) %collective-permute-start.8) | collective-permute-done | bytes 917536 | tf_op jit(solution)/shard_map/ppermute | solution.py:49
  106.5 1.5 %collective-permute-start.21 = (bf16[512,512]{1,0:T(8,128)(2,1)}, bf16[512,512]{1,0:T(8,128)(2,1)}, u32[]{:S(2)}, u32[]{:S(2)}) collective-permute-start(bf16[512,512]{1,0:T(8,128)(2,1)} %collective-permute-done.16.refs_2_), channel_id=1, source_target_pairs={{0,1},{1,0},{2,3},{3,2},{4,5},{5,4},{6,7},{7,6},{8,9},{9,8},{10,11... | collective-permute-start | bytes 1572872 | tf_op jit(solution)/shard_map/ppermute | solution.py:49
  108.0 1.3 collective-permute-start.6
  109.4 17.5 %collective-permute-done.10.d_ref = bf16[64,7168]{1,0:T(8,128)(2,1)} collective-permute-done((bf16[64,7168]{1,0:T(8,128)(2,1)}, bf16[64,7168]{1,0:T(8,128)(2,1)}, u32[]{:S(2)}, u32[]{:S(2)}) %collective-permute-start.10) | collective-permute-done | bytes 917536 | tf_op jit(solution)/shard_map/ppermute | solution.py:54
  127.0 3.7 %finish.1 = bf16[128,7168]{1,0:T(8,128)(2,1)} custom-call(s32[2]{0:T(128)S(1)} %pad_add_fusion.idx_ref, f32[1]{0:T(128)} %bitcast.1.sgn_ref, bf16[64,7168]{1,0:T(8,128)(2,1)S(1)} %copy-done.4, bf16[64,7168]{1,0:T(8,128)(2,1)} %collective-permute-done.8.b_ref, bf16[64,7168]{1,0:T(8,128)(2,1)} %collective-permute-done.9.c_ref, ...), custom_call_target="tpu_custom_call" | custom-call | flops 1835008 | bytes 5505024 | tf_op jit(solution)/shard_map/finish/pallas_call | solution.py:126
  133.8 3.9 %weight_grad.1 = f32[224,512]{1,0:T(8,128)S(1)} custom-call(s32[64]{0:T(128)S(1)} %add.90.at_ref, bf16[64,112,128]{2,1,0:T(8,128)(2,1)S(1)} %all-to-all-done.r_ref, bf16[512,512]{1,0:T(8,128)(2,1)} %pad_maximum_fusion.refs_0_, bf16[512,512]{1,0:T(8,128)(2,1)} %collective-permute-done.15.refs_1_, bf16[512,512]{1,0:T(8,128)(2,1)} %collective-permute-done.16.refs_2_, ...), custom_call_target="tpu_custom_call" | custom-call | flops 1879048192 | bytes 10223616 | tf_op jit(solution)/shard_map/weight_grad/pallas_call | solution.py:334
  137.8 3.0 %collective-permute-start.24 = (bf16[112,512]{1,0:T(8,128)(2,1)S(1)}, bf16[112,512]{1,0:T(8,128)(2,1)S(1)}, u32[]{:S(2)}, u32[]{:S(2)}) collective-permute-start(bf16[112,512]{1,0:T(8,128)(2,1)S(1)} %fusion.1), channel_id=1, source_target_pairs={{0,128},{128,0},{1,129},{129,1},{2,130},{130,2},{3,131},{131,3},{4... | collective-permute-start | bytes 344072 | tf_op jit(solution)/shard_map/ppermute | solution.py:49
  141.4 2.2 %collective-permute-done.24 = bf16[112,512]{1,0:T(8,128)(2,1)S(1)} collective-permute-done((bf16[112,512]{1,0:T(8,128)(2,1)S(1)}, bf16[112,512]{1,0:T(8,128)(2,1)S(1)}, u32[]{:S(2)}, u32[]{:S(2)}) %collective-permute-start.24) | collective-permute-done | bytes 114720 | tf_op jit(solution)/shard_map/ppermute | solution.py:49
  (94 shorter events, 17.8 us)
Async XLA Ops:
  5.5 32.2 %collective-permute-start.1 = (bf16[64,7168]{1,0:T(8,128)(2,1)}, bf16[64,7168]{1,0:T(8,128)(2,1)S(1)}, u32[]{:S(2)}, u32[]{:S(2)}) collective-permute-start(bf16[64,7168]{1,0:T(8,128)(2,1)} %get-tuple-element.16.rest_0_.own_ref), channel_id=1, source_target_pairs={{0,2},{2,0},{1,3},{3,1},{4,6},{6,4},{5,7},{7,5},{8,10},{10,8},{9,1... | collective-permute-start | bytes 2752520 | tf_op jit(solution)/shard_map/ppermute | solution.py:49
  7.6 8.7 %collective-permute-start.11 = (bf16[64,512]{1,0:T(8,128)(2,1)S(1)}, bf16[64,512]{1,0:T(8,128)(2,1)S(1)}, u32[]{:S(2)}, u32[]{:S(2)}) collective-permute-start(bf16[64,512]{1,0:T(8,128)(2,1)S(1)} %get-tuple-element.26.m_ref), channel_id=1, source_target_pairs={{0,64},{16,80},{32,96},{48,112},{64,0},{80,16},{96,32},{112,48},{1... | collective-permute-start | bytes 196616 | tf_op jit(solution)/shard_map/ppermute | solution.py:54
  16.4 14.7 %collective-permute-start.14 = (bf16[128,512]{1,0:T(8,128)(2,1)S(1)}, bf16[128,512]{1,0:T(8,128)(2,1)S(1)}, u32[]{:S(2)}, u32[]{:S(2)}) collective-permute-start(bf16[128,512]{1,0:T(8,128)(2,1)S(1)} %pad_maximum_fusion.1), channel_id=1, source_target_pairs={{0,48},{16,32},{32,16},{48,0},{64,112},{80,96},{96,80},{112,64},{1... | collective-permute-start | bytes 393224 | tf_op jit(solution)/shard_map/ppermute | solution.py:54
  19.2 12.5 %collective-permute-start.13 = (bf16[128,512]{1,0:T(8,128)(2,1)S(1)}, bf16[128,512]{1,0:T(8,128)(2,1)S(1)}, u32[]{:S(2)}, u32[]{:S(2)}) collective-permute-start(bf16[128,512]{1,0:T(8,128)(2,1)S(1)} %pad_maximum_fusion.1), channel_id=1, source_target_pairs={{0,32},{16,48},{32,0},{48,16},{64,96},{80,112},{96,64},{112,80},{1... | collective-permute-start | bytes 393224 | tf_op jit(solution)/shard_map/ppermute | solution.py:54
  19.2 39.4 %collective-permute-start = (bf16[64,7168]{1,0:T(8,128)(2,1)}, bf16[64,7168]{1,0:T(8,128)(2,1)}, u32[]{:S(2)}, u32[]{:S(2)}) collective-permute-start(bf16[64,7168]{1,0:T(8,128)(2,1)} %get-tuple-element.17), channel_id=1, source_target_pairs={{0,1},{1,0},{2,3},{3,2},{4,5},{5,4},{6,7},{7,6},{8,9},{9,8},{10,11... | collective-permute-start | bytes 2752520 | tf_op jit(solution)/shard_map/ppermute | solution.py:49
  21.6 37.0 %collective-permute-start.2 = (bf16[64,7168]{1,0:T(8,128)(2,1)}, bf16[64,7168]{1,0:T(8,128)(2,1)}, u32[]{:S(2)}, u32[]{:S(2)}) collective-permute-start(bf16[64,7168]{1,0:T(8,128)(2,1)} %get-tuple-element.17), channel_id=1, source_target_pairs={{0,3},{1,2},{2,1},{3,0},{4,7},{5,6},{6,5},{7,4},{8,11},{9,10},{10,... | collective-permute-start | bytes 2752520 | tf_op jit(solution)/shard_map/ppermute | solution.py:54
  25.9 14.5 %copy-start.19 = (s32[128,56]{0,1:T(8,128)S(1)}, s32[128,56]{0,1:T(8,128)}, u32[]{:S(2)}) copy-start(s32[128,56]{0,1:T(8,128)} %param.10) | copy-start | bytes 86020
  31.1 27.6 %copy-start.6 = (bf16[64,7168]{1,0:T(8,128)(2,1)S(1)}, bf16[64,7168]{1,0:T(8,128)(2,1)}, u32[]{:S(2)}) copy-start(bf16[64,7168]{1,0:T(8,128)(2,1)} %get-tuple-element.16.rest_0_.own_ref) | copy-start | bytes 2752516
  31.1 27.6 %copy-start.7 = (bf16[896,896]{1,0:T(8,128)(2,1)S(1)}, bf16[896,896]{1,0:T(8,128)(2,1)}, u32[]{:S(2)}) copy-start(bf16[896,896]{1,0:T(8,128)(2,1)} %constant.69.clone.table_ref) | copy-start | bytes 4816900
  31.1 27.6 %collective-permute-start.4 = (bf16[64,7168]{1,0:T(8,128)(2,1)}, bf16[64,7168]{1,0:T(8,128)(2,1)}, u32[]{:S(2)}, u32[]{:S(2)}) collective-permute-start(bf16[64,7168]{1,0:T(8,128)(2,1)} %get-tuple-element.19), channel_id=1, source_target_pairs={{0,1},{1,0},{2,3},{3,2},{4,5},{5,4},{6,7},{7,6},{8,9},{9,8},{10,11... | collective-permute-start | bytes 2752520 | tf_op jit(solution)/shard_map/ppermute | solution.py:49
  31.7 5.2 %collective-permute-start.12 = (bf16[128,512]{1,0:T(8,128)(2,1)S(1)}, bf16[128,512]{1,0:T(8,128)(2,1)S(1)}, u32[]{:S(2)}, u32[]{:S(2)}) collective-permute-start(bf16[128,512]{1,0:T(8,128)(2,1)S(1)} %pad_maximum_fusion.1), channel_id=1, source_target_pairs={{0,16},{16,0},{32,48},{48,32},{64,80},{80,64},{96,112},{112,96},{1... | collective-permute-start | bytes 393224 | tf_op jit(solution)/shard_map/ppermute | solution.py:54
  37.7 14.2 %collective-permute-start.15 = (bf16[512,512]{1,0:T(8,128)(2,1)}, bf16[512,512]{1,0:T(8,128)(2,1)}, u32[]{:S(2)}, u32[]{:S(2)}) collective-permute-start(bf16[512,512]{1,0:T(8,128)(2,1)} %pad_maximum_fusion.refs_0_), channel_id=1, source_target_pairs={{0,4},{4,8},{8,12},{12,0},{1,5},{5,9},{9,13},{13,1},{2,6},{6,10},{... | collective-permute-start | bytes 1572872 | tf_op jit(solution)/shard_map/ppermute | solution.py:59
  38.9 15.6 %collective-permute-start.16 = (bf16[512,512]{1,0:T(8,128)(2,1)}, bf16[512,512]{1,0:T(8,128)(2,1)}, u32[]{:S(2)}, u32[]{:S(2)}) collective-permute-start(bf16[512,512]{1,0:T(8,128)(2,1)} %pad_maximum_fusion.refs_0_), channel_id=1, source_target_pairs={{0,12},{4,0},{8,4},{12,8},{1,13},{5,1},{9,5},{13,9},{2,14},{6,2},{... | collective-permute-start | bytes 1572872 | tf_op jit(solution)/shard_map/ppermute | solution.py:59
  51.9 3.7 %collective-permute-start.3 = (f32[64,56]{1,0:T(8,128)S(1)}, f32[64,56]{1,0:T(8,128)S(1)}, u32[]{:S(2)}, u32[]{:S(2)}) collective-permute-start(f32[64,56]{1,0:T(8,128)S(1)} %get-tuple-element.31), channel_id=1, source_target_pairs={{0,1},{1,0},{2,3},{3,2},{4,5},{5,4},{6,7},{7,6},{8,9},{9,8},{10,11... | collective-permute-start | bytes 43016 | tf_op jit(solution)/shard_map/ppermute | solution.py:49
  54.6 13.8 %collective-permute-start.17 = (bf16[256,512]{1,0:T(8,128)(2,1)S(1)}, bf16[256,512]{1,0:T(8,128)(2,1)}, u32[]{:S(2)}, u32[]{:S(2)}) collective-permute-start(bf16[256,512]{1,0:T(8,128)(2,1)S(1)} %slice.8), channel_id=1, source_target_pairs={{0,4},{4,8},{8,12},{12,0},{1,5},{5,9},{9,13},{13,1},{2,6},{6,10},{... | collective-permute-start | bytes 786440 | tf_op jit(solution)/shard_map/ppermute | solution.py:59
  55.7 12.7 %collective-permute-start.18 = (bf16[256,512]{1,0:T(8,128)(2,1)S(1)}, bf16[256,512]{1,0:T(8,128)(2,1)}, u32[]{:S(2)}, u32[]{:S(2)}) collective-permute-start(bf16[256,512]{1,0:T(8,128)(2,1)S(1)} %slice.9), channel_id=1, source_target_pairs={{0,12},{4,0},{8,4},{12,8},{1,13},{5,1},{9,5},{13,9},{2,14},{6,2},{... | collective-permute-start | bytes 786440 | tf_op jit(solution)/shard_map/ppermute | solution.py:59
  68.4 64.5 %all-to-all-start = ((bf16[64,112,128]{2,1,0:T(8,128)(2,1)}), bf16[64,112,128]{2,1,0:T(8,128)(2,1)S(1)}, u32[]{:S(2)}, u32[]{:S(2)}) async-start(bf16[64,112,128]{2,1,0:T(8,128)(2,1)} %get-tuple-element.28), calls=%async_computation | async-start | bytes 3670016 | tf_op jit(solution)/shard_map/all_to_all | solution.py:411
  77.4 9.4 %collective-permute-start.5 = (bf16[64,7168]{1,0:T(8,128)(2,1)}, bf16[64,7168]{1,0:T(8,128)(2,1)S(1)}, u32[]{:S(2)}, u32[]{:S(2)}) collective-permute-start(bf16[64,7168]{1,0:T(8,128)(2,1)} %get-tuple-element.21), channel_id=1, source_target_pairs={{0,1},{1,0},{2,3},{3,2},{4,5},{5,4},{6,7},{7,6},{8,9},{9,8},{10,11... | collective-permute-start | bytes 2752520 | tf_op jit(solution)/shard_map/ppermute | solution.py:49
  80.7 5.5 %copy-start.20 = (s32[8]{0:T(128)S(1)}, s32[8]{0:T(128)}, u32[]{:S(2)}) copy-start(s32[8]{0:T(128)} %constant.70.clone) | copy-start | bytes 100
  84.3 22.1 %collective-permute-start.8 = (bf16[64,7168]{1,0:T(8,128)(2,1)}, bf16[64,7168]{1,0:T(8,128)(2,1)}, u32[]{:S(2)}, u32[]{:S(2)}) collective-permute-start(bf16[64,7168]{1,0:T(8,128)(2,1)} %get-tuple-element.23.refs_3_.a_ref), channel_id=1, source_target_pairs={{0,2},{2,0},{1,3},{3,1},{4,6},{6,4},{5,7},{7,5},{8,10},{10,8},{9,1... | collective-permute-start | bytes 2752520 | tf_op jit(solution)/shard_map/ppermute | solution.py:49
  85.6 22.3 %collective-permute-start.9 = (bf16[64,7168]{1,0:T(8,128)(2,1)}, bf16[64,7168]{1,0:T(8,128)(2,1)}, u32[]{:S(2)}, u32[]{:S(2)}) collective-permute-start(bf16[64,7168]{1,0:T(8,128)(2,1)} %get-tuple-element.24), channel_id=1, source_target_pairs={{0,1},{1,0},{2,3},{3,2},{4,5},{5,4},{6,7},{7,6},{8,9},{9,8},{10,11... | collective-permute-start | bytes 2752520 | tf_op jit(solution)/shard_map/ppermute | solution.py:49
  86.1 40.9 %collective-permute-start.10 = (bf16[64,7168]{1,0:T(8,128)(2,1)}, bf16[64,7168]{1,0:T(8,128)(2,1)}, u32[]{:S(2)}, u32[]{:S(2)}) collective-permute-start(bf16[64,7168]{1,0:T(8,128)(2,1)} %get-tuple-element.24), channel_id=1, source_target_pairs={{0,3},{1,2},{2,1},{3,0},{4,7},{5,6},{6,5},{7,4},{8,11},{9,10},{10,... | collective-permute-start | bytes 2752520 | tf_op jit(solution)/shard_map/ppermute | solution.py:54
  86.3 45.7 %collective-permute-start.19 = (bf16[512,512]{1,0:T(8,128)(2,1)}, bf16[512,512]{1,0:T(8,128)(2,1)S(1)}, u32[]{:S(2)}, u32[]{:S(2)}) collective-permute-start(bf16[512,512]{1,0:T(8,128)(2,1)} %pad_maximum_fusion.refs_0_), channel_id=1, source_target_pairs={{0,1},{1,0},{2,3},{3,2},{4,5},{5,4},{6,7},{7,6},{8,9},{9,8},{10,11... | collective-permute-start | bytes 1572872 | tf_op jit(solution)/shard_map/ppermute | solution.py:49
  87.7 45.2 %collective-permute-start.20 = (bf16[512,512]{1,0:T(8,128)(2,1)}, bf16[512,512]{1,0:T(8,128)(2,1)}, u32[]{:S(2)}, u32[]{:S(2)}) collective-permute-start(bf16[512,512]{1,0:T(8,128)(2,1)} %collective-permute-done.15.refs_1_), channel_id=1, source_target_pairs={{0,1},{1,0},{2,3},{3,2},{4,5},{5,4},{6,7},{7,6},{8,9},{9,8},{10,11... | collective-permute-start | bytes 1572872 | tf_op jit(solution)/shard_map/ppermute | solution.py:49
  94.4 32.6 %copy-start.4 = (bf16[64,7168]{1,0:T(8,128)(2,1)S(1)}, bf16[64,7168]{1,0:T(8,128)(2,1)}, u32[]{:S(2)}) copy-start(bf16[64,7168]{1,0:T(8,128)(2,1)} %get-tuple-element.23.refs_3_.a_ref) | copy-start | bytes 2752516
  94.4 32.6 %copy-start.14 = (s32[7168]{0:T(1024)S(1)}, s32[7168]{0:T(1024)}, u32[]{:S(2)}) copy-start(s32[7168]{0:T(1024)} %param.9) | copy-start | bytes 86020
  106.5 26.4 %collective-permute-start.21 = (bf16[512,512]{1,0:T(8,128)(2,1)}, bf16[512,512]{1,0:T(8,128)(2,1)}, u32[]{:S(2)}, u32[]{:S(2)}) collective-permute-start(bf16[512,512]{1,0:T(8,128)(2,1)} %collective-permute-done.16.refs_2_), channel_id=1, source_target_pairs={{0,1},{1,0},{2,3},{3,2},{4,5},{5,4},{6,7},{7,6},{8,9},{9,8},{10,11... | collective-permute-start | bytes 1572872 | tf_op jit(solution)/shard_map/ppermute | solution.py:49
  108.0 22.7 %collective-permute-start.6 = (bf16[2,32,512]{2,1,0:T(8,128)(2,1)S(1)}, bf16[2,32,512]{2,1,0:T(8,128)(2,1)}, u32[]{:S(2)}, u32[]{:S(2)}) collective-permute-start(bf16[2,32,512]{2,1,0:T(8,128)(2,1)S(1)} %dynamic-slice_bitcast_fusion), channel_id=1, source_target_pairs={{0,2},{2,0},{1,3},{3,1},{4,6},{6,4},{5,7},{7,5},{8,10},{10,8},{9,1... | collective-permute-start | bytes 196616 | tf_op jit(solution)/shard_map/ppermute | solution.py:49
  126.9 5.2 %collective-permute-start.22 = (bf16[256,512]{1,0:T(8,128)(2,1)}, bf16[256,512]{1,0:T(8,128)(2,1)S(1)}, u32[]{:S(2)}, u32[]{:S(2)}) collective-permute-start(bf16[256,512]{1,0:T(8,128)(2,1)} %collective-permute-done.17.refs_3_), channel_id=1, source_target_pairs={{0,1},{1,0},{2,3},{3,2},{4,5},{5,4},{6,7},{7,6},{8,9},{9,8},{10,11... | collective-permute-start | bytes 786440 | tf_op jit(solution)/shard_map/ppermute | solution.py:49
  130.7 2.2 %collective-permute-start.23 = (bf16[256,512]{1,0:T(8,128)(2,1)}, bf16[256,512]{1,0:T(8,128)(2,1)S(1)}, u32[]{:S(2)}, u32[]{:S(2)}) collective-permute-start(bf16[256,512]{1,0:T(8,128)(2,1)} %collective-permute-done.18.refs_4_), channel_id=1, source_target_pairs={{0,1},{1,0},{2,3},{3,2},{4,5},{5,4},{6,7},{7,6},{8,9},{9,8},{10,11... | collective-permute-start | bytes 786440 | tf_op jit(solution)/shard_map/ppermute | solution.py:49
  132.0 8.8 %collective-permute-start.7 = (bf16[32,512]{1,0:T(8,128)(2,1)S(1)}, bf16[32,512]{1,0:T(8,128)(2,1)S(1)}, u32[]{:S(2)}, u32[]{:S(2)}) collective-permute-start(bf16[32,512]{1,0:T(8,128)(2,1)S(1)} %fusion.3), channel_id=1, source_target_pairs={{0,1},{1,0},{2,3},{3,2},{4,5},{5,4},{6,7},{7,6},{8,9},{9,8},{10,11... | collective-permute-start | bytes 98312 | tf_op jit(solution)/shard_map/ppermute | solution.py:49
  137.8 5.8 %collective-permute-start.24 = (bf16[112,512]{1,0:T(8,128)(2,1)S(1)}, bf16[112,512]{1,0:T(8,128)(2,1)S(1)}, u32[]{:S(2)}, u32[]{:S(2)}) collective-permute-start(bf16[112,512]{1,0:T(8,128)(2,1)S(1)} %fusion.1), channel_id=1, source_target_pairs={{0,128},{128,0},{1,129},{129,1},{2,130},{130,2},{3,131},{131,3},{4... | collective-permute-start | bytes 344072 | tf_op jit(solution)/shard_map/ppermute | solution.py:49
  (16 other events, 29.8 us)

commit v4 on v3

--- a/solution.py
+++ b/solution.py
@@ -79,59 +79,56 @@
     return parts
 
 
-def flip_kernel(idx_ref, m_ref, p_ref, sign_ref, *rest):
-    mo_ref, po_ref = rest[-2:]
+def flip_kernel(idx_ref, h_ref, sign_ref, *rest):
     sign = (2 * sign_ref[...] - 1).astype(jnp.float32)
-    mo_ref[...] = (m_ref[...].astype(jnp.float32) * sign).astype(jnp.bfloat16)
-    po_ref[...] = (p_ref[...].astype(jnp.float32) * sign).astype(jnp.bfloat16)
-
-
-def flip(idx, hidden, sign_bits, rows, after=()):
+    rest[-1][...] = (h_ref[...].astype(jnp.float32) * sign).astype(jnp.bfloat16)
+
+
+def flip(idx, which, hidden, sign_bits, rows, after=()):
     cols = hidden.shape[1]
-    wide = 2 * BLOCK
-    block = pl.BlockSpec((rows, wide), lambda j, idx: (0, j))
     return pl.pallas_call(
         flip_kernel,
         grid_spec=pltpu.PrefetchScalarGridSpec(
             num_scalar_prefetch=1,
-            grid=(cols // wide,),
+            grid=(1,),
             in_specs=[
-                pl.BlockSpec((rows, wide), lambda j, idx: (idx[0], j)),
-                pl.BlockSpec((rows, wide), lambda j, idx: (idx[1], j)),
-                pl.BlockSpec((1, wide), lambda j, idx: (0, j)),
+                pl.BlockSpec((rows, cols), lambda i, idx: (idx[which], 0)),
+                pl.BlockSpec((1, cols), lambda i, idx: (0, 0)),
             ]
             + [ANY] * len(after),
-            out_specs=(block, block),
+            out_specs=pl.BlockSpec((rows, cols), lambda i, idx: (0, 0)),
         ),
-        out_shape=(pltpu.HBM((rows, cols), jnp.bfloat16),) * 2,
+        out_shape=jax.ShapeDtypeStruct((rows, cols), jnp.bfloat16),
         compiler_params=params(16),
-        cost_estimate=cost(2 * rows * cols, 8 * rows * cols),
+        cost_estimate=cost(rows * cols, 4 * rows * cols),
         name="flip",
-    )(idx, hidden, hidden, sign_bits, *after)
-
-
-def finish_kernel(idx_ref, sgn_ref, a_ref, b_ref, c_ref, d_ref, sign_ref, out_ref):
-    rows, cols = a_ref.shape
-    for at in range(0, cols, BLOCK):
-        here = pl.ds(at, BLOCK)
-        sign = (2 * sign_ref[:, here] - 1).astype(jnp.float32)
-        for i, (own, other) in enumerate(((a_ref, b_ref), (c_ref, d_ref))):
-            total = sgn_ref[0] * own[:, here].astype(jnp.float32) + other[:, here].astype(jnp.float32)
-            start = pl.multiple_of(idx_ref[i] * rows, rows)
-            out_ref[pl.ds(start, rows), here] = (total * sign).astype(jnp.bfloat16)
-
-
-def finish(idx, sgn, mine, part, sign_bits):
-    rows, cols = mine[0].shape
+    )(idx, hidden, sign_bits, *after)
+
+
+def finish_kernel(idx_ref, sgn_ref, own_ref, other_ref, sign_ref, *rest):
+    sign = (2 * sign_ref[...] - 1).astype(jnp.float32)
+    total = sgn_ref[0] * own_ref[...].astype(jnp.float32) + other_ref[...].astype(jnp.float32)
+    rest[-1][...] = (total * sign).astype(jnp.bfloat16)
+
+
+def finish(idx, which, sgn, own, other, sign_bits, into=None):
+    rows, cols = own.shape
+    block = pl.BlockSpec((rows, cols), lambda i, idx: (0, 0))
+    more = [] if into is None else [into]
     return pl.pallas_call(
         finish_kernel,
-        out_shape=jax.ShapeDtypeStruct((2 * rows, cols), jnp.bfloat16),
-        in_specs=[SM, SM] + [VM] * 5,
-        out_specs=VM,
+        grid_spec=pltpu.PrefetchScalarGridSpec(
+            num_scalar_prefetch=1,
+            grid=(1,),
+            in_specs=[SM, block, block, pl.BlockSpec((1, cols), lambda i, idx: (0, 0))] + [ANY] * len(more),
+            out_specs=pl.BlockSpec((rows, cols), lambda i, idx: (idx[which], 0)),
+        ),
+        out_shape=pltpu.HBM((2 * rows, cols), jnp.bfloat16),
+        input_output_aliases={5: 0} if more else {},
         compiler_params=params(16),
-        cost_estimate=cost(4 * rows * cols, 12 * rows * cols),
+        cost_estimate=cost(2 * rows * cols, 6 * rows * cols),
         name="finish",
-    )(idx, sgn, *mine, *part, sign_bits)
+    )(idx, sgn, own, other, sign_bits, *more)
 
 
 def back_kernel(m_ref, p_ref, w_ref, *rest):
@@ -351,17 +348,11 @@
     return jnp.concatenate([two] + [xor(two, ("z",), d) for d in (1, 2, 3)], axis=0)
 
 
-def gather_x(line):
-    half = line.shape[0] // 2
-    below, above = shift(line, "x", 1), shift(line, "x", -1)
-    return [line, below, above, shift(below[:half], "x", 1), shift(above[half:], "x", -1)]
-
-
 def source_places():
     nz, nx = lax.axis_size("z"), lax.axis_size("x")
     core = (lax.axis_index("core") ^ jnp.arange(2))[:, None, None]
     z = (lax.axis_index("z") ^ jnp.asarray([0, 4, 1, 5, 2, 6, 3, 7]))[None, None, :]
-    x = ((lax.axis_index("x") - jnp.asarray([0, 1, -1, -2])) & (nx - 1))[None, :, None]
+    x = ((lax.axis_index("x") - jnp.arange(nx)) & (nx - 1))[None, :, None]
     return ((core * nz + z) * nx + x).reshape(-1).astype(jnp.int32)
 
 
@@ -394,7 +385,8 @@
     def diagonal(value):
         return xor(value, ("yl", "core"), 3)
 
-    own, part = flip(idx, hidden, sign_bits, half)
+    own = flip(idx, 0, hidden, sign_bits, half)
+    part = flip(idx, 1, hidden, sign_bits, half, after=(own,))
     far, diag, near = swap(own, "yl"), diagonal(part), swap(part, "core")
 
     go_mine, go_part = of_mine(grad_out), of_part(grad_out)
@@ -403,26 +395,35 @@
     gq_there = swap(gq_give, "core")
     bound = 448.0 * jnp.exp2(exponents.astype(jnp.float32))
     bounds = (of_mine(bound), swap(of_part(bound), "core"))
-    pieces = gather_x(after(line, far, gq_here))
+    ring = after(line, far, gq_here)
+    pieces = [shift(ring, "x", s) if s else ring for s in range(4)]
 
     q_here, q_there, qt, grads = turn(
         sgn, core_at, (own, near, far, diag), table, bounds, (gq_here, gq_there), norm, 64
     )
-    got = lax.all_to_all(after(qt, *pieces), ("core", "z", "x"), 0, 0, tiled=True)
+    got = lax.all_to_all(after(qt, pieces[1], pieces[3]), ("core", "z", "x"), 0, 0, tiled=True)
     v_here, v_there = turn_back(grads, table, half, ff_local, norm)
-    cross, dcross, ncross = swap(v_here, "yl"), diagonal(v_there), swap(v_there, "core")
-    out_all = project((q_here, swap(q_there, "core")), down_weight, after=(v_here,)).reshape(2, 2, quarter, d_out)
+    cross, ncross = swap(v_here, "yl"), swap(v_there, "core")
+    early = [swap(pieces[i], "core") for i in (0, 1, 3)]
+
+    out_all = project((q_here, swap(q_there, "core")), down_weight, after=(v_here, *early)).reshape(2, 2, quarter, d_out)
+    give = lax.dynamic_index_in_dim(out_all, 1 - (yl ^ core), 0, keepdims=False)
+    across = swap(give, "yl")
+    dcross = diagonal(after(v_there, across))
+
+    grad_hidden = finish(idx, 0, sgn_y, v_here, cross, sign_bits)
+
+    late = swap(after(pieces[2], out_all), "core")
+    acc = weight_grad(source_places(), after(got, grad_hidden), pieces + [early[0], early[1], late, early[2]], half)
+
+    grad_hidden = finish(idx, 1, sgn_y, ncross, after(dcross, acc), sign_bits, into=grad_hidden)
+
     keep = lax.dynamic_index_in_dim(out_all, yl ^ core, 0, keepdims=False)
-    give = lax.dynamic_index_in_dim(out_all, 1 - (yl ^ core), 0, keepdims=False)
-    summed = keep.astype(jnp.float32) + swap(give, "yl").astype(jnp.float32)
+    summed = keep.astype(jnp.float32) + across.astype(jnp.float32)
     keep = lax.dynamic_index_in_dim(summed, core, 0, keepdims=False)
     give = lax.dynamic_index_in_dim(summed, 1 - core, 0, keepdims=False).astype(jnp.bfloat16)
     output = (keep + swap(give, "core").astype(jnp.float32)).astype(jnp.bfloat16)
 
-    grad_hidden = finish(idx, sgn_y, (v_here, cross), (ncross, dcross), sign_bits)
-
-    grads_all = pieces + [swap(p, "core") for p in pieces]
-    acc = weight_grad(source_places(), got, grads_all, half)
     acc = acc.reshape(2, -1, d_out)
     keep = lax.dynamic_index_in_dim(acc, yh, 0, keepdims=False)
     give = lax.dynamic_index_in_dim(acc, 1 - yh, 0, keepdims=False).astype(jnp.bfloat16)

time: 145 us -> 132 us (0.910); the launches traced: 144 us -> 130 us
  waiting for transfers between devices: 45.9 us -> 28.8 us
  local copies, waits for them, and re-layouts: 22 us -> 18.1 us
  starting transfers between devices: 41.8 us -> 44.2 us
  Pallas kernels: 30.4 us -> 32.7 us
  other arithmetic: 3.4 us -> 4.87 us
    ppermute x15 -> x14, waiting for transfers between devices: 11.3 us -> 0.29 us  [swap(): return lax.ppermute(value, axis, [(0, 1), (1, 0)])]
    ppermute x6, waiting for transfers between devices: 23.2 us -> 14.3 us  [xor(): return lax.ppermute(value, axes, [(i, i ^ by) for i in range(size)])]
    all_to_all x1, waiting for transfers between devices: 0.01 us -> 4.77 us  [local(): lax.all_to_all(after(qt, pieces[1], pieces[3]), ('core', 'z', 'x'), 0, 0,...]
    all_to_all x1, starting transfers between devices: 9 us -> 11.9 us  [local(): lax.all_to_all(after(qt, pieces[1], pieces[3]), ('core', 'z', 'x'), 0, 0,...]
    unnamed x44 -> x42, local copies, waits for them, and re-layouts: 19.8 us -> 17.1 us
    pallas_call x1 -> x2, Pallas kernels: 3.7 us -> 6.24 us  [finish(): pl.pallas_call(finish_kernel, grid_spec=pltpu.PrefetchScalarGridSpec(num_...]
    slice x2 -> x0, local copies, waits for them, and re-layouts: 1.94 us -> none  [the longest x1 0.97 us: gather_x(): above[half:]]
    ppermute x4 -> x3, waiting for transfers between devices: 11.4 us -> 9.46 us  [shift(): lax.ppermute(value, axis, [(i, (i + by) % size) for i in range(size)])]
  transfers between devices with their start and end apart: 26 -> 24, of which waited for: 6 -> 7; matrix products, arithmetic and copies ran while one was open for 3% -> 4% of each run, Pallas kernels for 19% -> 25%
where the time goes in v4:
time: 132 us; the launch traced here: 130 us
  starting transfers between devices  44.2 us (33%)
  Pallas kernels  32.7 us (25%)
  waiting for transfers between devices  28.8 us (22%)
  local copies, waits for them, and re-layouts  18.1 us (14%)
  other arithmetic  4.87 us (4%)
    unnamed x42, local copies, waits for them, and re-layouts  17.1 us
    ppermute x14, starting transfers between devices, swap(): return lax.ppermute(value, axis, [(0, 1), (1, 0)])  14.9 us
    ppermute x6, waiting for transfers between devices, xor(): return lax.ppermute(value, axes, [(i, i ^ by) for i in range(size)])  14.3 us
    all_to_all x1, starting transfers between devices, local(): lax.all_to_all(after(qt, pieces[1], pieces[3]), ('core', 'z', 'x'), 0, 0,...  11.9 us
    ppermute x6, starting transfers between devices, xor(): return lax.ppermute(value, axes, [(i, i ^ by) for i in range(size)])  11.8 us
    ppermute x3, waiting for transfers between devices, shift(): lax.ppermute(value, axis, [(i, (i + by) % size) for i in range(size)])  9.46 us
    pallas_call x1, Pallas kernels, turn(): pl.pallas_call(functools.partial(turn_kernel, nblk, norm), out_shape=(fla...  8.27 us
    pallas_call x2, Pallas kernels, finish(): pl.pallas_call(finish_kernel, grid_spec=pltpu.PrefetchScalarGridSpec(num_...  6.24 us
  transfers between devices with their start and end apart: 24, of which 7 were waited for; matrix products, arithmetic and copies ran while one was open for 4% of the time, Pallas kernels for 25%

profile of v4, /device:TPU:1, one launch (start us, length us, event | category | flops | bytes accessed | tf_op | source)
XLA Modules:
  0.0 129.5 jit_solution(1626138835500137120)
XLA Ops:
  0.7 1.5 %copy-done.2 = bf16[128,7168]{1,0:T(8,128)(2,1)S(1)} copy-done((bf16[128,7168]{1,0:T(8,128)(2,1)S(1)}, bf16[128,7168]{1,0:T(8,128)(2,1)}, u32[]{:S(2)}) %copy-start.2) | copy-done | bytes 1835032
  3.7 2.2 %collective-permute-start.1 = (bf16[64,7168]{1,0:T(8,128)(2,1)S(1)}, bf16[64,7168]{1,0:T(8,128)(2,1)}, u32[]{:S(2)}, u32[]{:S(2)}) collective-permute-start(bf16[64,7168]{1,0:T(8,128)(2,1)S(1)} %flip.2.rest_0_.own_ref), channel_id=1, source_target_pairs={{0,2},{2,0},{1,3},{3,1},{4,6},{6,4},{5,7},{7,5},{8,10},{10,8},{9,1... | collective-permute-start | bytes 2752520 | tf_op jit(solution)/shard_map/ppermute | solution.py:49
  5.9 7.0 %collective-permute-start.6 = (bf16[64,512]{1,0:T(8,128)(2,1)S(1)}, bf16[64,512]{1,0:T(8,128)(2,1)S(1)}, u32[]{:S(2)}, u32[]{:S(2)}) collective-permute-start(bf16[64,512]{1,0:T(8,128)(2,1)S(1)} %get-tuple-element.24.m_ref), channel_id=1, source_target_pairs={{0,64},{16,80},{32,96},{48,112},{64,0},{80,16},{96,32},{112,48},{1... | collective-permute-start | bytes 196616 | tf_op jit(solution)/shard_map/ppermute | solution.py:54
  12.9 1.7 %collective-permute-done.6 = bf16[64,512]{1,0:T(8,128)(2,1)S(1)} collective-permute-done((bf16[64,512]{1,0:T(8,128)(2,1)S(1)}, bf16[64,512]{1,0:T(8,128)(2,1)S(1)}, u32[]{:S(2)}, u32[]{:S(2)}) %collective-permute-start.6) | collective-permute-done | bytes 65568 | tf_op jit(solution)/shard_map/ppermute | solution.py:54
  15.3 2.7 %collective-permute-start.9 = (bf16[128,512]{1,0:T(8,128)(2,1)}, bf16[128,512]{1,0:T(8,128)(2,1)S(1)}, u32[]{:S(2)}, u32[]{:S(2)}) collective-permute-start(bf16[128,512]{1,0:T(8,128)(2,1)} %pad_maximum_fusion.1), channel_id=1, source_target_pairs={{0,48},{16,32},{32,16},{48,0},{64,112},{80,96},{96,80},{112,64},{1... | collective-permute-start | bytes 393224 | tf_op jit(solution)/shard_map/ppermute | solution.py:54
  18.0 1.6 %flip.3 = bf16[64,7168]{1,0:T(8,128)(2,1)} custom-call(s32[2]{0:T(128)S(1)} %pad_add_fusion.idx_ref, bf16[128,7168]{1,0:T(8,128)(2,1)S(1)} %copy-done.3, s32[1,7168]{1,0:T(1,128)S(1)} %bitcast.27, bf16[64,7168]{1,0:T(8,128)(2,1)S(1)} %flip.2.rest_0_.own_ref), custom_call_target="tpu_custom_call" | custom-call | flops 458752 | bytes 1835008 | tf_op jit(solution)/shard_map/flip/pallas_call | solution.py:89
  19.7 2.4 %collective-permute-start = (bf16[64,7168]{1,0:T(8,128)(2,1)}, bf16[64,7168]{1,0:T(8,128)(2,1)S(1)}, u32[]{:S(2)}, u32[]{:S(2)}) collective-permute-start(bf16[64,7168]{1,0:T(8,128)(2,1)} %flip.3), channel_id=1, source_target_pairs={{0,1},{1,0},{2,3},{3,2},{4,5},{5,4},{6,7},{7,6},{8,9},{9,8},{10,11... | collective-permute-start | bytes 2752520 | tf_op jit(solution)/shard_map/ppermute | solution.py:49
  22.1 3.1 %copy-done = bf16[7168,512]{1,0:T(8,128)(2,1)S(1)} copy-done((bf16[7168,512]{1,0:T(8,128)(2,1)S(1)}, bf16[7168,512]{1,0:T(8,128)(2,1)}, u32[]{:S(2)}) %copy-start) | copy-done | bytes 7340056
  25.2 5.1 %back.1 = (bf16[64,7168]{1,0:T(8,128)(2,1)}, bf16[64,7168]{1,0:T(8,128)(2,1)}) custom-call(bf16[64,512]{1,0:T(8,128)(2,1)S(1)} %get-tuple-element.24.m_ref, bf16[64,512]{1,0:T(8,128)(2,1)S(1)} %get-tuple-element.33.p_ref, bf16[7168,512]{1,0:T(8,128)(2,1)S(1)} %copy-done, bf16[64,7168]{1,0:T(8,128)(2,1)S(1)} %flip.2.rest_0_.own_ref), custom_call_target="tpu_custom_call" | custom-call | flops 939524096 | bytes 9175040 | tf_op jit(solution)/shard_map/back/pallas_call | solution.py:149
  32.4 1.2 collective-permute-start.7
  33.6 3.7 %collective-permute-done.7 = bf16[128,512]{1,0:T(8,128)(2,1)S(1)} collective-permute-done((bf16[128,512]{1,0:T(8,128)(2,1)}, bf16[128,512]{1,0:T(8,128)(2,1)S(1)}, u32[]{:S(2)}, u32[]{:S(2)}) %collective-permute-start.7) | collective-permute-done | bytes 131104 | tf_op jit(solution)/shard_map/ppermute | solution.py:54
  37.3 1.3 %collective-permute-start.3 = (f32[64,56]{1,0:T(8,128)S(1)}, f32[64,56]{1,0:T(8,128)S(1)}, u32[]{:S(2)}, u32[]{:S(2)}) collective-permute-start(f32[64,56]{1,0:T(8,128)S(1)} %get-tuple-element.35), channel_id=1, source_target_pairs={{0,1},{1,0},{2,3},{3,2},{4,5},{5,4},{6,7},{7,6},{8,9},{9,8},{10,11... | collective-permute-start | bytes 43016 | tf_op jit(solution)/shard_map/ppermute | solution.py:49
  38.6 1.9 %pad_maximum_fusion.refs_0_ = bf16[512,512]{1,0:T(8,128)(2,1)} fusion(bf16[128,512]{1,0:T(8,128)(2,1)} %copy-done.18, bf16[128,512]{1,0:T(8,128)(2,1)} %collective-permute-done.8, bf16[128,512]{1,0:T(8,128)(2,1)S(1)} %collective-permute-done.7, bf16[128,512]{1,0:T(8,128)(2,1)} %pad_maximum_fusion.1), kind=kLoop, calls=%fused_computation | loop fusion | flops 2097152 | bytes 1048576 | tf_op jit(solution)/shard_map/concatenate | solution.py:348
  40.5 1.2 collective-permute-start.11
  41.7 1.5 %collective-permute-start.13 = (bf16[512,512]{1,0:T(8,128)(2,1)}, bf16[512,512]{1,0:T(8,128)(2,1)}, u32[]{:S(2)}, u32[]{:S(2)}) collective-permute-start(bf16[512,512]{1,0:T(8,128)(2,1)} %pad_maximum_fusion.refs_0_), channel_id=1, source_target_pairs={{0,12},{4,0},{8,4},{12,8},{1,13},{5,1},{9,5},{13,9},{2,14},{6,2},{... | collective-permute-start | bytes 1572872 | tf_op jit(solution)/shard_map/ppermute | solution.py:59
  43.3 3.2 %collective-permute-done.2.diag_ref = bf16[64,7168]{1,0:T(8,128)(2,1)} collective-permute-done((bf16[64,7168]{1,0:T(8,128)(2,1)}, bf16[64,7168]{1,0:T(8,128)(2,1)}, u32[]{:S(2)}, u32[]{:S(2)}) %collective-permute-start.2) | collective-permute-done | bytes 917536 | tf_op jit(solution)/shard_map/ppermute | solution.py:54
  47.8 8.3 %turn.1 = (bf16[64,7168]{1,0:T(8,128)(2,1)}, bf16[64,7168]{1,0:T(8,128)(2,1)}, bf16[64,112,128]{2,1,0:T(8,128)(2,1)}, bf16[1024,896]{1,0:T(8,128)(2,1)}) custom-call(f32[2]{0:T(128)S(1)} %pad_maximum_fusion.2.sgn_ref, s32[1]{0:T(128)} %bitcast.2.core_ref, bf16[64,7168]{1,0:T(8,128)(2,1)S(1)} %flip.2.rest_0_.own_ref, ...), custom_call_target="tpu_custom_call" | custom-call | flops 1644167168 | bytes 9175040 | tf_op jit(solution)/shard_map/turn/pallas_call | solution.py:268
  56.0 11.9 %all-to-all-start = ((bf16[64,112,128]{2,1,0:T(8,128)(2,1)}), bf16[64,112,128]{2,1,0:T(8,128)(2,1)S(1)}, u32[]{:S(2)}, u32[]{:S(2)}) async-start(bf16[64,112,128]{2,1,0:T(8,128)(2,1)} %get-tuple-element.29), calls=%async_computation | async-start | bytes 3670016 | tf_op jit(solution)/shard_map/all_to_all | solution.py:404
  68.5 1.4 %copy-done.7 = bf16[896,896]{1,0:T(8,128)(2,1)S(1)} copy-done((bf16[896,896]{1,0:T(8,128)(2,1)S(1)}, bf16[896,896]{1,0:T(8,128)(2,1)}, u32[]{:S(2)}) %copy-start.7) | copy-done | bytes 1605656
  69.9 1.5 %copy-done.14 = bf16[1024,896]{1,0:T(8,128)(2,1)S(1)} copy-done((bf16[1024,896]{1,0:T(8,128)(2,1)S(1)}, bf16[1024,896]{1,0:T(8,128)(2,1)}, u32[]{:S(2)}) %copy-start.14) | copy-done | bytes 1835032
  71.4 3.7 %turn_back.1 = (bf16[64,7168]{1,0:T(8,128)(2,1)}, bf16[64,7168]{1,0:T(8,128)(2,1)}) custom-call(bf16[1024,896]{1,0:T(8,128)(2,1)S(1)} %copy-done.14, bf16[896,896]{1,0:T(8,128)(2,1)S(1)} %copy-done.7), custom_call_target="tpu_custom_call" | custom-call | flops 1644167168 | bytes 3670016 | tf_op jit(solution)/shard_map/turn_back/pallas_call | solution.py:299
  75.1 1.3 %collective-permute-start.19 = (bf16[64,7168]{1,0:T(8,128)(2,1)}, bf16[64,7168]{1,0:T(8,128)(2,1)}, u32[]{:S(2)}, u32[]{:S(2)}) collective-permute-start(bf16[64,7168]{1,0:T(8,128)(2,1)} %get-tuple-element.23.refs_3_.own_ref), channel_id=1, source_target_pairs={{0,2},{2,0},{1,3},{3,1},{4,6},{6,4},{5,7},{7,5},{8,10},{10,8},{9,1... | collective-permute-start | bytes 2752520 | tf_op jit(solution)/shard_map/ppermute | solution.py:49
  77.1 2.9 %collective-permute-start.20 = (bf16[512,512]{1,0:T(8,128)(2,1)}, bf16[512,512]{1,0:T(8,128)(2,1)}, u32[]{:S(2)}, u32[]{:S(2)}) collective-permute-start(bf16[512,512]{1,0:T(8,128)(2,1)} %pad_maximum_fusion.refs_0_), channel_id=1, source_target_pairs={{0,8},{4,12},{8,0},{12,4},{1,9},{5,13},{9,1},{13,5},{2,10},{6,14},... | collective-permute-start | bytes 1572872 | tf_op jit(solution)/shard_map/ppermute | solution.py:59
  81.0 3.1 %copy-done.1 = bf16[7168,512]{1,0:T(8,128)(2,1)S(1)} copy-done((bf16[7168,512]{1,0:T(8,128)(2,1)S(1)}, bf16[7168,512]{1,0:T(8,128)(2,1)}, u32[]{:S(2)}) %copy-start.1) | copy-done | bytes 7340056
  87.6 3.0 %project.1 = bf16[128,512]{1,0:T(8,128)(2,1)S(1)} custom-call(bf16[64,7168]{1,0:T(8,128)(2,1)S(1)} %copy-done.8, bf16[64,7168]{1,0:T(8,128)(2,1)S(1)} %copy-done.10, bf16[7168,512]{1,0:T(8,128)(2,1)S(1)} %copy-done.1, bf16[64,7168]{1,0:T(8,128)(2,1)S(1)} %copy-done.4, bf16[512,512]{1,0:T(8,128)(2,1)S(1)} %collective-permute-done.10.refs_4_, ...), custom_call_target="tpu_custom_call" | custom-call | flops 939524096 | bytes 7340032 | tf_op jit(solution)/shard_map/project/pallas_call | solution.py:184
  91.9 9.4 %collective-permute-done.20.refs_2_ = bf16[512,512]{1,0:T(8,128)(2,1)} collective-permute-done((bf16[512,512]{1,0:T(8,128)(2,1)}, bf16[512,512]{1,0:T(8,128)(2,1)}, u32[]{:S(2)}, u32[]{:S(2)}) %collective-permute-start.20) | collective-permute-done | bytes 524320 | tf_op jit(solution)/shard_map/ppermute | solution.py:59
  103.4 3.0 %finish.2.rest_0_ = bf16[128,7168]{1,0:T(8,128)(2,1)} custom-call(s32[2]{0:T(128)S(1)} %pad_add_fusion.idx_ref, f32[1]{0:T(128)} %bitcast.1.sgn_ref, bf16[64,7168]{1,0:T(8,128)(2,1)S(1)} %copy-done.5, bf16[64,7168]{1,0:T(8,128)(2,1)} %collective-permute-done.19.other_ref, s32[1,7168]{1,0:T(1,128)S(1)} %bitcast.28), custom_call_target="tpu_custom_call" | custom-call | flops 917504 | bytes 2752512 | tf_op jit(solution)/shard_map/finish/pallas_call | solution.py:118
  107.0 4.8 %all-to-all-done.r_ref = bf16[64,112,128]{2,1,0:T(8,128)(2,1)S(1)} async-done(((bf16[64,112,128]{2,1,0:T(8,128)(2,1)}), bf16[64,112,128]{2,1,0:T(8,128)(2,1)S(1)}, u32[]{:S(2)}, u32[]{:S(2)}) %all-to-all-start) | async-done | bytes 1835040 | tf_op jit(solution)/shard_map/all_to_all | solution.py:404
  111.8 4.1 %weight_grad.1 = f32[224,512]{1,0:T(8,128)S(1)} custom-call(s32[64]{0:T(128)S(1)} %add.90.at_ref, bf16[64,112,128]{2,1,0:T(8,128)(2,1)S(1)} %all-to-all-done.r_ref, bf16[512,512]{1,0:T(8,128)(2,1)} %pad_maximum_fusion.refs_0_, bf16[512,512]{1,0:T(8,128)(2,1)} %collective-permute-done.11.refs_1_, bf16[512,512]{1,0:T(8,128)(2,1)} %collective-permute-done.20.refs_2_, ...), custom_call_target="tpu_custom_call" | custom-call | flops 1879048192 | bytes 10223616 | tf_op jit(solution)/shard_map/weight_grad/pallas_call | solution.py:331
  115.9 3.0 %collective-permute-start.22 = (bf16[112,512]{1,0:T(8,128)(2,1)S(1)}, bf16[112,512]{1,0:T(8,128)(2,1)S(1)}, u32[]{:S(2)}, u32[]{:S(2)}) collective-permute-start(bf16[112,512]{1,0:T(8,128)(2,1)S(1)} %fusion.1), channel_id=1, source_target_pairs={{0,128},{128,0},{1,129},{129,1},{2,130},{130,2},{3,131},{131,3},{4... | collective-permute-start | bytes 344072 | tf_op jit(solution)/shard_map/ppermute | solution.py:49
  119.6 5.7 %collective-permute-done.18.other_ref = bf16[64,7168]{1,0:T(8,128)(2,1)} collective-permute-done((bf16[64,7168]{1,0:T(8,128)(2,1)}, bf16[64,7168]{1,0:T(8,128)(2,1)}, u32[]{:S(2)}, u32[]{:S(2)}) %collective-permute-start.18) | collective-permute-done | bytes 917536 | tf_op jit(solution)/shard_map/ppermute | solution.py:54
  125.3 3.3 %finish.3 = bf16[128,7168]{1,0:T(8,128)(2,1)} custom-call(s32[2]{0:T(128)S(1)} %pad_add_fusion.idx_ref, f32[1]{0:T(128)} %bitcast.1.sgn_ref, bf16[64,7168]{1,0:T(8,128)(2,1)} %collective-permute-done.17.own_ref, bf16[64,7168]{1,0:T(8,128)(2,1)} %collective-permute-done.18.other_ref, s32[1,7168]{1,0:T(1,128)S(1)} %bitcast.29, ...), custom_call_target="tpu_custom_call", output_to_operand_aliasing={{}: (5, {})} | custom-call | flops 917504 | bytes 2752512 | tf_op jit(solution)/shard_map/finish/pallas_call | solution.py:118
  (88 shorter events, 17.0 us)
Async XLA Ops:
  3.0 15.1 %copy-start.3 = (bf16[128,7168]{1,0:T(8,128)(2,1)S(1)}, bf16[128,7168]{1,0:T(8,128)(2,1)}, u32[]{:S(2)}) copy-start(bf16[128,7168]{1,0:T(8,128)(2,1)} %h_ref.3) | copy-start | bytes 5505028
  3.0 15.1 %copy-start.13 = (s32[7168]{0:T(1024)S(1)}, s32[7168]{0:T(1024)}, u32[]{:S(2)}) copy-start(s32[7168]{0:T(1024)} %param.8) | copy-start | bytes 86020
  3.7 36.8 %collective-permute-start.1 = (bf16[64,7168]{1,0:T(8,128)(2,1)S(1)}, bf16[64,7168]{1,0:T(8,128)(2,1)}, u32[]{:S(2)}, u32[]{:S(2)}) collective-permute-start(bf16[64,7168]{1,0:T(8,128)(2,1)S(1)} %flip.2.rest_0_.own_ref), channel_id=1, source_target_pairs={{0,2},{2,0},{1,3},{3,1},{4,6},{6,4},{5,7},{7,5},{8,10},{10,8},{9,1... | collective-permute-start | bytes 2752520 | tf_op jit(solution)/shard_map/ppermute | solution.py:49
  5.9 8.7 %collective-permute-start.6 = (bf16[64,512]{1,0:T(8,128)(2,1)S(1)}, bf16[64,512]{1,0:T(8,128)(2,1)S(1)}, u32[]{:S(2)}, u32[]{:S(2)}) collective-permute-start(bf16[64,512]{1,0:T(8,128)(2,1)S(1)} %get-tuple-element.24.m_ref), channel_id=1, source_target_pairs={{0,64},{16,80},{32,96},{48,112},{64,0},{80,16},{96,32},{112,48},{1... | collective-permute-start | bytes 196616 | tf_op jit(solution)/shard_map/ppermute | solution.py:54
  15.3 15.0 %collective-permute-start.9 = (bf16[128,512]{1,0:T(8,128)(2,1)}, bf16[128,512]{1,0:T(8,128)(2,1)S(1)}, u32[]{:S(2)}, u32[]{:S(2)}) collective-permute-start(bf16[128,512]{1,0:T(8,128)(2,1)} %pad_maximum_fusion.1), channel_id=1, source_target_pairs={{0,48},{16,32},{32,16},{48,0},{64,112},{80,96},{96,80},{112,64},{1... | collective-permute-start | bytes 393224 | tf_op jit(solution)/shard_map/ppermute | solution.py:54
  19.7 23.7 %collective-permute-start = (bf16[64,7168]{1,0:T(8,128)(2,1)}, bf16[64,7168]{1,0:T(8,128)(2,1)S(1)}, u32[]{:S(2)}, u32[]{:S(2)}) collective-permute-start(bf16[64,7168]{1,0:T(8,128)(2,1)} %flip.3), channel_id=1, source_target_pairs={{0,1},{1,0},{2,3},{3,2},{4,5},{5,4},{6,7},{7,6},{8,9},{9,8},{10,11... | collective-permute-start | bytes 2752520 | tf_op jit(solution)/shard_map/ppermute | solution.py:49
  22.0 24.5 %collective-permute-start.2 = (bf16[64,7168]{1,0:T(8,128)(2,1)}, bf16[64,7168]{1,0:T(8,128)(2,1)}, u32[]{:S(2)}, u32[]{:S(2)}) collective-permute-start(bf16[64,7168]{1,0:T(8,128)(2,1)} %flip.3), channel_id=1, source_target_pairs={{0,3},{1,2},{2,1},{3,0},{4,7},{5,6},{6,5},{7,4},{8,11},{9,10},{10,... | collective-permute-start | bytes 2752520 | tf_op jit(solution)/shard_map/ppermute | solution.py:54
  22.1 10.3 %collective-permute-start.8 = (bf16[128,512]{1,0:T(8,128)(2,1)}, bf16[128,512]{1,0:T(8,128)(2,1)}, u32[]{:S(2)}, u32[]{:S(2)}) collective-permute-start(bf16[128,512]{1,0:T(8,128)(2,1)} %pad_maximum_fusion.1), channel_id=1, source_target_pairs={{0,32},{16,48},{32,0},{48,16},{64,96},{80,112},{96,64},{112,80},{1... | collective-permute-start | bytes 393224 | tf_op jit(solution)/shard_map/ppermute | solution.py:54
  25.2 5.7 %copy-start.19 = (s32[128,56]{0,1:T(8,128)S(1)}, s32[128,56]{0,1:T(8,128)}, u32[]{:S(2)}) copy-start(s32[128,56]{0,1:T(8,128)} %param.9) | copy-start | bytes 86020
  25.2 21.4 %copy-start.6 = (bf16[896,896]{1,0:T(8,128)(2,1)S(1)}, bf16[896,896]{1,0:T(8,128)(2,1)}, u32[]{:S(2)}) copy-start(bf16[896,896]{1,0:T(8,128)(2,1)} %constant.67.clone.table_ref) | copy-start | bytes 4816900
  30.3 16.3 %collective-permute-start.4 = (bf16[64,7168]{1,0:T(8,128)(2,1)}, bf16[64,7168]{1,0:T(8,128)(2,1)}, u32[]{:S(2)}, u32[]{:S(2)}) collective-permute-start(bf16[64,7168]{1,0:T(8,128)(2,1)} %get-tuple-element.19), channel_id=1, source_target_pairs={{0,1},{1,0},{2,3},{3,2},{4,5},{5,4},{6,7},{7,6},{8,9},{9,8},{10,11... | collective-permute-start | bytes 2752520 | tf_op jit(solution)/shard_map/ppermute | solution.py:49
  32.4 4.9 %collective-permute-start.7 = (bf16[128,512]{1,0:T(8,128)(2,1)}, bf16[128,512]{1,0:T(8,128)(2,1)S(1)}, u32[]{:S(2)}, u32[]{:S(2)}) collective-permute-start(bf16[128,512]{1,0:T(8,128)(2,1)} %pad_maximum_fusion.1), channel_id=1, source_target_pairs={{0,16},{16,0},{32,48},{48,32},{64,80},{80,64},{96,112},{112,96},{1... | collective-permute-start | bytes 393224 | tf_op jit(solution)/shard_map/ppermute | solution.py:54
  37.3 4.4 %collective-permute-start.3 = (f32[64,56]{1,0:T(8,128)S(1)}, f32[64,56]{1,0:T(8,128)S(1)}, u32[]{:S(2)}, u32[]{:S(2)}) collective-permute-start(f32[64,56]{1,0:T(8,128)S(1)} %get-tuple-element.35), channel_id=1, source_target_pairs={{0,1},{1,0},{2,3},{3,2},{4,5},{5,4},{6,7},{7,6},{8,9},{9,8},{10,11... | collective-permute-start | bytes 43016 | tf_op jit(solution)/shard_map/ppermute | solution.py:49
  40.5 15.5 %collective-permute-start.11 = (bf16[512,512]{1,0:T(8,128)(2,1)}, bf16[512,512]{1,0:T(8,128)(2,1)}, u32[]{:S(2)}, u32[]{:S(2)}) collective-permute-start(bf16[512,512]{1,0:T(8,128)(2,1)} %pad_maximum_fusion.refs_0_), channel_id=1, source_target_pairs={{0,4},{4,8},{8,12},{12,0},{1,5},{5,9},{9,13},{13,1},{2,6},{6,10},{... | collective-permute-start | bytes 1572872 | tf_op jit(solution)/shard_map/ppermute | solution.py:59
  41.7 14.3 %collective-permute-start.13 = (bf16[512,512]{1,0:T(8,128)(2,1)}, bf16[512,512]{1,0:T(8,128)(2,1)}, u32[]{:S(2)}, u32[]{:S(2)}) collective-permute-start(bf16[512,512]{1,0:T(8,128)(2,1)} %pad_maximum_fusion.refs_0_), channel_id=1, source_target_pairs={{0,12},{4,0},{8,4},{12,8},{1,13},{5,1},{9,5},{13,9},{2,14},{6,2},{... | collective-permute-start | bytes 1572872 | tf_op jit(solution)/shard_map/ppermute | solution.py:59
  56.0 55.7 %all-to-all-start = ((bf16[64,112,128]{2,1,0:T(8,128)(2,1)}), bf16[64,112,128]{2,1,0:T(8,128)(2,1)S(1)}, u32[]{:S(2)}, u32[]{:S(2)}) async-start(bf16[64,112,128]{2,1,0:T(8,128)(2,1)} %get-tuple-element.29), calls=%async_computation | async-start | bytes 3670016 | tf_op jit(solution)/shard_map/all_to_all | solution.py:404
  67.9 12.1 %collective-permute-start.5 = (bf16[64,7168]{1,0:T(8,128)(2,1)}, bf16[64,7168]{1,0:T(8,128)(2,1)S(1)}, u32[]{:S(2)}, u32[]{:S(2)}) collective-permute-start(bf16[64,7168]{1,0:T(8,128)(2,1)} %get-tuple-element.21), channel_id=1, source_target_pairs={{0,1},{1,0},{2,3},{3,2},{4,5},{5,4},{6,7},{7,6},{8,9},{9,8},{10,11... | collective-permute-start | bytes 2752520 | tf_op jit(solution)/shard_map/ppermute | solution.py:49
  68.4 8.7 %collective-permute-start.10 = (bf16[512,512]{1,0:T(8,128)(2,1)}, bf16[512,512]{1,0:T(8,128)(2,1)S(1)}, u32[]{:S(2)}, u32[]{:S(2)}) collective-permute-start(bf16[512,512]{1,0:T(8,128)(2,1)} %pad_maximum_fusion.refs_0_), channel_id=1, source_target_pairs={{0,1},{1,0},{2,3},{3,2},{4,5},{5,4},{6,7},{7,6},{8,9},{9,8},{10,11... | collective-permute-start | bytes 1572872 | tf_op jit(solution)/shard_map/ppermute | solution.py:49
  71.4 5.6 %copy-start.20 = (s32[8]{0:T(128)S(1)}, s32[8]{0:T(128)}, u32[]{:S(2)}) copy-start(s32[8]{0:T(128)} %constant.68.clone) | copy-start | bytes 100
  75.1 28.3 %collective-permute-start.19 = (bf16[64,7168]{1,0:T(8,128)(2,1)}, bf16[64,7168]{1,0:T(8,128)(2,1)}, u32[]{:S(2)}, u32[]{:S(2)}) collective-permute-start(bf16[64,7168]{1,0:T(8,128)(2,1)} %get-tuple-element.23.refs_3_.own_ref), channel_id=1, source_target_pairs={{0,2},{2,0},{1,3},{3,1},{4,6},{6,4},{5,7},{7,5},{8,10},{10,8},{9,1... | collective-permute-start | bytes 2752520 | tf_op jit(solution)/shard_map/ppermute | solution.py:49
  76.4 4.6 %collective-permute-start.12 = (bf16[512,512]{1,0:T(8,128)(2,1)}, bf16[512,512]{1,0:T(8,128)(2,1)}, u32[]{:S(2)}, u32[]{:S(2)}) collective-permute-start(bf16[512,512]{1,0:T(8,128)(2,1)} %collective-permute-done.11.refs_1_), channel_id=1, source_target_pairs={{0,1},{1,0},{2,3},{3,2},{4,5},{5,4},{6,7},{7,6},{8,9},{9,8},{10,11... | collective-permute-start | bytes 1572872 | tf_op jit(solution)/shard_map/ppermute | solution.py:49
  77.0 3.9 %collective-permute-start.14 = (bf16[512,512]{1,0:T(8,128)(2,1)}, bf16[512,512]{1,0:T(8,128)(2,1)}, u32[]{:S(2)}, u32[]{:S(2)}) collective-permute-start(bf16[512,512]{1,0:T(8,128)(2,1)} %collective-permute-done.13.refs_3_), channel_id=1, source_target_pairs={{0,1},{1,0},{2,3},{3,2},{4,5},{5,4},{6,7},{7,6},{8,9},{9,8},{10,11... | collective-permute-start | bytes 1572872 | tf_op jit(solution)/shard_map/ppermute | solution.py:49
  77.1 24.3 %collective-permute-start.20 = (bf16[512,512]{1,0:T(8,128)(2,1)}, bf16[512,512]{1,0:T(8,128)(2,1)}, u32[]{:S(2)}, u32[]{:S(2)}) collective-permute-start(bf16[512,512]{1,0:T(8,128)(2,1)} %pad_maximum_fusion.refs_0_), channel_id=1, source_target_pairs={{0,8},{4,12},{8,0},{12,4},{1,9},{5,13},{9,1},{13,5},{2,10},{6,14},... | collective-permute-start | bytes 1572872 | tf_op jit(solution)/shard_map/ppermute | solution.py:59
  87.6 15.8 %copy-start.5 = (bf16[64,7168]{1,0:T(8,128)(2,1)S(1)}, bf16[64,7168]{1,0:T(8,128)(2,1)}, u32[]{:S(2)}) copy-start(bf16[64,7168]{1,0:T(8,128)(2,1)} %get-tuple-element.23.refs_3_.own_ref) | copy-start | bytes 2752516
  90.6 11.7 %collective-permute-start.15 = (bf16[2,32,512]{2,1,0:T(8,128)(2,1)S(1)}, bf16[2,32,512]{2,1,0:T(8,128)(2,1)S(1)}, u32[]{:S(2)}, u32[]{:S(2)}) collective-permute-start(bf16[2,32,512]{2,1,0:T(8,128)(2,1)S(1)} %dynamic-slice_bitcast_fusion), channel_id=1, source_target_pairs={{0,2},{2,0},{1,3},{3,1},{4,6},{6,4},{5,7},{7,5},{8,10},{10,8},{9,1... | collective-permute-start | bytes 196616 | tf_op jit(solution)/shard_map/ppermute | solution.py:49
  90.9 34.4 %collective-permute-start.17 = (bf16[64,7168]{1,0:T(8,128)(2,1)}, bf16[64,7168]{1,0:T(8,128)(2,1)}, u32[]{:S(2)}, u32[]{:S(2)}) collective-permute-start(bf16[64,7168]{1,0:T(8,128)(2,1)} %get-tuple-element.27), channel_id=1, source_target_pairs={{0,1},{1,0},{2,3},{3,2},{4,5},{5,4},{6,7},{7,6},{8,9},{9,8},{10,11... | collective-permute-start | bytes 2752520 | tf_op jit(solution)/shard_map/ppermute | solution.py:49
  101.4 10.4 %collective-permute-start.21 = (bf16[512,512]{1,0:T(8,128)(2,1)}, bf16[512,512]{1,0:T(8,128)(2,1)}, u32[]{:S(2)}, u32[]{:S(2)}) collective-permute-start(bf16[512,512]{1,0:T(8,128)(2,1)} %collective-permute-done.20.refs_2_), channel_id=1, source_target_pairs={{0,1},{1,0},{2,3},{3,2},{4,5},{5,4},{6,7},{7,6},{8,9},{9,8},{10,11... | collective-permute-start | bytes 1572872 | tf_op jit(solution)/shard_map/ppermute | solution.py:49
  102.4 22.9 %collective-permute-start.18 = (bf16[64,7168]{1,0:T(8,128)(2,1)}, bf16[64,7168]{1,0:T(8,128)(2,1)}, u32[]{:S(2)}, u32[]{:S(2)}) collective-permute-start(bf16[64,7168]{1,0:T(8,128)(2,1)} %get-tuple-element.27), channel_id=1, source_target_pairs={{0,3},{1,2},{2,1},{3,0},{4,7},{5,6},{6,5},{7,4},{8,11},{9,10},{10,... | collective-permute-start | bytes 2752520 | tf_op jit(solution)/shard_map/ppermute | solution.py:54
  106.4 5.4 %copy-start.15 = (f32[2,32,512]{2,1,0:T(8,128)}, f32[2,32,512]{2,1,0:T(8,128)S(1)}, u32[]{:S(2)}) copy-start(f32[2,32,512]{2,1,0:T(8,128)S(1)} %convert_add_fusion) | copy-start | bytes 393220
  106.4 12.5 %collective-permute-start.16 = (bf16[32,512]{1,0:T(8,128)(2,1)S(1)}, bf16[32,512]{1,0:T(8,128)(2,1)S(1)}, u32[]{:S(2)}, u32[]{:S(2)}) collective-permute-start(bf16[32,512]{1,0:T(8,128)(2,1)S(1)} %fusion.3), channel_id=1, source_target_pairs={{0,1},{1,0},{2,3},{3,2},{4,5},{5,4},{6,7},{7,6},{8,9},{9,8},{10,11... | collective-permute-start | bytes 98312 | tf_op jit(solution)/shard_map/ppermute | solution.py:49
  111.8 7.2 %copy-start.16 = (f32[2,32,512]{2,1,0:T(8,128)S(1)}, f32[2,32,512]{2,1,0:T(8,128)}, u32[]{:S(2)}) copy-start(f32[2,32,512]{2,1,0:T(8,128)} %copy-done.15) | copy-start | bytes 393220
  115.9 12.9 %collective-permute-start.22 = (bf16[112,512]{1,0:T(8,128)(2,1)S(1)}, bf16[112,512]{1,0:T(8,128)(2,1)S(1)}, u32[]{:S(2)}, u32[]{:S(2)}) collective-permute-start(bf16[112,512]{1,0:T(8,128)(2,1)S(1)} %fusion.1), channel_id=1, source_target_pairs={{0,128},{128,0},{1,129},{129,1},{2,130},{130,2},{3,131},{131,3},{4... | collective-permute-start | bytes 344072 | tf_op jit(solution)/shard_map/ppermute | solution.py:49
  (13 other events, 20.6 us)

commit v5 on v4

--- a/solution.py
+++ b/solution.py
@@ -57,6 +57,10 @@
 def shift(value, axis, by):
     size = lax.axis_size(axis)
     return lax.ppermute(value, axis, [(i, (i + by) % size) for i in range(size)])
+
+
+def in_hbm(value):
+    return pltpu.with_memory_space_constraint(value, pltpu.HBM)
 
 
 def params(mib):
@@ -106,9 +110,12 @@
 
 
 def finish_kernel(idx_ref, sgn_ref, own_ref, other_ref, sign_ref, *rest):
-    sign = (2 * sign_ref[...] - 1).astype(jnp.float32)
-    total = sgn_ref[0] * own_ref[...].astype(jnp.float32) + other_ref[...].astype(jnp.float32)
-    rest[-1][...] = (total * sign).astype(jnp.bfloat16)
+    out_ref = rest[-1]
+    for at in range(0, out_ref.shape[1], BLOCK):
+        here = pl.ds(at, BLOCK)
+        sign = (2 * sign_ref[:, here] - 1).astype(jnp.float32)
+        total = sgn_ref[0] * own_ref[:, here].astype(jnp.float32) + other_ref[:, here].astype(jnp.float32)
+        out_ref[:, here] = (total * sign).astype(jnp.bfloat16)
 
 
 def finish(idx, which, sgn, own, other, sign_bits, into=None):
@@ -274,7 +281,7 @@
         compiler_params=params(32),
         cost_estimate=cost(2 * deep * BLOCK * BLOCK, 2 * rows * cols * 10),
         name="turn",
-    )(sgn, core, *ins, table, *bounds, *gqs)
+    )(sgn, core, *ins, table, *bounds, *[in_hbm(g) for g in gqs])
 
 
 def return_kernel(nblk, norm, u_ref, table_ref, here_ref, there_ref, spun_ref):
@@ -305,42 +312,38 @@
         compiler_params=params(24),
         cost_estimate=cost(2 * deep * BLOCK * BLOCK, 4 * rows * cols * 2),
         name="turn_back",
-    )(grads, table)
+    )(in_hbm(grads), in_hbm(table))
 
 
 def weight_grad_kernel(rows, toks, at_ref, r_ref, *refs):
-    grad_refs, (out_ref, lhs_ref, rhs_ref) = refs[:-3], refs[-3:]
-    slabs = LANES // toks
-    slab = lax.broadcasted_iota(jnp.int32, (rows, LANES), 1) // toks
-    blocks = [(ref, at) for ref in grad_refs for at in range(0, ref.shape[0], toks)]
-    for place, (ref, start) in enumerate(blocks):
-        value = r_ref[at_ref[place]]
-        zero = jnp.zeros_like(value)
-        at = place * LANES
-        grads = ref[pl.ds(start, toks), :]
-        for i in range(slabs):
-            lhs_ref[i * rows : (i + 1) * rows, pl.ds(at, LANES)] = jnp.where(slab == i, value, zero)
-            rhs_ref[pl.ds(at + i * toks, toks), :] = grads
-    out_ref[...] = jnp.dot(lhs_ref[...], rhs_ref[...], preferred_element_type=jnp.float32)
+    grad_refs, (out_ref, lhs_ref) = refs[:-2], refs[-2:]
+    low = lax.broadcasted_iota(jnp.int32, (rows, LANES), 1) < toks
+    for place in range(0, r_ref.shape[0], 2):
+        first, second = r_ref[at_ref[place]], r_ref[at_ref[place + 1]]
+        cols = pl.ds(place * toks, LANES)
+        lhs_ref[0:rows, cols] = jnp.where(low, first, jnp.roll(second, toks, 1))
+        lhs_ref[rows : 2 * rows, cols] = jnp.where(low, jnp.roll(first, toks, 1), second)
+    total, at = None, 0
+    for ref in grad_refs:
+        deep = ref.shape[0]
+        part = jnp.dot(lhs_ref[:, at : at + deep], ref[...], preferred_element_type=jnp.float32)
+        total, at = part if total is None else total + part, at + deep
+    out_ref[...] = total
 
 
 def weight_grad(places, received, grads, toks):
     nsrc, rows, _ = received.shape
     wide = grads[0].shape[1]
-    slabs = LANES // toks
     return pl.pallas_call(
         functools.partial(weight_grad_kernel, rows, toks),
-        out_shape=jax.ShapeDtypeStruct((slabs * rows, wide), jnp.float32),
+        out_shape=jax.ShapeDtypeStruct((2 * rows, wide), jnp.float32),
         in_specs=[SM] + [VM] * (1 + len(grads)),
         out_specs=VM,
-        scratch_shapes=[
-            pltpu.VMEM((slabs * rows, nsrc * LANES), jnp.bfloat16),
-            pltpu.VMEM((nsrc * LANES, wide), jnp.bfloat16),
-        ],
-        compiler_params=params(40),
-        cost_estimate=cost(2 * slabs * rows * nsrc * LANES * wide, 2 * nsrc * LANES * (rows + wide)),
+        scratch_shapes=[pltpu.VMEM((2 * rows, nsrc * toks), jnp.bfloat16)],
+        compiler_params=params(32),
+        cost_estimate=cost(4 * rows * nsrc * toks * wide, 2 * nsrc * toks * (2 * rows + wide)),
         name="weight_grad",
-    )(places, received, *grads)
+    )(places, received, *[in_hbm(g) if g.shape[0] > 4 * toks else g for g in grads])
 
 
 def gather_z(value, *gates):
@@ -396,13 +399,14 @@
     bound = 448.0 * jnp.exp2(exponents.astype(jnp.float32))
     bounds = (of_mine(bound), swap(of_part(bound), "core"))
     ring = after(line, far, gq_here)
-    pieces = [shift(ring, "x", s) if s else ring for s in range(4)]
+    pieces = [ring, shift(ring, "x", 1), None, shift(ring, "x", 3)]
 
     q_here, q_there, qt, grads = turn(
         sgn, core_at, (own, near, far, diag), table, bounds, (gq_here, gq_there), norm, 64
     )
     got = lax.all_to_all(after(qt, pieces[1], pieces[3]), ("core", "z", "x"), 0, 0, tiled=True)
     v_here, v_there = turn_back(grads, table, half, ff_local, norm)
+    pieces[2] = shift(after(ring, v_here), "x", 2)
     cross, ncross = swap(v_here, "yl"), swap(v_there, "core")
     early = [swap(pieces[i], "core") for i in (0, 1, 3)]
 
@@ -413,8 +417,10 @@
 
     grad_hidden = finish(idx, 0, sgn_y, v_here, cross, sign_bits)
 
-    late = swap(after(pieces[2], out_all), "core")
-    acc = weight_grad(source_places(), after(got, grad_hidden), pieces + [early[0], early[1], late, early[2]], half)
+    gated = after(pieces[2], across)
+    quads = gated.shape[0] // 4
+    late = [swap(gated[i * quads : (i + 1) * quads], "core") for i in range(4)]
+    acc = weight_grad(source_places(), after(got, grad_hidden), pieces + [early[0], early[1], *late, early[2]], half)
 
     grad_hidden = finish(idx, 1, sgn_y, ncross, after(dcross, acc), sign_bits, into=grad_hidden)
 

time: 132 us -> 126 us (0.955); the launches traced: 130 us -> 126 us
  local copies, waits for them, and re-layouts: 18.1 us -> 12.3 us
  Pallas kernels: 32.7 us -> 36.7 us
  waiting for transfers between devices: 28.8 us -> 25.9 us
    ppermute x3, waiting for transfers between devices: 9.46 us -> 0.96 us  [shift(): lax.ppermute(value, axis, [(i, (i + by) % size) for i in range(size)])]
    ppermute x14 -> x17, waiting for transfers between devices: 0.29 us -> 8.17 us  [swap(): return lax.ppermute(value, axis, [(0, 1), (1, 0)])]
    unnamed x42 -> x36, local copies, waits for them, and re-layouts: 17.1 us -> 10.4 us
    ppermute x6, waiting for transfers between devices: 14.3 us -> 11.6 us  [xor(): return lax.ppermute(value, axes, [(i, i ^ by) for i in range(size)])]
    pallas_call x1, Pallas kernels: 3.02 us -> 5.42 us  [project(): pl.pallas_call(functools.partial(project_kernel, n), grid=(cols // BLOCK,...]
    pallas_call x1, Pallas kernels: 3.65 us -> 5.71 us  [turn_back(): pl.pallas_call(functools.partial(return_kernel, cols // BLOCK, norm), out...]
    ppermute x6, starting transfers between devices: 11.8 us -> 13.3 us  [xor(): return lax.ppermute(value, axes, [(i, i ^ by) for i in range(size)])]
    ppermute x14 -> x17, starting transfers between devices: 14.9 us -> 14.7 us  [swap(): return lax.ppermute(value, axis, [(0, 1), (1, 0)])]
  transfers between devices with their start and end apart: 24 -> 27, of which waited for: 7 -> 9; matrix products, arithmetic and copies ran while one was open for 4% -> 5% of each run, Pallas kernels for 25% -> 29%
where the time goes in v5:
time: 126 us
  starting transfers between devices  45.3 us (36%)
  Pallas kernels  36.7 us (29%)
  waiting for transfers between devices  25.9 us (21%)
  local copies, waits for them, and re-layouts  12.3 us (10%)
  other arithmetic  4.85 us (4%)
    ppermute x17, starting transfers between devices, swap(): return lax.ppermute(value, axis, [(0, 1), (1, 0)])  14.7 us
    ppermute x6, starting transfers between devices, xor(): return lax.ppermute(value, axes, [(i, i ^ by) for i in range(size)])  13.3 us
    all_to_all x1, starting transfers between devices, local(): lax.all_to_all(after(qt, pieces[1], pieces[3]), ('core', 'z', 'x'), 0, 0,...  11.7 us
    ppermute x6, waiting for transfers between devices, xor(): return lax.ppermute(value, axes, [(i, i ^ by) for i in range(size)])  11.6 us
    unnamed x36, local copies, waits for them, and re-layouts  10.4 us
    pallas_call x1, Pallas kernels, turn(): pl.pallas_call(functools.partial(turn_kernel, nblk, norm), out_shape=(fla...  8.6 us
    ppermute x17, waiting for transfers between devices, swap(): return lax.ppermute(value, axis, [(0, 1), (1, 0)])  8.17 us
    pallas_call x2, Pallas kernels, finish(): pl.pallas_call(finish_kernel, grid_spec=pltpu.PrefetchScalarGridSpec(num_...  6.25 us
  transfers between devices with their start and end apart: 27, of which 9 were waited for; matrix products, arithmetic and copies ran while one was open for 5% of the time, Pallas kernels for 29%

profile of v5, /device:TPU:1, one launch (start us, length us, event | category | flops | bytes accessed | tf_op | source)
XLA Modules:
  0.0 125.8 jit_solution(10086781077727649437)
XLA Ops:
  0.7 1.5 %copy-done.2 = bf16[128,7168]{1,0:T(8,128)(2,1)S(1)} copy-done((bf16[128,7168]{1,0:T(8,128)(2,1)S(1)}, bf16[128,7168]{1,0:T(8,128)(2,1)}, u32[]{:S(2)}) %copy-start.2) | copy-done | bytes 1835032
  3.7 2.2 %collective-permute-start.1 = (bf16[64,7168]{1,0:T(8,128)(2,1)S(1)}, bf16[64,7168]{1,0:T(8,128)(2,1)}, u32[]{:S(2)}, u32[]{:S(2)}) collective-permute-start(bf16[64,7168]{1,0:T(8,128)(2,1)S(1)} %flip.2.rest_0_.own_ref), channel_id=1, source_target_pairs={{0,2},{2,0},{1,3},{3,1},{4,6},{6,4},{5,7},{7,5},{8,10},{10,8},{9,1... | collective-permute-start | bytes 2752520 | tf_op jit(solution)/shard_map/ppermute | solution.py:49
  5.9 7.0 %collective-permute-start.6 = (bf16[64,512]{1,0:T(8,128)(2,1)S(1)}, bf16[64,512]{1,0:T(8,128)(2,1)S(1)}, u32[]{:S(2)}, u32[]{:S(2)}) collective-permute-start(bf16[64,512]{1,0:T(8,128)(2,1)S(1)} %get-tuple-element.25.m_ref), channel_id=1, source_target_pairs={{0,64},{16,80},{32,96},{48,112},{64,0},{80,16},{96,32},{112,48},{1... | collective-permute-start | bytes 196616 | tf_op jit(solution)/shard_map/ppermute | solution.py:54
  12.9 1.7 %collective-permute-done.6 = bf16[64,512]{1,0:T(8,128)(2,1)S(1)} collective-permute-done((bf16[64,512]{1,0:T(8,128)(2,1)S(1)}, bf16[64,512]{1,0:T(8,128)(2,1)S(1)}, u32[]{:S(2)}, u32[]{:S(2)}) %collective-permute-start.6) | collective-permute-done | bytes 65568 | tf_op jit(solution)/shard_map/ppermute | solution.py:54
  15.3 2.7 %collective-permute-start.9 = (bf16[128,512]{1,0:T(8,128)(2,1)}, bf16[128,512]{1,0:T(8,128)(2,1)}, u32[]{:S(2)}, u32[]{:S(2)}) collective-permute-start(bf16[128,512]{1,0:T(8,128)(2,1)} %pad_maximum_fusion.1), channel_id=1, source_target_pairs={{0,48},{16,32},{32,16},{48,0},{64,112},{80,96},{96,80},{112,64},{1... | collective-permute-start | bytes 393224 | tf_op jit(solution)/shard_map/ppermute | solution.py:54
  18.0 1.6 %flip.3 = bf16[64,7168]{1,0:T(8,128)(2,1)} custom-call(s32[2]{0:T(128)S(1)} %pad_add_fusion.idx_ref, bf16[128,7168]{1,0:T(8,128)(2,1)S(1)} %copy-done.3, s32[1,7168]{1,0:T(1,128)S(1)} %bitcast.29, bf16[64,7168]{1,0:T(8,128)(2,1)S(1)} %flip.2.rest_0_.own_ref), custom_call_target="tpu_custom_call" | custom-call | flops 458752 | bytes 1835008 | tf_op jit(solution)/shard_map/flip/pallas_call | solution.py:93
  19.7 2.4 %collective-permute-start = (bf16[64,7168]{1,0:T(8,128)(2,1)}, bf16[64,7168]{1,0:T(8,128)(2,1)S(1)}, u32[]{:S(2)}, u32[]{:S(2)}) collective-permute-start(bf16[64,7168]{1,0:T(8,128)(2,1)} %flip.3), channel_id=1, source_target_pairs={{0,1},{1,0},{2,3},{3,2},{4,5},{5,4},{6,7},{7,6},{8,9},{9,8},{10,11... | collective-permute-start | bytes 2752520 | tf_op jit(solution)/shard_map/ppermute | solution.py:49
  22.1 3.1 %copy-done = bf16[7168,512]{1,0:T(8,128)(2,1)S(1)} copy-done((bf16[7168,512]{1,0:T(8,128)(2,1)S(1)}, bf16[7168,512]{1,0:T(8,128)(2,1)}, u32[]{:S(2)}) %copy-start) | copy-done | bytes 7340056
  25.2 5.1 %back.1 = (bf16[64,7168]{1,0:T(8,128)(2,1)}, bf16[64,7168]{1,0:T(8,128)(2,1)}) custom-call(bf16[64,512]{1,0:T(8,128)(2,1)S(1)} %get-tuple-element.25.m_ref, bf16[64,512]{1,0:T(8,128)(2,1)S(1)} %get-tuple-element.39.p_ref, bf16[7168,512]{1,0:T(8,128)(2,1)S(1)} %copy-done, bf16[64,7168]{1,0:T(8,128)(2,1)S(1)} %flip.2.rest_0_.own_ref), custom_call_target="tpu_custom_call" | custom-call | flops 939524096 | bytes 9175040 | tf_op jit(solution)/shard_map/back/pallas_call | solution.py:156
  32.3 1.3 %collective-permute-start.7 = (bf16[128,512]{1,0:T(8,128)(2,1)}, bf16[128,512]{1,0:T(8,128)(2,1)S(1)}, u32[]{:S(2)}, u32[]{:S(2)}) collective-permute-start(bf16[128,512]{1,0:T(8,128)(2,1)} %pad_maximum_fusion.1), channel_id=1, source_target_pairs={{0,16},{16,0},{32,48},{48,32},{64,80},{80,64},{96,112},{112,96},{1... | collective-permute-start | bytes 393224 | tf_op jit(solution)/shard_map/ppermute | solution.py:54
  33.6 4.2 %collective-permute-done.7 = bf16[128,512]{1,0:T(8,128)(2,1)S(1)} collective-permute-done((bf16[128,512]{1,0:T(8,128)(2,1)}, bf16[128,512]{1,0:T(8,128)(2,1)S(1)}, u32[]{:S(2)}, u32[]{:S(2)}) %collective-permute-start.7) | collective-permute-done | bytes 131104 | tf_op jit(solution)/shard_map/ppermute | solution.py:54
  38.5 1.9 %pad_maximum_fusion.refs_0_ = bf16[512,512]{1,0:T(8,128)(2,1)} fusion(bf16[128,512]{1,0:T(8,128)(2,1)} %collective-permute-done.9, bf16[128,512]{1,0:T(8,128)(2,1)} %collective-permute-done.8, bf16[128,512]{1,0:T(8,128)(2,1)S(1)} %collective-permute-done.7, bf16[128,512]{1,0:T(8,128)(2,1)} %pad_maximum_fusion.1), kind=kLoop, calls=%fused_computation | loop fusion | flops 2097152 | bytes 1048576 | tf_op jit(solution)/shard_map/concatenate | solution.py:351
  40.4 1.2 collective-permute-start.11
  41.6 1.5 %collective-permute-start.13 = (bf16[512,512]{1,0:T(8,128)(2,1)}, bf16[512,512]{1,0:T(8,128)(2,1)}, u32[]{:S(2)}, u32[]{:S(2)}) collective-permute-start(bf16[512,512]{1,0:T(8,128)(2,1)} %pad_maximum_fusion.refs_0_), channel_id=1, source_target_pairs={{0,12},{4,0},{8,4},{12,8},{1,13},{5,1},{9,5},{13,9},{2,14},{6,2},{... | collective-permute-start | bytes 1572872 | tf_op jit(solution)/shard_map/ppermute | solution.py:59
  43.2 3.4 %collective-permute-done.2.diag_ref = bf16[64,7168]{1,0:T(8,128)(2,1)} collective-permute-done((bf16[64,7168]{1,0:T(8,128)(2,1)}, bf16[64,7168]{1,0:T(8,128)(2,1)}, u32[]{:S(2)}, u32[]{:S(2)}) %collective-permute-start.2) | collective-permute-done | bytes 917536 | tf_op jit(solution)/shard_map/ppermute | solution.py:54
  46.6 8.6 %turn.1 = (bf16[64,7168]{1,0:T(8,128)(2,1)}, bf16[64,7168]{1,0:T(8,128)(2,1)}, bf16[64,112,128]{2,1,0:T(8,128)(2,1)}, bf16[1024,896]{1,0:T(8,128)(2,1)}) custom-call(f32[2]{0:T(128)S(1)} %pad_maximum_fusion.2.sgn_ref, s32[1]{0:T(128)} %bitcast.2.core_ref, bf16[64,7168]{1,0:T(8,128)(2,1)S(1)} %flip.2.rest_0_.own_ref, ...), custom_call_target="tpu_custom_call" | custom-call | flops 1644167168 | bytes 9175040 | tf_op jit(solution)/shard_map/turn/pallas_call | solution.py:275
  55.5 11.7 %all-to-all-start = ((bf16[64,112,128]{2,1,0:T(8,128)(2,1)}), bf16[64,112,128]{2,1,0:T(8,128)(2,1)S(1)}, u32[]{:S(2)}, u32[]{:S(2)}) async-start(bf16[64,112,128]{2,1,0:T(8,128)(2,1)} %get-tuple-element.30), calls=%async_computation | async-start | bytes 3670016 | tf_op jit(solution)/shard_map/all_to_all | solution.py:407
  68.3 5.7 %turn_back.1 = (bf16[64,7168]{1,0:T(8,128)(2,1)}, bf16[64,7168]{1,0:T(8,128)(2,1)}) custom-call(bf16[1024,896]{1,0:T(8,128)(2,1)} %get-tuple-element.23.u_ref, bf16[896,896]{1,0:T(8,128)(2,1)} %constant.67.clone.table_ref), custom_call_target="tpu_custom_call" | custom-call | flops 1644167168 | bytes 3670016 | tf_op jit(solution)/shard_map/turn_back/pallas_call | solution.py:306
  74.0 1.3 %collective-permute-start.19 = (bf16[64,7168]{1,0:T(8,128)(2,1)}, bf16[64,7168]{1,0:T(8,128)(2,1)}, u32[]{:S(2)}, u32[]{:S(2)}) collective-permute-start(bf16[64,7168]{1,0:T(8,128)(2,1)} %get-tuple-element.24.refs_3_.own_ref), channel_id=1, source_target_pairs={{0,2},{2,0},{1,3},{3,1},{4,6},{6,4},{5,7},{7,5},{8,10},{10,8},{9,1... | collective-permute-start | bytes 2752520 | tf_op jit(solution)/shard_map/ppermute | solution.py:49
  75.3 2.9 %collective-permute-start.20 = (bf16[512,512]{1,0:T(8,128)(2,1)}, bf16[512,512]{1,0:T(8,128)(2,1)S(1)}, u32[]{:S(2)}, u32[]{:S(2)}) collective-permute-start(bf16[512,512]{1,0:T(8,128)(2,1)} %pad_maximum_fusion.refs_0_), channel_id=1, source_target_pairs={{0,8},{4,12},{8,0},{12,4},{1,9},{5,13},{9,1},{13,5},{2,10},{6,14},... | collective-permute-start | bytes 1572872 | tf_op jit(solution)/shard_map/ppermute | solution.py:59
  78.3 3.1 %copy-done.1 = bf16[7168,512]{1,0:T(8,128)(2,1)S(1)} copy-done((bf16[7168,512]{1,0:T(8,128)(2,1)S(1)}, bf16[7168,512]{1,0:T(8,128)(2,1)}, u32[]{:S(2)}) %copy-start.1) | copy-done | bytes 7340056
  81.3 1.2 copy-done.4
  82.5 5.4 %project.1 = bf16[128,512]{1,0:T(8,128)(2,1)S(1)} custom-call(bf16[64,7168]{1,0:T(8,128)(2,1)S(1)} %copy-done.9, bf16[64,7168]{1,0:T(8,128)(2,1)} %collective-permute-done.5.refs_1_, bf16[7168,512]{1,0:T(8,128)(2,1)S(1)} %copy-done.1, bf16[64,7168]{1,0:T(8,128)(2,1)S(1)} %copy-done.4, bf16[512,512]{1,0:T(8,128)(2,1)S(1)} %collective-permute-done.10.refs_4_, ...), custom_call_target="tpu_custom_call" | custom-call | flops 939524096 | bytes 7340032 | tf_op jit(solution)/shard_map/project/pallas_call | solution.py:191
  89.0 1.1 collective-permute-start.17
  90.1 7.2 %collective-permute-done.15 = bf16[2,32,512]{2,1,0:T(8,128)(2,1)S(1)} collective-permute-done((bf16[2,32,512]{2,1,0:T(8,128)(2,1)S(1)}, bf16[2,32,512]{2,1,0:T(8,128)(2,1)S(1)}, u32[]{:S(2)}, u32[]{:S(2)}) %collective-permute-start.15) | collective-permute-done | bytes 65568 | tf_op jit(solution)/shard_map/ppermute | solution.py:49
  97.3 2.3 %collective-permute-start.18 = (bf16[64,7168]{1,0:T(8,128)(2,1)}, bf16[64,7168]{1,0:T(8,128)(2,1)}, u32[]{:S(2)}, u32[]{:S(2)}) collective-permute-start(bf16[64,7168]{1,0:T(8,128)(2,1)} %get-tuple-element.28), channel_id=1, source_target_pairs={{0,3},{1,2},{2,1},{3,0},{4,7},{5,6},{6,5},{7,4},{8,11},{9,10},{10,... | collective-permute-start | bytes 2752520 | tf_op jit(solution)/shard_map/ppermute | solution.py:54
  102.2 3.0 %finish.2.rest_0_ = bf16[128,7168]{1,0:T(8,128)(2,1)} custom-call(s32[2]{0:T(128)S(1)} %pad_add_fusion.idx_ref, f32[1]{0:T(128)} %bitcast.1.sgn_ref, bf16[64,7168]{1,0:T(8,128)(2,1)S(1)} %copy-done.5, bf16[64,7168]{1,0:T(8,128)(2,1)} %collective-permute-done.19.other_ref, s32[1,7168]{1,0:T(1,128)S(1)} %bitcast.30), custom_call_target="tpu_custom_call" | custom-call | flops 917504 | bytes 2752512 | tf_op jit(solution)/shard_map/finish/pallas_call | solution.py:125
  105.8 5.2 %all-to-all-done.r_ref = bf16[64,112,128]{2,1,0:T(8,128)(2,1)S(1)} async-done(((bf16[64,112,128]{2,1,0:T(8,128)(2,1)}), bf16[64,112,128]{2,1,0:T(8,128)(2,1)S(1)}, u32[]{:S(2)}, u32[]{:S(2)}) %all-to-all-start) | async-done | bytes 1835040 | tf_op jit(solution)/shard_map/all_to_all | solution.py:407
  111.6 3.3 %weight_grad.1 = f32[224,512]{1,0:T(8,128)S(1)} custom-call(s32[64]{0:T(128)S(1)} %add.90.at_ref, bf16[64,112,128]{2,1,0:T(8,128)(2,1)S(1)} %all-to-all-done.r_ref, bf16[512,512]{1,0:T(8,128)(2,1)} %pad_maximum_fusion.refs_0_, bf16[512,512]{1,0:T(8,128)(2,1)} %collective-permute-done.11.refs_1_, bf16[512,512]{1,0:T(8,128)(2,1)} %copy-done.12, ...), custom_call_target="tpu_custom_call" | custom-call | flops 939524096 | bytes 6029312 | tf_op jit(solution)/shard_map/weight_grad/pallas_call | solution.py:337
  114.9 3.0 %collective-permute-start.25 = (bf16[112,512]{1,0:T(8,128)(2,1)S(1)}, bf16[112,512]{1,0:T(8,128)(2,1)S(1)}, u32[]{:S(2)}, u32[]{:S(2)}) collective-permute-start(bf16[112,512]{1,0:T(8,128)(2,1)S(1)} %fusion.1), channel_id=1, source_target_pairs={{0,128},{128,0},{1,129},{129,1},{2,130},{130,2},{3,131},{131,3},{4... | collective-permute-start | bytes 344072 | tf_op jit(solution)/shard_map/ppermute | solution.py:49
  118.5 2.3 %collective-permute-done.18.other_ref = bf16[64,7168]{1,0:T(8,128)(2,1)} collective-permute-done((bf16[64,7168]{1,0:T(8,128)(2,1)}, bf16[64,7168]{1,0:T(8,128)(2,1)}, u32[]{:S(2)}, u32[]{:S(2)}) %collective-permute-start.18) | collective-permute-done | bytes 917536 | tf_op jit(solution)/shard_map/ppermute | solution.py:54
  120.8 3.3 %finish.3 = bf16[128,7168]{1,0:T(8,128)(2,1)} custom-call(s32[2]{0:T(128)S(1)} %pad_add_fusion.idx_ref, f32[1]{0:T(128)} %bitcast.1.sgn_ref, bf16[64,7168]{1,0:T(8,128)(2,1)} %collective-permute-done.17.own_ref, bf16[64,7168]{1,0:T(8,128)(2,1)} %collective-permute-done.18.other_ref, s32[1,7168]{1,0:T(1,128)S(1)} %bitcast.31, ...), custom_call_target="tpu_custom_call", output_to_operand_aliasing={{}: (5, {})} | custom-call | flops 917504 | bytes 2752512 | tf_op jit(solution)/shard_map/finish/pallas_call | solution.py:125
  (89 shorter events, 13.8 us)
Async XLA Ops:
  3.0 15.1 %copy-start.3 = (bf16[128,7168]{1,0:T(8,128)(2,1)S(1)}, bf16[128,7168]{1,0:T(8,128)(2,1)}, u32[]{:S(2)}) copy-start(bf16[128,7168]{1,0:T(8,128)(2,1)} %h_ref.3) | copy-start | bytes 5505028
  3.0 15.1 %copy-start.11 = (s32[7168]{0:T(1024)S(1)}, s32[7168]{0:T(1024)}, u32[]{:S(2)}) copy-start(s32[7168]{0:T(1024)} %param.8) | copy-start | bytes 86020
  3.7 36.7 %collective-permute-start.1 = (bf16[64,7168]{1,0:T(8,128)(2,1)S(1)}, bf16[64,7168]{1,0:T(8,128)(2,1)}, u32[]{:S(2)}, u32[]{:S(2)}) collective-permute-start(bf16[64,7168]{1,0:T(8,128)(2,1)S(1)} %flip.2.rest_0_.own_ref), channel_id=1, source_target_pairs={{0,2},{2,0},{1,3},{3,1},{4,6},{6,4},{5,7},{7,5},{8,10},{10,8},{9,1... | collective-permute-start | bytes 2752520 | tf_op jit(solution)/shard_map/ppermute | solution.py:49
  5.9 8.7 %collective-permute-start.6 = (bf16[64,512]{1,0:T(8,128)(2,1)S(1)}, bf16[64,512]{1,0:T(8,128)(2,1)S(1)}, u32[]{:S(2)}, u32[]{:S(2)}) collective-permute-start(bf16[64,512]{1,0:T(8,128)(2,1)S(1)} %get-tuple-element.25.m_ref), channel_id=1, source_target_pairs={{0,64},{16,80},{32,96},{48,112},{64,0},{80,16},{96,32},{112,48},{1... | collective-permute-start | bytes 196616 | tf_op jit(solution)/shard_map/ppermute | solution.py:54
  15.3 15.0 %collective-permute-start.9 = (bf16[128,512]{1,0:T(8,128)(2,1)}, bf16[128,512]{1,0:T(8,128)(2,1)}, u32[]{:S(2)}, u32[]{:S(2)}) collective-permute-start(bf16[128,512]{1,0:T(8,128)(2,1)} %pad_maximum_fusion.1), channel_id=1, source_target_pairs={{0,48},{16,32},{32,16},{48,0},{64,112},{80,96},{96,80},{112,64},{1... | collective-permute-start | bytes 393224 | tf_op jit(solution)/shard_map/ppermute | solution.py:54
  19.7 23.6 %collective-permute-start = (bf16[64,7168]{1,0:T(8,128)(2,1)}, bf16[64,7168]{1,0:T(8,128)(2,1)S(1)}, u32[]{:S(2)}, u32[]{:S(2)}) collective-permute-start(bf16[64,7168]{1,0:T(8,128)(2,1)} %flip.3), channel_id=1, source_target_pairs={{0,1},{1,0},{2,3},{3,2},{4,5},{5,4},{6,7},{7,6},{8,9},{9,8},{10,11... | collective-permute-start | bytes 2752520 | tf_op jit(solution)/shard_map/ppermute | solution.py:49
  22.0 24.5 %collective-permute-start.2 = (bf16[64,7168]{1,0:T(8,128)(2,1)}, bf16[64,7168]{1,0:T(8,128)(2,1)}, u32[]{:S(2)}, u32[]{:S(2)}) collective-permute-start(bf16[64,7168]{1,0:T(8,128)(2,1)} %flip.3), channel_id=1, source_target_pairs={{0,3},{1,2},{2,1},{3,0},{4,7},{5,6},{6,5},{7,4},{8,11},{9,10},{10,... | collective-permute-start | bytes 2752520 | tf_op jit(solution)/shard_map/ppermute | solution.py:54
  22.1 10.2 %collective-permute-start.8 = (bf16[128,512]{1,0:T(8,128)(2,1)}, bf16[128,512]{1,0:T(8,128)(2,1)}, u32[]{:S(2)}, u32[]{:S(2)}) collective-permute-start(bf16[128,512]{1,0:T(8,128)(2,1)} %pad_maximum_fusion.1), channel_id=1, source_target_pairs={{0,32},{16,48},{32,0},{48,16},{64,96},{80,112},{96,64},{112,80},{1... | collective-permute-start | bytes 393224 | tf_op jit(solution)/shard_map/ppermute | solution.py:54
  25.2 21.4 %copy-start.8 = (bf16[896,896]{1,0:T(8,128)(2,1)S(1)}, bf16[896,896]{1,0:T(8,128)(2,1)}, u32[]{:S(2)}) copy-start(bf16[896,896]{1,0:T(8,128)(2,1)} %constant.67.clone.table_ref) | copy-start | bytes 4816900
  30.3 16.3 %collective-permute-start.4 = (bf16[64,7168]{1,0:T(8,128)(2,1)}, bf16[64,7168]{1,0:T(8,128)(2,1)}, u32[]{:S(2)}, u32[]{:S(2)}) collective-permute-start(bf16[64,7168]{1,0:T(8,128)(2,1)} %get-tuple-element.20), channel_id=1, source_target_pairs={{0,1},{1,0},{2,3},{3,2},{4,5},{5,4},{6,7},{7,6},{8,9},{9,8},{10,11... | collective-permute-start | bytes 2752520 | tf_op jit(solution)/shard_map/ppermute | solution.py:49
  32.3 5.5 %collective-permute-start.7 = (bf16[128,512]{1,0:T(8,128)(2,1)}, bf16[128,512]{1,0:T(8,128)(2,1)S(1)}, u32[]{:S(2)}, u32[]{:S(2)}) collective-permute-start(bf16[128,512]{1,0:T(8,128)(2,1)} %pad_maximum_fusion.1), channel_id=1, source_target_pairs={{0,16},{16,0},{32,48},{48,32},{64,80},{80,64},{96,112},{112,96},{1... | collective-permute-start | bytes 393224 | tf_op jit(solution)/shard_map/ppermute | solution.py:54
  37.8 3.8 %collective-permute-start.3 = (f32[64,56]{1,0:T(8,128)S(1)}, f32[64,56]{1,0:T(8,128)S(1)}, u32[]{:S(2)}, u32[]{:S(2)}) collective-permute-start(f32[64,56]{1,0:T(8,128)S(1)} %get-tuple-element.41), channel_id=1, source_target_pairs={{0,1},{1,0},{2,3},{3,2},{4,5},{5,4},{6,7},{7,6},{8,9},{9,8},{10,11... | collective-permute-start | bytes 43016 | tf_op jit(solution)/shard_map/ppermute | solution.py:49
  40.4 15.1 %collective-permute-start.11 = (bf16[512,512]{1,0:T(8,128)(2,1)}, bf16[512,512]{1,0:T(8,128)(2,1)}, u32[]{:S(2)}, u32[]{:S(2)}) collective-permute-start(bf16[512,512]{1,0:T(8,128)(2,1)} %pad_maximum_fusion.refs_0_), channel_id=1, source_target_pairs={{0,4},{4,8},{8,12},{12,0},{1,5},{5,9},{9,13},{13,1},{2,6},{6,10},{... | collective-permute-start | bytes 1572872 | tf_op jit(solution)/shard_map/ppermute | solution.py:59
  41.6 13.9 %collective-permute-start.13 = (bf16[512,512]{1,0:T(8,128)(2,1)}, bf16[512,512]{1,0:T(8,128)(2,1)}, u32[]{:S(2)}, u32[]{:S(2)}) collective-permute-start(bf16[512,512]{1,0:T(8,128)(2,1)} %pad_maximum_fusion.refs_0_), channel_id=1, source_target_pairs={{0,12},{4,0},{8,4},{12,8},{1,13},{5,1},{9,5},{13,9},{2,14},{6,2},{... | collective-permute-start | bytes 1572872 | tf_op jit(solution)/shard_map/ppermute | solution.py:59
  55.5 12.8 %copy-start.17 = (s32[8]{0:T(128)S(1)}, s32[8]{0:T(128)}, u32[]{:S(2)}) copy-start(s32[8]{0:T(128)} %constant.68.clone) | copy-start | bytes 100
  55.5 55.5 %all-to-all-start = ((bf16[64,112,128]{2,1,0:T(8,128)(2,1)}), bf16[64,112,128]{2,1,0:T(8,128)(2,1)S(1)}, u32[]{:S(2)}, u32[]{:S(2)}) async-start(bf16[64,112,128]{2,1,0:T(8,128)(2,1)} %get-tuple-element.30), calls=%async_computation | async-start | bytes 3670016 | tf_op jit(solution)/shard_map/all_to_all | solution.py:407
  67.1 11.1 %collective-permute-start.5 = (bf16[64,7168]{1,0:T(8,128)(2,1)}, bf16[64,7168]{1,0:T(8,128)(2,1)}, u32[]{:S(2)}, u32[]{:S(2)}) collective-permute-start(bf16[64,7168]{1,0:T(8,128)(2,1)} %get-tuple-element.22), channel_id=1, source_target_pairs={{0,1},{1,0},{2,3},{3,2},{4,5},{5,4},{6,7},{7,6},{8,9},{9,8},{10,11... | collective-permute-start | bytes 2752520 | tf_op jit(solution)/shard_map/ppermute | solution.py:49
  67.6 7.7 %collective-permute-start.10 = (bf16[512,512]{1,0:T(8,128)(2,1)}, bf16[512,512]{1,0:T(8,128)(2,1)S(1)}, u32[]{:S(2)}, u32[]{:S(2)}) collective-permute-start(bf16[512,512]{1,0:T(8,128)(2,1)} %pad_maximum_fusion.refs_0_), channel_id=1, source_target_pairs={{0,1},{1,0},{2,3},{3,2},{4,5},{5,4},{6,7},{7,6},{8,9},{9,8},{10,11... | collective-permute-start | bytes 1572872 | tf_op jit(solution)/shard_map/ppermute | solution.py:49
  67.7 10.5 %collective-permute-start.12 = (bf16[512,512]{1,0:T(8,128)(2,1)}, bf16[512,512]{1,0:T(8,128)(2,1)S(1)}, u32[]{:S(2)}, u32[]{:S(2)}) collective-permute-start(bf16[512,512]{1,0:T(8,128)(2,1)} %collective-permute-done.11.refs_1_), channel_id=1, source_target_pairs={{0,1},{1,0},{2,3},{3,2},{4,5},{5,4},{6,7},{7,6},{8,9},{9,8},{10,11... | collective-permute-start | bytes 1572872 | tf_op jit(solution)/shard_map/ppermute | solution.py:49
  68.1 10.1 %collective-permute-start.14 = (bf16[512,512]{1,0:T(8,128)(2,1)}, bf16[512,512]{1,0:T(8,128)(2,1)}, u32[]{:S(2)}, u32[]{:S(2)}) collective-permute-start(bf16[512,512]{1,0:T(8,128)(2,1)} %collective-permute-done.13.refs_3_), channel_id=1, source_target_pairs={{0,1},{1,0},{2,3},{3,2},{4,5},{5,4},{6,7},{7,6},{8,9},{9,8},{10,11... | collective-permute-start | bytes 1572872 | tf_op jit(solution)/shard_map/ppermute | solution.py:49
  74.0 28.2 %collective-permute-start.19 = (bf16[64,7168]{1,0:T(8,128)(2,1)}, bf16[64,7168]{1,0:T(8,128)(2,1)}, u32[]{:S(2)}, u32[]{:S(2)}) collective-permute-start(bf16[64,7168]{1,0:T(8,128)(2,1)} %get-tuple-element.24.refs_3_.own_ref), channel_id=1, source_target_pairs={{0,2},{2,0},{1,3},{3,1},{4,6},{6,4},{5,7},{7,5},{8,10},{10,8},{9,1... | collective-permute-start | bytes 2752520 | tf_op jit(solution)/shard_map/ppermute | solution.py:49
  75.3 24.9 %collective-permute-start.20 = (bf16[512,512]{1,0:T(8,128)(2,1)}, bf16[512,512]{1,0:T(8,128)(2,1)S(1)}, u32[]{:S(2)}, u32[]{:S(2)}) collective-permute-start(bf16[512,512]{1,0:T(8,128)(2,1)} %pad_maximum_fusion.refs_0_), channel_id=1, source_target_pairs={{0,8},{4,12},{8,0},{12,4},{1,9},{5,13},{9,1},{13,5},{2,10},{6,14},... | collective-permute-start | bytes 1572872 | tf_op jit(solution)/shard_map/ppermute | solution.py:59
  88.7 13.4 %copy-start.5 = (bf16[64,7168]{1,0:T(8,128)(2,1)S(1)}, bf16[64,7168]{1,0:T(8,128)(2,1)}, u32[]{:S(2)}) copy-start(bf16[64,7168]{1,0:T(8,128)(2,1)} %get-tuple-element.24.refs_3_.own_ref) | copy-start | bytes 2752516
  88.7 8.5 %collective-permute-start.15 = (bf16[2,32,512]{2,1,0:T(8,128)(2,1)S(1)}, bf16[2,32,512]{2,1,0:T(8,128)(2,1)S(1)}, u32[]{:S(2)}, u32[]{:S(2)}) collective-permute-start(bf16[2,32,512]{2,1,0:T(8,128)(2,1)S(1)} %dynamic-slice_bitcast_fusion), channel_id=1, source_target_pairs={{0,2},{2,0},{1,3},{3,1},{4,6},{6,4},{5,7},{7,5},{8,10},{10,8},{9,1... | collective-permute-start | bytes 196616 | tf_op jit(solution)/shard_map/ppermute | solution.py:49
  89.0 31.8 %collective-permute-start.17 = (bf16[64,7168]{1,0:T(8,128)(2,1)}, bf16[64,7168]{1,0:T(8,128)(2,1)}, u32[]{:S(2)}, u32[]{:S(2)}) collective-permute-start(bf16[64,7168]{1,0:T(8,128)(2,1)} %get-tuple-element.28), channel_id=1, source_target_pairs={{0,1},{1,0},{2,3},{3,2},{4,5},{5,4},{6,7},{7,6},{8,9},{9,8},{10,11... | collective-permute-start | bytes 2752520 | tf_op jit(solution)/shard_map/ppermute | solution.py:49
  97.3 23.5 %collective-permute-start.18 = (bf16[64,7168]{1,0:T(8,128)(2,1)}, bf16[64,7168]{1,0:T(8,128)(2,1)}, u32[]{:S(2)}, u32[]{:S(2)}) collective-permute-start(bf16[64,7168]{1,0:T(8,128)(2,1)} %get-tuple-element.28), channel_id=1, source_target_pairs={{0,3},{1,2},{2,1},{3,0},{4,7},{5,6},{6,5},{7,4},{8,11},{9,10},{10,... | collective-permute-start | bytes 2752520 | tf_op jit(solution)/shard_map/ppermute | solution.py:54
  101.1 4.6 %collective-permute-start.21 = (bf16[128,512]{1,0:T(8,128)(2,1)S(1)}, bf16[128,512]{1,0:T(8,128)(2,1)S(1)}, u32[]{:S(2)}, u32[]{:S(2)}) collective-permute-start(bf16[128,512]{1,0:T(8,128)(2,1)S(1)} %get-tuple-element.38), channel_id=1, source_target_pairs={{0,1},{1,0},{2,3},{3,2},{4,5},{5,4},{6,7},{7,6},{8,9},{9,8},{10,11... | collective-permute-start | bytes 393224 | tf_op jit(solution)/shard_map/ppermute | solution.py:49
  105.2 5.8 %collective-permute-start.22 = (bf16[128,512]{1,0:T(8,128)(2,1)}, bf16[128,512]{1,0:T(8,128)(2,1)S(1)}, u32[]{:S(2)}, u32[]{:S(2)}) collective-permute-start(bf16[128,512]{1,0:T(8,128)(2,1)} %get-tuple-element.37), channel_id=1, source_target_pairs={{0,1},{1,0},{2,3},{3,2},{4,5},{5,4},{6,7},{7,6},{8,9},{9,8},{10,11... | collective-permute-start | bytes 393224 | tf_op jit(solution)/shard_map/ppermute | solution.py:49
  105.3 6.3 %collective-permute-start.23 = (bf16[128,512]{1,0:T(8,128)(2,1)}, bf16[128,512]{1,0:T(8,128)(2,1)S(1)}, u32[]{:S(2)}, u32[]{:S(2)}) collective-permute-start(bf16[128,512]{1,0:T(8,128)(2,1)} %get-tuple-element.36), channel_id=1, source_target_pairs={{0,1},{1,0},{2,3},{3,2},{4,5},{5,4},{6,7},{7,6},{8,9},{9,8},{10,11... | collective-permute-start | bytes 393224 | tf_op jit(solution)/shard_map/ppermute | solution.py:49
  105.7 5.9 %collective-permute-start.24 = (bf16[128,512]{1,0:T(8,128)(2,1)}, bf16[128,512]{1,0:T(8,128)(2,1)S(1)}, u32[]{:S(2)}, u32[]{:S(2)}) collective-permute-start(bf16[128,512]{1,0:T(8,128)(2,1)} %get-tuple-element.35), channel_id=1, source_target_pairs={{0,1},{1,0},{2,3},{3,2},{4,5},{5,4},{6,7},{7,6},{8,9},{9,8},{10,11... | collective-permute-start | bytes 393224 | tf_op jit(solution)/shard_map/ppermute | solution.py:49
  111.0 6.9 %collective-permute-start.16 = (bf16[32,512]{1,0:T(8,128)(2,1)S(1)}, bf16[32,512]{1,0:T(8,128)(2,1)S(1)}, u32[]{:S(2)}, u32[]{:S(2)}) collective-permute-start(bf16[32,512]{1,0:T(8,128)(2,1)S(1)} %fusion.3), channel_id=1, source_target_pairs={{0,1},{1,0},{2,3},{3,2},{4,5},{5,4},{6,7},{7,6},{8,9},{9,8},{10,11... | collective-permute-start | bytes 98312 | tf_op jit(solution)/shard_map/ppermute | solution.py:49
  114.9 10.1 %collective-permute-start.25 = (bf16[112,512]{1,0:T(8,128)(2,1)S(1)}, bf16[112,512]{1,0:T(8,128)(2,1)S(1)}, u32[]{:S(2)}, u32[]{:S(2)}) collective-permute-start(bf16[112,512]{1,0:T(8,128)(2,1)S(1)} %fusion.1), channel_id=1, source_target_pairs={{0,128},{128,0},{1,129},{129,1},{2,130},{130,2},{3,131},{131,3},{4... | collective-permute-start | bytes 344072 | tf_op jit(solution)/shard_map/ppermute | solution.py:49
  (13 other events, 50.8 us)

commit v6 on v5

--- a/solution.py
+++ b/solution.py
@@ -407,33 +407,35 @@
     got = lax.all_to_all(after(qt, pieces[1], pieces[3]), ("core", "z", "x"), 0, 0, tiled=True)
     v_here, v_there = turn_back(grads, table, half, ff_local, norm)
     pieces[2] = shift(after(ring, v_here), "x", 2)
-    cross, ncross = swap(v_here, "yl"), swap(v_there, "core")
+    cross, dcross, ncross = swap(v_here, "yl"), diagonal(v_there), swap(v_there, "core")
     early = [swap(pieces[i], "core") for i in (0, 1, 3)]
 
     out_all = project((q_here, swap(q_there, "core")), down_weight, after=(v_here, *early)).reshape(2, 2, quarter, d_out)
-    give = lax.dynamic_index_in_dim(out_all, 1 - (yl ^ core), 0, keepdims=False)
-    across = swap(give, "yl")
-    dcross = diagonal(after(v_there, across))
-
+
+    def share(y, c):
+        tokens = lax.dynamic_index_in_dim(out_all, y ^ core, 0, keepdims=False)
+        return lax.dynamic_index_in_dim(tokens, c, 0, keepdims=False)
+
+    given = [swap(share(1 - yl, core), "yl"), swap(share(yl, 1 - core), "core"), diagonal(share(1 - yl, 1 - core))]
     grad_hidden = finish(idx, 0, sgn_y, v_here, cross, sign_bits)
 
-    gated = after(pieces[2], across)
+    gated = after(pieces[2], out_all)
     quads = gated.shape[0] // 4
     late = [swap(gated[i * quads : (i + 1) * quads], "core") for i in range(4)]
     acc = weight_grad(source_places(), after(got, grad_hidden), pieces + [early[0], early[1], *late, early[2]], half)
 
     grad_hidden = finish(idx, 1, sgn_y, ncross, after(dcross, acc), sign_bits, into=grad_hidden)
 
-    keep = lax.dynamic_index_in_dim(out_all, yl ^ core, 0, keepdims=False)
-    summed = keep.astype(jnp.float32) + across.astype(jnp.float32)
-    keep = lax.dynamic_index_in_dim(summed, core, 0, keepdims=False)
-    give = lax.dynamic_index_in_dim(summed, 1 - core, 0, keepdims=False).astype(jnp.bfloat16)
-    output = (keep + swap(give, "core").astype(jnp.float32)).astype(jnp.bfloat16)
-
     acc = acc.reshape(2, -1, d_out)
     keep = lax.dynamic_index_in_dim(acc, yh, 0, keepdims=False)
     give = lax.dynamic_index_in_dim(acc, 1 - yh, 0, keepdims=False).astype(jnp.bfloat16)
-    grad_weight = (keep + swap(give, "yh").astype(jnp.float32)) * (1.0 / math.sqrt(tok_count * n_data))
+    taken = swap(give, "yh")
+    grad_weight = (keep + taken.astype(jnp.float32)) * (1.0 / math.sqrt(tok_count * n_data))
+
+    output = share(yl, core).astype(jnp.float32)
+    for other in given:
+        output = output + after(other, taken, grad_hidden).astype(jnp.float32)
+    output = output.astype(jnp.bfloat16)
     return (output, grad_hidden, grad_weight)
 
 

time: 126 us -> 126 us (level)
  waiting for transfers between devices: 25.9 us -> 20.8 us
  local copies, waits for them, and re-layouts: 12.3 us -> 15.6 us
    ppermute x17, waiting for transfers between devices: 8.17 us -> 0.42 us  [swap(): return lax.ppermute(value, axis, [(0, 1), (1, 0)])]
    ppermute x3, waiting for transfers between devices: 0.96 us -> 6.22 us  [shift(): lax.ppermute(value, axis, [(i, (i + by) % size) for i in range(size)])]
    ppermute x6 -> x7, waiting for transfers between devices: 11.6 us -> 8.8 us  [xor(): return lax.ppermute(value, axes, [(i, i ^ by) for i in range(size)])]
    unnamed x36 -> x34, local copies, waits for them, and re-layouts: 10.4 us -> 12.7 us
    ppermute x17, starting transfers between devices: 14.7 us -> 16.8 us  [swap(): return lax.ppermute(value, axis, [(0, 1), (1, 0)])]
    ppermute x6 -> x7, starting transfers between devices: 13.3 us -> 12.3 us  [xor(): return lax.ppermute(value, axes, [(i, i ^ by) for i in range(size)])]
  transfers between devices with their start and end apart: 27 -> 28, of which waited for: 9 -> 8; matrix products, arithmetic and copies ran while one was open for 5% -> 5% of each run, Pallas kernels for 29% -> 29%
where the time goes in v6:
time: 126 us; the launch traced here: 125 us
  starting transfers between devices  46.2 us (37%)
  Pallas kernels  36.6 us (29%)
  waiting for transfers between devices  20.8 us (17%)
  local copies, waits for them, and re-layouts  15.6 us (12%)
  other arithmetic  4.82 us (4%)
    ppermute x17, starting transfers between devices, swap(): return lax.ppermute(value, axis, [(0, 1), (1, 0)])  16.8 us
    unnamed x34, local copies, waits for them, and re-layouts  12.7 us
    ppermute x7, starting transfers between devices, xor(): return lax.ppermute(value, axes, [(i, i ^ by) for i in range(size)])  12.3 us
    all_to_all x1, starting transfers between devices, local(): lax.all_to_all(after(qt, pieces[1], pieces[3]), ('core', 'z', 'x'), 0, 0,...  11.5 us
    ppermute x7, waiting for transfers between devices, xor(): return lax.ppermute(value, axes, [(i, i ^ by) for i in range(size)])  8.8 us
    pallas_call x1, Pallas kernels, turn(): pl.pallas_call(functools.partial(turn_kernel, nblk, norm), out_shape=(fla...  8.52 us
    pallas_call x2, Pallas kernels, finish(): pl.pallas_call(finish_kernel, grid_spec=pltpu.PrefetchScalarGridSpec(num_...  6.25 us
    ppermute x3, waiting for transfers between devices, shift(): lax.ppermute(value, axis, [(i, (i + by) % size) for i in range(size)])  6.22 us
  transfers between devices with their start and end apart: 28, of which 8 were waited for; matrix products, arithmetic and copies ran while one was open for 5% of the time, Pallas kernels for 29%

profile of v6, /device:TPU:1, one launch (start us, length us, event | category | flops | bytes accessed | tf_op | source)
XLA Modules:
  0.0 124.7 jit_solution(10015216776419887475)
XLA Ops:
  0.7 1.5 %copy-done.2 = bf16[128,7168]{1,0:T(8,128)(2,1)S(1)} copy-done((bf16[128,7168]{1,0:T(8,128)(2,1)S(1)}, bf16[128,7168]{1,0:T(8,128)(2,1)}, u32[]{:S(2)}) %copy-start.2) | copy-done | bytes 1835032
  3.7 2.2 %collective-permute-start.1 = (bf16[64,7168]{1,0:T(8,128)(2,1)S(1)}, bf16[64,7168]{1,0:T(8,128)(2,1)}, u32[]{:S(2)}, u32[]{:S(2)}) collective-permute-start(bf16[64,7168]{1,0:T(8,128)(2,1)S(1)} %flip.2.rest_0_.own_ref), channel_id=1, source_target_pairs={{0,2},{2,0},{1,3},{3,1},{4,6},{6,4},{5,7},{7,5},{8,10},{10,8},{9,1... | collective-permute-start | bytes 2752520 | tf_op jit(solution)/shard_map/ppermute | solution.py:49
  5.9 7.0 %collective-permute-start.6 = (bf16[64,512]{1,0:T(8,128)(2,1)S(1)}, bf16[64,512]{1,0:T(8,128)(2,1)S(1)}, u32[]{:S(2)}, u32[]{:S(2)}) collective-permute-start(bf16[64,512]{1,0:T(8,128)(2,1)S(1)} %get-tuple-element.27.m_ref), channel_id=1, source_target_pairs={{0,64},{16,80},{32,96},{48,112},{64,0},{80,16},{96,32},{112,48},{1... | collective-permute-start | bytes 196616 | tf_op jit(solution)/shard_map/ppermute | solution.py:54
  12.9 1.7 %collective-permute-done.6 = bf16[64,512]{1,0:T(8,128)(2,1)S(1)} collective-permute-done((bf16[64,512]{1,0:T(8,128)(2,1)S(1)}, bf16[64,512]{1,0:T(8,128)(2,1)S(1)}, u32[]{:S(2)}, u32[]{:S(2)}) %collective-permute-start.6) | collective-permute-done | bytes 65568 | tf_op jit(solution)/shard_map/ppermute | solution.py:54
  15.3 2.7 %collective-permute-start.9 = (bf16[128,512]{1,0:T(8,128)(2,1)}, bf16[128,512]{1,0:T(8,128)(2,1)S(1)}, u32[]{:S(2)}, u32[]{:S(2)}) collective-permute-start(bf16[128,512]{1,0:T(8,128)(2,1)} %pad_maximum_fusion.1), channel_id=1, source_target_pairs={{0,48},{16,32},{32,16},{48,0},{64,112},{80,96},{96,80},{112,64},{1... | collective-permute-start | bytes 393224 | tf_op jit(solution)/shard_map/ppermute | solution.py:54
  18.0 1.6 %flip.3 = bf16[64,7168]{1,0:T(8,128)(2,1)} custom-call(s32[2]{0:T(128)S(1)} %pad_add_fusion.idx_ref, bf16[128,7168]{1,0:T(8,128)(2,1)S(1)} %copy-done.3, s32[1,7168]{1,0:T(1,128)S(1)} %bitcast.27, bf16[64,7168]{1,0:T(8,128)(2,1)S(1)} %flip.2.rest_0_.own_ref), custom_call_target="tpu_custom_call" | custom-call | flops 458752 | bytes 1835008 | tf_op jit(solution)/shard_map/flip/pallas_call | solution.py:93
  19.7 2.4 %collective-permute-start = (bf16[64,7168]{1,0:T(8,128)(2,1)}, bf16[64,7168]{1,0:T(8,128)(2,1)S(1)}, u32[]{:S(2)}, u32[]{:S(2)}) collective-permute-start(bf16[64,7168]{1,0:T(8,128)(2,1)} %flip.3), channel_id=1, source_target_pairs={{0,1},{1,0},{2,3},{3,2},{4,5},{5,4},{6,7},{7,6},{8,9},{9,8},{10,11... | collective-permute-start | bytes 2752520 | tf_op jit(solution)/shard_map/ppermute | solution.py:49
  22.1 3.1 %copy-done = bf16[7168,512]{1,0:T(8,128)(2,1)S(1)} copy-done((bf16[7168,512]{1,0:T(8,128)(2,1)S(1)}, bf16[7168,512]{1,0:T(8,128)(2,1)}, u32[]{:S(2)}) %copy-start) | copy-done | bytes 7340056
  25.2 5.1 %back.1 = (bf16[64,7168]{1,0:T(8,128)(2,1)}, bf16[64,7168]{1,0:T(8,128)(2,1)}) custom-call(bf16[64,512]{1,0:T(8,128)(2,1)S(1)} %get-tuple-element.27.m_ref, bf16[64,512]{1,0:T(8,128)(2,1)S(1)} %get-tuple-element.46.p_ref, bf16[7168,512]{1,0:T(8,128)(2,1)S(1)} %copy-done, bf16[64,7168]{1,0:T(8,128)(2,1)S(1)} %flip.2.rest_0_.own_ref), custom_call_target="tpu_custom_call" | custom-call | flops 939524096 | bytes 9175040 | tf_op jit(solution)/shard_map/back/pallas_call | solution.py:156
  33.6 3.7 %collective-permute-done.7 = bf16[128,512]{1,0:T(8,128)(2,1)S(1)} collective-permute-done((bf16[128,512]{1,0:T(8,128)(2,1)}, bf16[128,512]{1,0:T(8,128)(2,1)S(1)}, u32[]{:S(2)}, u32[]{:S(2)}) %collective-permute-start.7) | collective-permute-done | bytes 131104 | tf_op jit(solution)/shard_map/ppermute | solution.py:54
  37.3 1.3 %collective-permute-start.3 = (f32[64,56]{1,0:T(8,128)S(1)}, f32[64,56]{1,0:T(8,128)S(1)}, u32[]{:S(2)}, u32[]{:S(2)}) collective-permute-start(f32[64,56]{1,0:T(8,128)S(1)} %get-tuple-element.48), channel_id=1, source_target_pairs={{0,1},{1,0},{2,3},{3,2},{4,5},{5,4},{6,7},{7,6},{8,9},{9,8},{10,11... | collective-permute-start | bytes 43016 | tf_op jit(solution)/shard_map/ppermute | solution.py:49
  38.6 1.9 %pad_maximum_fusion.refs_0_ = bf16[512,512]{1,0:T(8,128)(2,1)} fusion(bf16[128,512]{1,0:T(8,128)(2,1)} %copy-done.14, bf16[128,512]{1,0:T(8,128)(2,1)} %collective-permute-done.8, bf16[128,512]{1,0:T(8,128)(2,1)S(1)} %collective-permute-done.7, bf16[128,512]{1,0:T(8,128)(2,1)} %pad_maximum_fusion.1), kind=kLoop, calls=%fused_computation | loop fusion | flops 2097152 | bytes 1048576 | tf_op jit(solution)/shard_map/concatenate | solution.py:351
  40.5 1.2 collective-permute-start.11
  41.7 1.5 %collective-permute-start.13 = (bf16[512,512]{1,0:T(8,128)(2,1)}, bf16[512,512]{1,0:T(8,128)(2,1)}, u32[]{:S(2)}, u32[]{:S(2)}) collective-permute-start(bf16[512,512]{1,0:T(8,128)(2,1)} %pad_maximum_fusion.refs_0_), channel_id=1, source_target_pairs={{0,12},{4,0},{8,4},{12,8},{1,13},{5,1},{9,5},{13,9},{2,14},{6,2},{... | collective-permute-start | bytes 1572872 | tf_op jit(solution)/shard_map/ppermute | solution.py:59
  43.3 3.3 %collective-permute-done.2.diag_ref = bf16[64,7168]{1,0:T(8,128)(2,1)} collective-permute-done((bf16[64,7168]{1,0:T(8,128)(2,1)}, bf16[64,7168]{1,0:T(8,128)(2,1)}, u32[]{:S(2)}, u32[]{:S(2)}) %collective-permute-start.2) | collective-permute-done | bytes 917536 | tf_op jit(solution)/shard_map/ppermute | solution.py:54
  46.6 8.5 %turn.1 = (bf16[64,7168]{1,0:T(8,128)(2,1)}, bf16[64,7168]{1,0:T(8,128)(2,1)}, bf16[64,112,128]{2,1,0:T(8,128)(2,1)}, bf16[1024,896]{1,0:T(8,128)(2,1)}) custom-call(f32[2]{0:T(128)S(1)} %pad_maximum_fusion.2.sgn_ref, s32[1]{0:T(128)} %bitcast.2.core_ref, bf16[64,7168]{1,0:T(8,128)(2,1)S(1)} %flip.2.rest_0_.own_ref, ...), custom_call_target="tpu_custom_call" | custom-call | flops 1644167168 | bytes 9175040 | tf_op jit(solution)/shard_map/turn/pallas_call | solution.py:275
  55.6 11.5 %all-to-all-start = ((bf16[64,112,128]{2,1,0:T(8,128)(2,1)}), bf16[64,112,128]{2,1,0:T(8,128)(2,1)S(1)}, u32[]{:S(2)}, u32[]{:S(2)}) async-start(bf16[64,112,128]{2,1,0:T(8,128)(2,1)} %get-tuple-element.30), calls=%async_computation | async-start | bytes 3670016 | tf_op jit(solution)/shard_map/all_to_all | solution.py:407
  68.2 5.5 %turn_back.1 = (bf16[64,7168]{1,0:T(8,128)(2,1)}, bf16[64,7168]{1,0:T(8,128)(2,1)}) custom-call(bf16[1024,896]{1,0:T(8,128)(2,1)} %get-tuple-element.25.u_ref, bf16[896,896]{1,0:T(8,128)(2,1)} %constant.154.clone.table_ref), custom_call_target="tpu_custom_call" | custom-call | flops 1644167168 | bytes 3670016 | tf_op jit(solution)/shard_map/turn_back/pallas_call | solution.py:306
  73.7 2.9 %collective-permute-start.17 = (bf16[512,512]{1,0:T(8,128)(2,1)}, bf16[512,512]{1,0:T(8,128)(2,1)}, u32[]{:S(2)}, u32[]{:S(2)}) collective-permute-start(bf16[512,512]{1,0:T(8,128)(2,1)} %pad_maximum_fusion.refs_0_), channel_id=1, source_target_pairs={{0,8},{4,12},{8,0},{12,4},{1,9},{5,13},{9,1},{13,5},{2,10},{6,14},... | collective-permute-start | bytes 1572872 | tf_op jit(solution)/shard_map/ppermute | solution.py:59
  76.6 1.3 %collective-permute-start.16 = (bf16[64,7168]{1,0:T(8,128)(2,1)}, bf16[64,7168]{1,0:T(8,128)(2,1)}, u32[]{:S(2)}, u32[]{:S(2)}) collective-permute-start(bf16[64,7168]{1,0:T(8,128)(2,1)} %get-tuple-element.26.refs_3_.own_ref), channel_id=1, source_target_pairs={{0,2},{2,0},{1,3},{3,1},{4,6},{6,4},{5,7},{7,5},{8,10},{10,8},{9,1... | collective-permute-start | bytes 2752520 | tf_op jit(solution)/shard_map/ppermute | solution.py:49
  79.7 3.1 %copy-done.1 = bf16[7168,512]{1,0:T(8,128)(2,1)S(1)} copy-done((bf16[7168,512]{1,0:T(8,128)(2,1)S(1)}, bf16[7168,512]{1,0:T(8,128)(2,1)}, u32[]{:S(2)}) %copy-start.1) | copy-done | bytes 7340056
  86.2 5.5 %project.1 = bf16[128,512]{1,0:T(8,128)(2,1)S(1)} custom-call(bf16[64,7168]{1,0:T(8,128)(2,1)S(1)} %copy-done.10, bf16[64,7168]{1,0:T(8,128)(2,1)} %collective-permute-done.5.refs_1_, bf16[7168,512]{1,0:T(8,128)(2,1)S(1)} %copy-done.1, bf16[64,7168]{1,0:T(8,128)(2,1)S(1)} %copy-done.4, bf16[512,512]{1,0:T(8,128)(2,1)S(1)} %collective-permute-done.10.refs_4_, ...), custom_call_target="tpu_custom_call" | custom-call | flops 939524096 | bytes 7340032 | tf_op jit(solution)/shard_map/project/pallas_call | solution.py:191
  91.7 5.8 %collective-permute-done.17.refs_2_ = bf16[512,512]{1,0:T(8,128)(2,1)} collective-permute-done((bf16[512,512]{1,0:T(8,128)(2,1)}, bf16[512,512]{1,0:T(8,128)(2,1)}, u32[]{:S(2)}, u32[]{:S(2)}) %collective-permute-start.17) | collective-permute-done | bytes 524320 | tf_op jit(solution)/shard_map/ppermute | solution.py:59
  97.5 1.8 %fusion.5 = (bf16[128,512]{1,0:T(8,128)(2,1)}, bf16[128,512]{1,0:T(8,128)(2,1)}, bf16[128,512]{1,0:T(8,128)(2,1)}, bf16[128,512]{1,0:T(8,128)(2,1)S(1)}) fusion(bf16[512,512]{1,0:T(8,128)(2,1)} %collective-permute-done.17.refs_2_), kind=kLoop, calls=%fused_computation.25 | loop fusion | bytes 1048576 | tf_op jit(solution)/shard_map/slice | solution.py:424
  99.3 1.7 %collective-permute-start.18 = (bf16[128,512]{1,0:T(8,128)(2,1)S(1)}, bf16[128,512]{1,0:T(8,128)(2,1)S(1)}, u32[]{:S(2)}, u32[]{:S(2)}) collective-permute-start(bf16[128,512]{1,0:T(8,128)(2,1)S(1)} %get-tuple-element.42), channel_id=1, source_target_pairs={{0,1},{1,0},{2,3},{3,2},{4,5},{5,4},{6,7},{7,6},{8,9},{9,8},{10,11... | collective-permute-start | bytes 393224 | tf_op jit(solution)/shard_map/ppermute | solution.py:49
  102.6 3.0 %finish.2.rest_0_ = bf16[128,7168]{1,0:T(8,128)(2,1)} custom-call(s32[2]{0:T(128)S(1)} %pad_add_fusion.idx_ref, f32[1]{0:T(128)} %bitcast.1.sgn_ref, bf16[64,7168]{1,0:T(8,128)(2,1)S(1)} %copy-done.5, bf16[64,7168]{1,0:T(8,128)(2,1)} %collective-permute-done.16.other_ref, s32[1,7168]{1,0:T(1,128)S(1)} %bitcast.28), custom_call_target="tpu_custom_call" | custom-call | flops 917504 | bytes 2752512 | tf_op jit(solution)/shard_map/finish/pallas_call | solution.py:125
  105.6 5.3 %all-to-all-done.r_ref = bf16[64,112,128]{2,1,0:T(8,128)(2,1)S(1)} async-done(((bf16[64,112,128]{2,1,0:T(8,128)(2,1)}), bf16[64,112,128]{2,1,0:T(8,128)(2,1)S(1)}, u32[]{:S(2)}, u32[]{:S(2)}) %all-to-all-start) | async-done | bytes 1835040 | tf_op jit(solution)/shard_map/all_to_all | solution.py:407
  110.9 3.3 %weight_grad.1 = f32[224,512]{1,0:T(8,128)S(1)} custom-call(s32[64]{0:T(128)S(1)} %add.109.at_ref, bf16[64,112,128]{2,1,0:T(8,128)(2,1)S(1)} %all-to-all-done.r_ref, bf16[512,512]{1,0:T(8,128)(2,1)} %pad_maximum_fusion.refs_0_, bf16[512,512]{1,0:T(8,128)(2,1)} %collective-permute-done.11.refs_1_, bf16[512,512]{1,0:T(8,128)(2,1)} %collective-permute-done.17.refs_2_, ...), custom_call_target="tpu_custom_call" | custom-call | flops 939524096 | bytes 6029312 | tf_op jit(solution)/shard_map/weight_grad/pallas_call | solution.py:337
  114.3 3.0 %collective-permute-start.22 = (bf16[112,512]{1,0:T(8,128)(2,1)S(1)}, bf16[112,512]{1,0:T(8,128)(2,1)S(1)}, u32[]{:S(2)}, u32[]{:S(2)}) collective-permute-start(bf16[112,512]{1,0:T(8,128)(2,1)S(1)} %fusion.1), channel_id=1, source_target_pairs={{0,128},{128,0},{1,129},{129,1},{2,130},{130,2},{3,131},{131,3},{4... | collective-permute-start | bytes 344072 | tf_op jit(solution)/shard_map/ppermute | solution.py:49
  117.3 1.2 collective-permute-start.26
  118.6 1.4 %collective-permute-start.15 = (bf16[32,512]{1,0:T(8,128)(2,1)S(1)}, bf16[32,512]{1,0:T(8,128)(2,1)S(1)}, u32[]{:S(2)}, u32[]{:S(2)}) collective-permute-start(bf16[32,512]{1,0:T(8,128)(2,1)S(1)} %get-tuple-element.43), channel_id=1, source_target_pairs={{0,2},{2,0},{1,3},{3,1},{4,6},{6,4},{5,7},{7,5},{8,10},{10,8},{9,1... | collective-permute-start | bytes 98312 | tf_op jit(solution)/shard_map/ppermute | solution.py:49
  120.0 3.3 %finish.3 = bf16[128,7168]{1,0:T(8,128)(2,1)} custom-call(s32[2]{0:T(128)S(1)} %pad_add_fusion.idx_ref, f32[1]{0:T(128)} %bitcast.1.sgn_ref, bf16[64,7168]{1,0:T(8,128)(2,1)} %collective-permute-done.23.own_ref, bf16[64,7168]{1,0:T(8,128)(2,1)} %collective-permute-done.24.other_ref, s32[1,7168]{1,0:T(1,128)S(1)} %bitcast.29, ...), custom_call_target="tpu_custom_call", output_to_operand_aliasing={{}: (5, {})} | custom-call | flops 917504 | bytes 2752512 | tf_op jit(solution)/shard_map/finish/pallas_call | solution.py:125
  (87 shorter events, 15.6 us)
Async XLA Ops:
  3.0 15.1 %copy-start.12 = (s32[7168]{0:T(1024)S(1)}, s32[7168]{0:T(1024)}, u32[]{:S(2)}) copy-start(s32[7168]{0:T(1024)} %param.8) | copy-start | bytes 86020
  3.7 36.8 %collective-permute-start.1 = (bf16[64,7168]{1,0:T(8,128)(2,1)S(1)}, bf16[64,7168]{1,0:T(8,128)(2,1)}, u32[]{:S(2)}, u32[]{:S(2)}) collective-permute-start(bf16[64,7168]{1,0:T(8,128)(2,1)S(1)} %flip.2.rest_0_.own_ref), channel_id=1, source_target_pairs={{0,2},{2,0},{1,3},{3,1},{4,6},{6,4},{5,7},{7,5},{8,10},{10,8},{9,1... | collective-permute-start | bytes 2752520 | tf_op jit(solution)/shard_map/ppermute | solution.py:49
  5.9 8.7 %collective-permute-start.6 = (bf16[64,512]{1,0:T(8,128)(2,1)S(1)}, bf16[64,512]{1,0:T(8,128)(2,1)S(1)}, u32[]{:S(2)}, u32[]{:S(2)}) collective-permute-start(bf16[64,512]{1,0:T(8,128)(2,1)S(1)} %get-tuple-element.27.m_ref), channel_id=1, source_target_pairs={{0,64},{16,80},{32,96},{48,112},{64,0},{80,16},{96,32},{112,48},{1... | collective-permute-start | bytes 196616 | tf_op jit(solution)/shard_map/ppermute | solution.py:54
  15.3 15.0 %collective-permute-start.9 = (bf16[128,512]{1,0:T(8,128)(2,1)}, bf16[128,512]{1,0:T(8,128)(2,1)S(1)}, u32[]{:S(2)}, u32[]{:S(2)}) collective-permute-start(bf16[128,512]{1,0:T(8,128)(2,1)} %pad_maximum_fusion.1), channel_id=1, source_target_pairs={{0,48},{16,32},{32,16},{48,0},{64,112},{80,96},{96,80},{112,64},{1... | collective-permute-start | bytes 393224 | tf_op jit(solution)/shard_map/ppermute | solution.py:54
  19.7 23.7 %collective-permute-start = (bf16[64,7168]{1,0:T(8,128)(2,1)}, bf16[64,7168]{1,0:T(8,128)(2,1)S(1)}, u32[]{:S(2)}, u32[]{:S(2)}) collective-permute-start(bf16[64,7168]{1,0:T(8,128)(2,1)} %flip.3), channel_id=1, source_target_pairs={{0,1},{1,0},{2,3},{3,2},{4,5},{5,4},{6,7},{7,6},{8,9},{9,8},{10,11... | collective-permute-start | bytes 2752520 | tf_op jit(solution)/shard_map/ppermute | solution.py:49
  22.0 24.5 %collective-permute-start.2 = (bf16[64,7168]{1,0:T(8,128)(2,1)}, bf16[64,7168]{1,0:T(8,128)(2,1)}, u32[]{:S(2)}, u32[]{:S(2)}) collective-permute-start(bf16[64,7168]{1,0:T(8,128)(2,1)} %flip.3), channel_id=1, source_target_pairs={{0,3},{1,2},{2,1},{3,0},{4,7},{5,6},{6,5},{7,4},{8,11},{9,10},{10,... | collective-permute-start | bytes 2752520 | tf_op jit(solution)/shard_map/ppermute | solution.py:54
  22.1 10.3 %collective-permute-start.8 = (bf16[128,512]{1,0:T(8,128)(2,1)}, bf16[128,512]{1,0:T(8,128)(2,1)}, u32[]{:S(2)}, u32[]{:S(2)}) collective-permute-start(bf16[128,512]{1,0:T(8,128)(2,1)} %pad_maximum_fusion.1), channel_id=1, source_target_pairs={{0,32},{16,48},{32,0},{48,16},{64,96},{80,112},{96,64},{112,80},{1... | collective-permute-start | bytes 393224 | tf_op jit(solution)/shard_map/ppermute | solution.py:54
  25.2 21.4 %copy-start.9 = (bf16[896,896]{1,0:T(8,128)(2,1)S(1)}, bf16[896,896]{1,0:T(8,128)(2,1)}, u32[]{:S(2)}) copy-start(bf16[896,896]{1,0:T(8,128)(2,1)} %constant.154.clone.table_ref) | copy-start | bytes 4816900
  30.3 16.3 %collective-permute-start.4 = (bf16[64,7168]{1,0:T(8,128)(2,1)}, bf16[64,7168]{1,0:T(8,128)(2,1)}, u32[]{:S(2)}, u32[]{:S(2)}) collective-permute-start(bf16[64,7168]{1,0:T(8,128)(2,1)} %get-tuple-element.22), channel_id=1, source_target_pairs={{0,1},{1,0},{2,3},{3,2},{4,5},{5,4},{6,7},{7,6},{8,9},{9,8},{10,11... | collective-permute-start | bytes 2752520 | tf_op jit(solution)/shard_map/ppermute | solution.py:49
  32.4 4.9 %collective-permute-start.7 = (bf16[128,512]{1,0:T(8,128)(2,1)}, bf16[128,512]{1,0:T(8,128)(2,1)S(1)}, u32[]{:S(2)}, u32[]{:S(2)}) collective-permute-start(bf16[128,512]{1,0:T(8,128)(2,1)} %pad_maximum_fusion.1), channel_id=1, source_target_pairs={{0,16},{16,0},{32,48},{48,32},{64,80},{80,64},{96,112},{112,96},{1... | collective-permute-start | bytes 393224 | tf_op jit(solution)/shard_map/ppermute | solution.py:54
  37.3 4.4 %collective-permute-start.3 = (f32[64,56]{1,0:T(8,128)S(1)}, f32[64,56]{1,0:T(8,128)S(1)}, u32[]{:S(2)}, u32[]{:S(2)}) collective-permute-start(f32[64,56]{1,0:T(8,128)S(1)} %get-tuple-element.48), channel_id=1, source_target_pairs={{0,1},{1,0},{2,3},{3,2},{4,5},{5,4},{6,7},{7,6},{8,9},{9,8},{10,11... | collective-permute-start | bytes 43016 | tf_op jit(solution)/shard_map/ppermute | solution.py:49
  40.5 15.1 %collective-permute-start.11 = (bf16[512,512]{1,0:T(8,128)(2,1)}, bf16[512,512]{1,0:T(8,128)(2,1)}, u32[]{:S(2)}, u32[]{:S(2)}) collective-permute-start(bf16[512,512]{1,0:T(8,128)(2,1)} %pad_maximum_fusion.refs_0_), channel_id=1, source_target_pairs={{0,4},{4,8},{8,12},{12,0},{1,5},{5,9},{9,13},{13,1},{2,6},{6,10},{... | collective-permute-start | bytes 1572872 | tf_op jit(solution)/shard_map/ppermute | solution.py:59
  41.7 13.9 %collective-permute-start.13 = (bf16[512,512]{1,0:T(8,128)(2,1)}, bf16[512,512]{1,0:T(8,128)(2,1)}, u32[]{:S(2)}, u32[]{:S(2)}) collective-permute-start(bf16[512,512]{1,0:T(8,128)(2,1)} %pad_maximum_fusion.refs_0_), channel_id=1, source_target_pairs={{0,12},{4,0},{8,4},{12,8},{1,13},{5,1},{9,5},{13,9},{2,14},{6,2},{... | collective-permute-start | bytes 1572872 | tf_op jit(solution)/shard_map/ppermute | solution.py:59
  55.6 55.3 %all-to-all-start = ((bf16[64,112,128]{2,1,0:T(8,128)(2,1)}), bf16[64,112,128]{2,1,0:T(8,128)(2,1)S(1)}, u32[]{:S(2)}, u32[]{:S(2)}) async-start(bf16[64,112,128]{2,1,0:T(8,128)(2,1)} %get-tuple-element.30), calls=%async_computation | async-start | bytes 3670016 | tf_op jit(solution)/shard_map/all_to_all | solution.py:407
  67.0 10.8 %collective-permute-start.5 = (bf16[64,7168]{1,0:T(8,128)(2,1)}, bf16[64,7168]{1,0:T(8,128)(2,1)}, u32[]{:S(2)}, u32[]{:S(2)}) collective-permute-start(bf16[64,7168]{1,0:T(8,128)(2,1)} %get-tuple-element.24), channel_id=1, source_target_pairs={{0,1},{1,0},{2,3},{3,2},{4,5},{5,4},{6,7},{7,6},{8,9},{9,8},{10,11... | collective-permute-start | bytes 2752520 | tf_op jit(solution)/shard_map/ppermute | solution.py:49
  67.5 9.1 %collective-permute-start.10 = (bf16[512,512]{1,0:T(8,128)(2,1)}, bf16[512,512]{1,0:T(8,128)(2,1)S(1)}, u32[]{:S(2)}, u32[]{:S(2)}) collective-permute-start(bf16[512,512]{1,0:T(8,128)(2,1)} %pad_maximum_fusion.refs_0_), channel_id=1, source_target_pairs={{0,1},{1,0},{2,3},{3,2},{4,5},{5,4},{6,7},{7,6},{8,9},{9,8},{10,11... | collective-permute-start | bytes 1572872 | tf_op jit(solution)/shard_map/ppermute | solution.py:49
  67.6 11.2 %collective-permute-start.12 = (bf16[512,512]{1,0:T(8,128)(2,1)}, bf16[512,512]{1,0:T(8,128)(2,1)S(1)}, u32[]{:S(2)}, u32[]{:S(2)}) collective-permute-start(bf16[512,512]{1,0:T(8,128)(2,1)} %collective-permute-done.11.refs_1_), channel_id=1, source_target_pairs={{0,1},{1,0},{2,3},{3,2},{4,5},{5,4},{6,7},{7,6},{8,9},{9,8},{10,11... | collective-permute-start | bytes 1572872 | tf_op jit(solution)/shard_map/ppermute | solution.py:49
  68.0 11.7 %collective-permute-start.14 = (bf16[512,512]{1,0:T(8,128)(2,1)}, bf16[512,512]{1,0:T(8,128)(2,1)}, u32[]{:S(2)}, u32[]{:S(2)}) collective-permute-start(bf16[512,512]{1,0:T(8,128)(2,1)} %collective-permute-done.13.refs_3_), channel_id=1, source_target_pairs={{0,1},{1,0},{2,3},{3,2},{4,5},{5,4},{6,7},{7,6},{8,9},{9,8},{10,11... | collective-permute-start | bytes 1572872 | tf_op jit(solution)/shard_map/ppermute | solution.py:49
  73.7 23.8 %collective-permute-start.17 = (bf16[512,512]{1,0:T(8,128)(2,1)}, bf16[512,512]{1,0:T(8,128)(2,1)}, u32[]{:S(2)}, u32[]{:S(2)}) collective-permute-start(bf16[512,512]{1,0:T(8,128)(2,1)} %pad_maximum_fusion.refs_0_), channel_id=1, source_target_pairs={{0,8},{4,12},{8,0},{12,4},{1,9},{5,13},{9,1},{13,5},{2,10},{6,14},... | collective-permute-start | bytes 1572872 | tf_op jit(solution)/shard_map/ppermute | solution.py:59
  76.6 15.2 %copy-start.6 = (bf16[512,512]{1,0:T(8,128)(2,1)}, bf16[512,512]{1,0:T(8,128)(2,1)S(1)}, u32[]{:S(2)}) copy-start(bf16[512,512]{1,0:T(8,128)(2,1)S(1)} %collective-permute-done.10.refs_4_) | copy-start | bytes 1572868
  76.6 24.6 %collective-permute-start.16 = (bf16[64,7168]{1,0:T(8,128)(2,1)}, bf16[64,7168]{1,0:T(8,128)(2,1)}, u32[]{:S(2)}, u32[]{:S(2)}) collective-permute-start(bf16[64,7168]{1,0:T(8,128)(2,1)} %get-tuple-element.26.refs_3_.own_ref), channel_id=1, source_target_pairs={{0,2},{2,0},{1,3},{3,1},{4,6},{6,4},{5,7},{7,5},{8,10},{10,8},{9,1... | collective-permute-start | bytes 2752520 | tf_op jit(solution)/shard_map/ppermute | solution.py:49
  77.9 42.1 %collective-permute-start.23 = (bf16[64,7168]{1,0:T(8,128)(2,1)}, bf16[64,7168]{1,0:T(8,128)(2,1)}, u32[]{:S(2)}, u32[]{:S(2)}) collective-permute-start(bf16[64,7168]{1,0:T(8,128)(2,1)} %get-tuple-element.34), channel_id=1, source_target_pairs={{0,1},{1,0},{2,3},{3,2},{4,5},{5,4},{6,7},{7,6},{8,9},{9,8},{10,11... | collective-permute-start | bytes 2752520 | tf_op jit(solution)/shard_map/ppermute | solution.py:49
  79.7 39.0 %collective-permute-start.24 = (bf16[64,7168]{1,0:T(8,128)(2,1)}, bf16[64,7168]{1,0:T(8,128)(2,1)}, u32[]{:S(2)}, u32[]{:S(2)}) collective-permute-start(bf16[64,7168]{1,0:T(8,128)(2,1)} %get-tuple-element.34), channel_id=1, source_target_pairs={{0,3},{1,2},{2,1},{3,0},{4,7},{5,6},{6,5},{7,4},{8,11},{9,10},{10,... | collective-permute-start | bytes 2752520 | tf_op jit(solution)/shard_map/ppermute | solution.py:54
  86.2 16.4 %copy-start.5 = (bf16[64,7168]{1,0:T(8,128)(2,1)S(1)}, bf16[64,7168]{1,0:T(8,128)(2,1)}, u32[]{:S(2)}) copy-start(bf16[64,7168]{1,0:T(8,128)(2,1)} %get-tuple-element.26.refs_3_.own_ref) | copy-start | bytes 2752516
  99.3 2.7 %collective-permute-start.18 = (bf16[128,512]{1,0:T(8,128)(2,1)S(1)}, bf16[128,512]{1,0:T(8,128)(2,1)S(1)}, u32[]{:S(2)}, u32[]{:S(2)}) collective-permute-start(bf16[128,512]{1,0:T(8,128)(2,1)S(1)} %get-tuple-element.42), channel_id=1, source_target_pairs={{0,1},{1,0},{2,3},{3,2},{4,5},{5,4},{6,7},{7,6},{8,9},{9,8},{10,11... | collective-permute-start | bytes 393224 | tf_op jit(solution)/shard_map/ppermute | solution.py:49
  101.1 9.7 %collective-permute-start.19 = (bf16[128,512]{1,0:T(8,128)(2,1)}, bf16[128,512]{1,0:T(8,128)(2,1)S(1)}, u32[]{:S(2)}, u32[]{:S(2)}) collective-permute-start(bf16[128,512]{1,0:T(8,128)(2,1)} %get-tuple-element.41), channel_id=1, source_target_pairs={{0,1},{1,0},{2,3},{3,2},{4,5},{5,4},{6,7},{7,6},{8,9},{9,8},{10,11... | collective-permute-start | bytes 393224 | tf_op jit(solution)/shard_map/ppermute | solution.py:49
  101.2 9.7 %collective-permute-start.20 = (bf16[128,512]{1,0:T(8,128)(2,1)}, bf16[128,512]{1,0:T(8,128)(2,1)S(1)}, u32[]{:S(2)}, u32[]{:S(2)}) collective-permute-start(bf16[128,512]{1,0:T(8,128)(2,1)} %get-tuple-element.40), channel_id=1, source_target_pairs={{0,1},{1,0},{2,3},{3,2},{4,5},{5,4},{6,7},{7,6},{8,9},{9,8},{10,11... | collective-permute-start | bytes 393224 | tf_op jit(solution)/shard_map/ppermute | solution.py:49
  102.1 8.8 %collective-permute-start.21 = (bf16[128,512]{1,0:T(8,128)(2,1)}, bf16[128,512]{1,0:T(8,128)(2,1)S(1)}, u32[]{:S(2)}, u32[]{:S(2)}) collective-permute-start(bf16[128,512]{1,0:T(8,128)(2,1)} %get-tuple-element.39), channel_id=1, source_target_pairs={{0,1},{1,0},{2,3},{3,2},{4,5},{5,4},{6,7},{7,6},{8,9},{9,8},{10,11... | collective-permute-start | bytes 393224 | tf_op jit(solution)/shard_map/ppermute | solution.py:49
  114.3 9.0 %collective-permute-start.22 = (bf16[112,512]{1,0:T(8,128)(2,1)S(1)}, bf16[112,512]{1,0:T(8,128)(2,1)S(1)}, u32[]{:S(2)}, u32[]{:S(2)}) collective-permute-start(bf16[112,512]{1,0:T(8,128)(2,1)S(1)} %fusion.1), channel_id=1, source_target_pairs={{0,128},{128,0},{1,129},{129,1},{2,130},{130,2},{3,131},{131,3},{4... | collective-permute-start | bytes 344072 | tf_op jit(solution)/shard_map/ppermute | solution.py:49
  117.3 6.0 %collective-permute-start.26 = (bf16[32,512]{1,0:T(8,128)(2,1)S(1)}, bf16[32,512]{1,0:T(8,128)(2,1)S(1)}, u32[]{:S(2)}, u32[]{:S(2)}) collective-permute-start(bf16[32,512]{1,0:T(8,128)(2,1)S(1)} %get-tuple-element.44), channel_id=1, source_target_pairs={{0,3},{1,2},{2,1},{3,0},{4,7},{5,6},{6,5},{7,4},{8,11},{9,10},{10,... | collective-permute-start | bytes 98312 | tf_op jit(solution)/shard_map/ppermute | solution.py:54
  118.5 4.8 %collective-permute-start.25 = (bf16[32,512]{1,0:T(8,128)(2,1)S(1)}, bf16[32,512]{1,0:T(8,128)(2,1)S(1)}, u32[]{:S(2)}, u32[]{:S(2)}) collective-permute-start(bf16[32,512]{1,0:T(8,128)(2,1)S(1)} %get-tuple-element.45), channel_id=1, source_target_pairs={{0,1},{1,0},{2,3},{3,2},{4,5},{5,4},{6,7},{7,6},{8,9},{9,8},{10,11... | collective-permute-start | bytes 98312 | tf_op jit(solution)/shard_map/ppermute | solution.py:49
  118.6 4.7 %collective-permute-start.15 = (bf16[32,512]{1,0:T(8,128)(2,1)S(1)}, bf16[32,512]{1,0:T(8,128)(2,1)S(1)}, u32[]{:S(2)}, u32[]{:S(2)}) collective-permute-start(bf16[32,512]{1,0:T(8,128)(2,1)S(1)} %get-tuple-element.43), channel_id=1, source_target_pairs={{0,2},{2,0},{1,3},{3,1},{4,6},{6,4},{5,7},{7,5},{8,10},{10,8},{9,1... | collective-permute-start | bytes 98312 | tf_op jit(solution)/shard_map/ppermute | solution.py:49
  (13 other events, 46.8 us)
